TPU v7x, 512 devices: a whole 4x4x16 slice. The times are simulated.
512 devices in a mesh: blk: 16 (over y, z_hi, core), uly: 32 (over x, z_lo).
Axes of the slice: x: 4, y: 4, z: 16 (z_hi: 2, z_lo: 8; z = z_hi * 8 + z_lo), core: 2. Of those that a mesh axis runs over, the one named last changes fastest.
Arguments:
- queries: bfloat16 [4096, 1024], P(('blk', 'uly')), may hold values from -12 to 12
- keys: bfloat16 [65536, 1024], P(('blk', 'uly')), may hold values from -6 to 6
- values: bfloat16 [65536, 1024], P(('blk', 'uly')), may hold values from -6 to 6
- w_out: bfloat16 [1024, 1024], replicated, may hold values from -0.1875 to 0.1875
Outputs:
- projected: bfloat16 [4096, 1024], P(('blk', 'uly'))
All inputs are finite; a program needn't handle non-finite values.
Results may differ from a plain program's by a relative error of at most 0.02.
Values may be sent and summed in bfloat16 or wider, within the bound.
No kernel may reach another device: no remote copies, remote signals or barrier semaphores. Data moves between devices by JAX's collectives and lax.ppermute only.
A program may use at most 64 MiB of HBM per device.

v0:
```python
import jax
import jax.numpy as jnp
from jax import lax
from jax.sharding import PartitionSpec as P

HD = 64


def from_behind(block, axis, distance):
    devices = range(lax.axis_size(axis))
    route = [((i - distance) % len(devices), i) for i in devices]
    return lax.ppermute(block, axis, route)


def absorb_block(carry_state, kv_block, query_block):
    run_max, run_sum, run_out = carry_state
    score = jnp.einsum(
        "qph,kph->qpk", query_block, kv_block[:, :, 0], preferred_element_type=jnp.float32
    ) * HD ** (-0.5)
    new_max = jnp.maximum(run_max, jnp.max(score, axis=2))
    factor = jnp.exp(run_max - new_max)
    weights = jnp.exp(score - new_max[:, :, None])
    new_sum = run_sum * factor + jnp.sum(weights, axis=2)
    contrib = jnp.einsum(
        "qpk,kph->qph",
        weights.astype(jnp.bfloat16),
        kv_block[:, :, 1],
        preferred_element_type=jnp.float32,
    )
    return (new_max, new_sum, run_out * factor[:, :, None] + contrib)


def fresh_state(rows, per_dev):
    return (
        jnp.full((rows, per_dev), -jnp.inf, jnp.float32),
        jnp.zeros((rows, per_dev), jnp.float32),
        jnp.zeros((rows, per_dev, HD), jnp.float32),
    )


def local(queries, keys, values, w_out):
    n_uly = lax.axis_size("uly")
    n_blk = lax.axis_size("blk")
    head_count = queries.shape[1] // HD
    per_dev = max(head_count // n_uly, 1)
    groups = head_count // per_dev
    ksplit = n_uly // groups
    q_rows = queries.shape[0]
    k_rows = keys.shape[0]
    q_half = q_rows // ksplit
    row_width = per_dev * HD
    q_send = queries.reshape(ksplit, q_half, groups, row_width).transpose(2, 0, 1, 3)
    q_send = q_send.reshape(n_uly, q_half, row_width)
    kv_local = jnp.stack(
        [keys.reshape(k_rows, groups, per_dev, HD), values.reshape(k_rows, groups, per_dev, HD)],
        axis=3,
    )
    kv_local = kv_local.reshape(k_rows, groups, row_width * 2).transpose(1, 0, 2)
    kv_send = jnp.broadcast_to(kv_local[:, None], (groups, ksplit, k_rows, row_width * 2)).reshape(
        n_uly, k_rows, row_width * 2
    )
    q_recv, kv_recv = (
        lax.all_to_all(q_send, "uly", split_axis=0, concat_axis=0, tiled=True),
        lax.all_to_all(kv_send, "uly", split_axis=0, concat_axis=0, tiled=True),
    )
    group_rows = n_uly * q_half
    query_block = q_recv.reshape(group_rows, per_dev, HD)
    kv_block = kv_recv.reshape(n_uly * k_rows, per_dev, 2, HD)
    initial = fresh_state(group_rows, per_dev)
    opening = absorb_block(initial, kv_block, query_block)

    def visit(step_index, carry):
        moving = from_behind(carry[0], "blk", 1)
        return (moving, absorb_block(carry[1], moving, query_block))

    carry_state = lax.fori_loop(0, n_blk - 1, visit, (kv_block, opening))[1]
    run_max, run_sum, run_out = carry_state
    attended = (run_out / run_sum[:, :, None]).astype(jnp.bfloat16)
    back_send = attended.reshape(n_uly, q_half, row_width)
    back_recv = lax.all_to_all(back_send, "uly", split_axis=0, concat_axis=0, tiled=True)
    token_rows = back_recv.reshape(groups, ksplit, q_half, row_width).transpose(1, 2, 0, 3)
    token_rows = token_rows.reshape(q_rows, groups * row_width)
    return jnp.dot(token_rows, w_out, preferred_element_type=jnp.float32).astype(jnp.bfloat16)


def solution(mesh):
    return jax.shard_map(
        local,
        mesh=mesh,
        in_specs=(P(("blk", "uly"), None), P(("blk", "uly"), None), P(("blk", "uly"), None), P()),
        out_specs=P(("blk", "uly"), None),
        check_vma=False,
    )
```

profile of v0, /device:TPU:2, one launch (start us, length us, event | category | flops | bytes accessed | tf_op | source)
XLA Modules:
  0.0 869.5 jit_solution(5867178767080789550)
XLA Ops:
  0.0 1.0 reshape.122
  1.7 15.7 %all-to-all-start.1 = ((bf16[32,2,128]{2,1,0:T(2,128)(2,1)}), bf16[32,2,128]{2,1,0:T(2,128)(2,1)S(1)}, u32[]{:S(2)}, u32[]{:S(2)}) async-start(bf16[32,2,128]{2,1,0:T(2,128)(2,1)} %reshape.131), calls=%async_computation.1 | async-start | bytes 32768 | tf_op jit(solution)/shard_map/all_to_all | solution.py:63
  17.4 1.1 copy.14
  18.5 1.1 copy.15
  19.7 8.9 %all-to-all-done.1 = bf16[32,2,128]{2,1,0:T(2,128)(2,1)S(1)} async-done(((bf16[32,2,128]{2,1,0:T(2,128)(2,1)}), bf16[32,2,128]{2,1,0:T(2,128)(2,1)S(1)}, u32[]{:S(2)}, u32[]{:S(2)}) %all-to-all-start.1) | async-done | bytes 16416 | tf_op jit(solution)/shard_map/all_to_all | solution.py:63
  28.6 1.2 broadcast_in_dim.10
  29.8 5.0 all-to-all-start
  35.1 47.3 %all-to-all-done = bf16[32,128,128]{1,2,0:T(8,128)(2,1)S(1)} async-done(((bf16[32,128,128]{1,2,0:T(8,128)(2,1)}), bf16[32,128,128]{1,2,0:T(8,128)(2,1)S(1)}, u32[]{:S(2)}, u32[]{:S(2)}) %all-to-all-start) | async-done | bytes 1048608 | tf_op jit(solution)/shard_map/all_to_all | solution.py:64
  82.4 1.7 copy.17
  84.1 2.3 reshape.120
  86.4 1.8 fusion.18
  88.8 1.5 fusion.13
  90.3 748.4 %while.16 = (s32[]{:T(128)}, bf16[4096,1,2,64]{0,3,2,1:T(8,128)(2,1)}, f32[128,1]{0,1:T(1,128)S(1)}, f32[128,1]{0,1:T(1,128)S(1)}, f32[128,1,64]{0,2,1:T(8,128)S(1)}, /*index=5*/bf16[128,1,64]{0,2,1:T(8,128)(2,1)S(1)}, s32[]{:T(128)}) while((s32[]{:T(128)}, bf16[4096,1,2,64]{0,3,2,1:T(8,128)(2,1)}, f32[128,1]{0,1:T(1,128)S(1)}, ...), condition=%wide.region_5.0_spmd, body=%wide.region_2.0_spmd.sunk | while | flops 137380224 | bytes 13721717 | solution.py:76
  90.3 1.9 collective-permute-start
  92.2 53.8 %collective-permute-done = bf16[4096,1,2,64]{0,3,2,1:T(8,128)(2,1)S(1)} collective-permute-done((bf16[4096,1,2,64]{0,3,2,1:T(8,128)(2,1)}, bf16[4096,1,2,64]{0,3,2,1:T(8,128)(2,1)S(1)}, u32[]{:S(2)}, u32[]{:S(2)}) %collective-permute-start) | collective-permute-done | bytes 1048608 | tf_op jit(solution)/shard_map/while/body/eval_jaxpr/ppermute | solution.py:12
  146.0 0.7 fusion.28
  147.3 1.0 copy.35
  148.9 1.9 collective-permute-start
  150.8 39.9 %collective-permute-done = bf16[4096,1,2,64]{0,3,2,1:T(8,128)(2,1)S(1)} collective-permute-done((bf16[4096,1,2,64]{0,3,2,1:T(8,128)(2,1)}, bf16[4096,1,2,64]{0,3,2,1:T(8,128)(2,1)S(1)}, u32[]{:S(2)}, u32[]{:S(2)}) %collective-permute-start) | collective-permute-done | bytes 1048608 | tf_op jit(solution)/shard_map/while/body/eval_jaxpr/ppermute | solution.py:12
  190.7 0.7 fusion.28
  192.0 1.0 copy.35
  193.6 1.9 collective-permute-start
  195.5 43.5 %collective-permute-done = bf16[4096,1,2,64]{0,3,2,1:T(8,128)(2,1)S(1)} collective-permute-done((bf16[4096,1,2,64]{0,3,2,1:T(8,128)(2,1)}, bf16[4096,1,2,64]{0,3,2,1:T(8,128)(2,1)S(1)}, u32[]{:S(2)}, u32[]{:S(2)}) %collective-permute-start) | collective-permute-done | bytes 1048608 | tf_op jit(solution)/shard_map/while/body/eval_jaxpr/ppermute | solution.py:12
  240.4 1.0 copy.35
  241.9 1.9 collective-permute-start
  243.8 46.4 %collective-permute-done = bf16[4096,1,2,64]{0,3,2,1:T(8,128)(2,1)S(1)} collective-permute-done((bf16[4096,1,2,64]{0,3,2,1:T(8,128)(2,1)}, bf16[4096,1,2,64]{0,3,2,1:T(8,128)(2,1)S(1)}, u32[]{:S(2)}, u32[]{:S(2)}) %collective-permute-start) | collective-permute-done | bytes 1048608 | tf_op jit(solution)/shard_map/while/body/eval_jaxpr/ppermute | solution.py:12
  290.2 0.7 fusion.28
  291.5 1.0 copy.35
  293.0 1.9 collective-permute-start
  295.0 43.5 %collective-permute-done = bf16[4096,1,2,64]{0,3,2,1:T(8,128)(2,1)S(1)} collective-permute-done((bf16[4096,1,2,64]{0,3,2,1:T(8,128)(2,1)}, bf16[4096,1,2,64]{0,3,2,1:T(8,128)(2,1)S(1)}, u32[]{:S(2)}, u32[]{:S(2)}) %collective-permute-start) | collective-permute-done | bytes 1048608 | tf_op jit(solution)/shard_map/while/body/eval_jaxpr/ppermute | solution.py:12
  339.8 1.0 copy.35
  341.4 1.9 collective-permute-start
  343.3 46.4 %collective-permute-done = bf16[4096,1,2,64]{0,3,2,1:T(8,128)(2,1)S(1)} collective-permute-done((bf16[4096,1,2,64]{0,3,2,1:T(8,128)(2,1)}, bf16[4096,1,2,64]{0,3,2,1:T(8,128)(2,1)S(1)}, u32[]{:S(2)}, u32[]{:S(2)}) %collective-permute-start) | collective-permute-done | bytes 1048608 | tf_op jit(solution)/shard_map/while/body/eval_jaxpr/ppermute | solution.py:12
  391.0 1.0 copy.35
  392.5 1.9 collective-permute-start
  394.5 43.5 %collective-permute-done = bf16[4096,1,2,64]{0,3,2,1:T(8,128)(2,1)S(1)} collective-permute-done((bf16[4096,1,2,64]{0,3,2,1:T(8,128)(2,1)}, bf16[4096,1,2,64]{0,3,2,1:T(8,128)(2,1)S(1)}, u32[]{:S(2)}, u32[]{:S(2)}) %collective-permute-start) | collective-permute-done | bytes 1048608 | tf_op jit(solution)/shard_map/while/body/eval_jaxpr/ppermute | solution.py:12
  438.0 0.7 fusion.28
  439.3 1.0 copy.35
  440.9 1.9 collective-permute-start
  442.8 46.4 %collective-permute-done = bf16[4096,1,2,64]{0,3,2,1:T(8,128)(2,1)S(1)} collective-permute-done((bf16[4096,1,2,64]{0,3,2,1:T(8,128)(2,1)}, bf16[4096,1,2,64]{0,3,2,1:T(8,128)(2,1)S(1)}, u32[]{:S(2)}, u32[]{:S(2)}) %collective-permute-start) | collective-permute-done | bytes 1048608 | tf_op jit(solution)/shard_map/while/body/eval_jaxpr/ppermute | solution.py:12
  490.5 1.0 copy.35
  492.0 1.9 collective-permute-start
  494.0 43.5 %collective-permute-done = bf16[4096,1,2,64]{0,3,2,1:T(8,128)(2,1)S(1)} collective-permute-done((bf16[4096,1,2,64]{0,3,2,1:T(8,128)(2,1)}, bf16[4096,1,2,64]{0,3,2,1:T(8,128)(2,1)S(1)}, u32[]{:S(2)}, u32[]{:S(2)}) %collective-permute-start) | collective-permute-done | bytes 1048608 | tf_op jit(solution)/shard_map/while/body/eval_jaxpr/ppermute | solution.py:12
  538.8 1.0 copy.35
  540.4 1.9 collective-permute-start
  542.3 46.4 %collective-permute-done = bf16[4096,1,2,64]{0,3,2,1:T(8,128)(2,1)S(1)} collective-permute-done((bf16[4096,1,2,64]{0,3,2,1:T(8,128)(2,1)}, bf16[4096,1,2,64]{0,3,2,1:T(8,128)(2,1)S(1)}, u32[]{:S(2)}, u32[]{:S(2)}) %collective-permute-start) | collective-permute-done | bytes 1048608 | tf_op jit(solution)/shard_map/while/body/eval_jaxpr/ppermute | solution.py:12
  590.0 1.0 copy.35
  591.5 1.9 collective-permute-start
  593.5 43.5 %collective-permute-done = bf16[4096,1,2,64]{0,3,2,1:T(8,128)(2,1)S(1)} collective-permute-done((bf16[4096,1,2,64]{0,3,2,1:T(8,128)(2,1)}, bf16[4096,1,2,64]{0,3,2,1:T(8,128)(2,1)S(1)}, u32[]{:S(2)}, u32[]{:S(2)}) %collective-permute-start) | collective-permute-done | bytes 1048608 | tf_op jit(solution)/shard_map/while/body/eval_jaxpr/ppermute | solution.py:12
  638.3 1.0 copy.35
  639.9 1.9 collective-permute-start
  641.8 46.4 %collective-permute-done = bf16[4096,1,2,64]{0,3,2,1:T(8,128)(2,1)S(1)} collective-permute-done((bf16[4096,1,2,64]{0,3,2,1:T(8,128)(2,1)}, bf16[4096,1,2,64]{0,3,2,1:T(8,128)(2,1)S(1)}, u32[]{:S(2)}, u32[]{:S(2)}) %collective-permute-start) | collective-permute-done | bytes 1048608 | tf_op jit(solution)/shard_map/while/body/eval_jaxpr/ppermute | solution.py:12
  689.5 1.0 copy.35
  691.0 1.9 collective-permute-start
  693.0 43.5 %collective-permute-done = bf16[4096,1,2,64]{0,3,2,1:T(8,128)(2,1)S(1)} collective-permute-done((bf16[4096,1,2,64]{0,3,2,1:T(8,128)(2,1)}, bf16[4096,1,2,64]{0,3,2,1:T(8,128)(2,1)S(1)}, u32[]{:S(2)}, u32[]{:S(2)}) %collective-permute-start) | collective-permute-done | bytes 1048608 | tf_op jit(solution)/shard_map/while/body/eval_jaxpr/ppermute | solution.py:12
  737.8 1.0 copy.35
  739.4 1.9 collective-permute-start
  741.3 46.4 %collective-permute-done = bf16[4096,1,2,64]{0,3,2,1:T(8,128)(2,1)S(1)} collective-permute-done((bf16[4096,1,2,64]{0,3,2,1:T(8,128)(2,1)}, bf16[4096,1,2,64]{0,3,2,1:T(8,128)(2,1)S(1)}, u32[]{:S(2)}, u32[]{:S(2)}) %collective-permute-start) | collective-permute-done | bytes 1048608 | tf_op jit(solution)/shard_map/while/body/eval_jaxpr/ppermute | solution.py:12
  789.0 1.0 copy.35
  790.5 1.9 collective-permute-start
  792.5 43.4 %collective-permute-done = bf16[4096,1,2,64]{0,3,2,1:T(8,128)(2,1)S(1)} collective-permute-done((bf16[4096,1,2,64]{0,3,2,1:T(8,128)(2,1)}, bf16[4096,1,2,64]{0,3,2,1:T(8,128)(2,1)S(1)}, u32[]{:S(2)}, u32[]{:S(2)}) %collective-permute-start) | collective-permute-done | bytes 1048608 | tf_op jit(solution)/shard_map/while/body/eval_jaxpr/ppermute | solution.py:12
  837.2 1.0 copy.35
  839.0 29.3 %all_to_all.15 = bf16[32,2,128]{2,1,0:T(2,128)(2,1)S(1)} all-to-all(bf16[32,2,128]{2,1,0:T(2,128)(2,1)S(1)} %reshape.133), channel_id=1, replica_groups=mesh['blk'=16,'uly'=32] {'uly'}, dimensions={0} | all-to-all | bytes 32768 | tf_op jit(solution)/shard_map/all_to_all | solution.py:80
  868.5 1.0 convolution_convert_fusion
  (103 shorter events, 26.7 us)
Async XLA Ops:
  0.0 868.5 %copy-start = (bf16[1024,1024]{1,0:T(8,128)(2,1)S(1)}, bf16[1024,1024]{1,0:T(8,128)(2,1)}, u32[]{:S(2)}) copy-start(bf16[1024,1024]{1,0:T(8,128)(2,1)} %param.9) | copy-start | bytes 6291460
  1.7 26.9 %all-to-all-start.1 = ((bf16[32,2,128]{2,1,0:T(2,128)(2,1)}), bf16[32,2,128]{2,1,0:T(2,128)(2,1)S(1)}, u32[]{:S(2)}, u32[]{:S(2)}) async-start(bf16[32,2,128]{2,1,0:T(2,128)(2,1)} %reshape.131), calls=%async_computation.1 | async-start | bytes 32768 | tf_op jit(solution)/shard_map/all_to_all | solution.py:63
  29.8 52.5 %all-to-all-start = ((bf16[32,128,128]{1,2,0:T(8,128)(2,1)}), bf16[32,128,128]{1,2,0:T(8,128)(2,1)S(1)}, u32[]{:S(2)}, u32[]{:S(2)}) async-start(bf16[32,128,128]{1,2,0:T(8,128)(2,1)} %bitcast.124), calls=%async_computation | async-start | bytes 2097152 | tf_op jit(solution)/shard_map/all_to_all | solution.py:64
  90.3 55.7 %collective-permute-start = (bf16[4096,1,2,64]{0,3,2,1:T(8,128)(2,1)}, bf16[4096,1,2,64]{0,3,2,1:T(8,128)(2,1)S(1)}, u32[]{:S(2)}, u32[]{:S(2)}) collective-permute-start(bf16[4096,1,2,64]{0,3,2,1:T(8,128)(2,1)} %get-tuple-element.123), channel_id=1, source_target_pairs={{480,0},{0,32},{32,64},{64,96},{96,128},{128,160},{160,192},{192,2... | collective-permute-start | bytes 3145736 | tf_op jit(solution)/shard_map/while/body/eval_jaxpr/ppermute | solution.py:12
  148.9 41.8 %collective-permute-start = (bf16[4096,1,2,64]{0,3,2,1:T(8,128)(2,1)}, bf16[4096,1,2,64]{0,3,2,1:T(8,128)(2,1)S(1)}, u32[]{:S(2)}, u32[]{:S(2)}) collective-permute-start(bf16[4096,1,2,64]{0,3,2,1:T(8,128)(2,1)} %get-tuple-element.123), channel_id=1, source_target_pairs={{480,0},{0,32},{32,64},{64,96},{96,128},{128,160},{160,192},{192,2... | collective-permute-start | bytes 3145736 | tf_op jit(solution)/shard_map/while/body/eval_jaxpr/ppermute | solution.py:12
  193.6 45.5 %collective-permute-start = (bf16[4096,1,2,64]{0,3,2,1:T(8,128)(2,1)}, bf16[4096,1,2,64]{0,3,2,1:T(8,128)(2,1)S(1)}, u32[]{:S(2)}, u32[]{:S(2)}) collective-permute-start(bf16[4096,1,2,64]{0,3,2,1:T(8,128)(2,1)} %get-tuple-element.123), channel_id=1, source_target_pairs={{480,0},{0,32},{32,64},{64,96},{96,128},{128,160},{160,192},{192,2... | collective-permute-start | bytes 3145736 | tf_op jit(solution)/shard_map/while/body/eval_jaxpr/ppermute | solution.py:12
  241.9 48.3 %collective-permute-start = (bf16[4096,1,2,64]{0,3,2,1:T(8,128)(2,1)}, bf16[4096,1,2,64]{0,3,2,1:T(8,128)(2,1)S(1)}, u32[]{:S(2)}, u32[]{:S(2)}) collective-permute-start(bf16[4096,1,2,64]{0,3,2,1:T(8,128)(2,1)} %get-tuple-element.123), channel_id=1, source_target_pairs={{480,0},{0,32},{32,64},{64,96},{96,128},{128,160},{160,192},{192,2... | collective-permute-start | bytes 3145736 | tf_op jit(solution)/shard_map/while/body/eval_jaxpr/ppermute | solution.py:12
  293.0 45.5 %collective-permute-start = (bf16[4096,1,2,64]{0,3,2,1:T(8,128)(2,1)}, bf16[4096,1,2,64]{0,3,2,1:T(8,128)(2,1)S(1)}, u32[]{:S(2)}, u32[]{:S(2)}) collective-permute-start(bf16[4096,1,2,64]{0,3,2,1:T(8,128)(2,1)} %get-tuple-element.123), channel_id=1, source_target_pairs={{480,0},{0,32},{32,64},{64,96},{96,128},{128,160},{160,192},{192,2... | collective-permute-start | bytes 3145736 | tf_op jit(solution)/shard_map/while/body/eval_jaxpr/ppermute | solution.py:12
  341.4 48.3 %collective-permute-start = (bf16[4096,1,2,64]{0,3,2,1:T(8,128)(2,1)}, bf16[4096,1,2,64]{0,3,2,1:T(8,128)(2,1)S(1)}, u32[]{:S(2)}, u32[]{:S(2)}) collective-permute-start(bf16[4096,1,2,64]{0,3,2,1:T(8,128)(2,1)} %get-tuple-element.123), channel_id=1, source_target_pairs={{480,0},{0,32},{32,64},{64,96},{96,128},{128,160},{160,192},{192,2... | collective-permute-start | bytes 3145736 | tf_op jit(solution)/shard_map/while/body/eval_jaxpr/ppermute | solution.py:12
  392.5 45.5 %collective-permute-start = (bf16[4096,1,2,64]{0,3,2,1:T(8,128)(2,1)}, bf16[4096,1,2,64]{0,3,2,1:T(8,128)(2,1)S(1)}, u32[]{:S(2)}, u32[]{:S(2)}) collective-permute-start(bf16[4096,1,2,64]{0,3,2,1:T(8,128)(2,1)} %get-tuple-element.123), channel_id=1, source_target_pairs={{480,0},{0,32},{32,64},{64,96},{96,128},{128,160},{160,192},{192,2... | collective-permute-start | bytes 3145736 | tf_op jit(solution)/shard_map/while/body/eval_jaxpr/ppermute | solution.py:12
  440.9 48.3 %collective-permute-start = (bf16[4096,1,2,64]{0,3,2,1:T(8,128)(2,1)}, bf16[4096,1,2,64]{0,3,2,1:T(8,128)(2,1)S(1)}, u32[]{:S(2)}, u32[]{:S(2)}) collective-permute-start(bf16[4096,1,2,64]{0,3,2,1:T(8,128)(2,1)} %get-tuple-element.123), channel_id=1, source_target_pairs={{480,0},{0,32},{32,64},{64,96},{96,128},{128,160},{160,192},{192,2... | collective-permute-start | bytes 3145736 | tf_op jit(solution)/shard_map/while/body/eval_jaxpr/ppermute | solution.py:12
  492.0 45.5 %collective-permute-start = (bf16[4096,1,2,64]{0,3,2,1:T(8,128)(2,1)}, bf16[4096,1,2,64]{0,3,2,1:T(8,128)(2,1)S(1)}, u32[]{:S(2)}, u32[]{:S(2)}) collective-permute-start(bf16[4096,1,2,64]{0,3,2,1:T(8,128)(2,1)} %get-tuple-element.123), channel_id=1, source_target_pairs={{480,0},{0,32},{32,64},{64,96},{96,128},{128,160},{160,192},{192,2... | collective-permute-start | bytes 3145736 | tf_op jit(solution)/shard_map/while/body/eval_jaxpr/ppermute | solution.py:12
  540.4 48.3 %collective-permute-start = (bf16[4096,1,2,64]{0,3,2,1:T(8,128)(2,1)}, bf16[4096,1,2,64]{0,3,2,1:T(8,128)(2,1)S(1)}, u32[]{:S(2)}, u32[]{:S(2)}) collective-permute-start(bf16[4096,1,2,64]{0,3,2,1:T(8,128)(2,1)} %get-tuple-element.123), channel_id=1, source_target_pairs={{480,0},{0,32},{32,64},{64,96},{96,128},{128,160},{160,192},{192,2... | collective-permute-start | bytes 3145736 | tf_op jit(solution)/shard_map/while/body/eval_jaxpr/ppermute | solution.py:12
  591.5 45.5 %collective-permute-start = (bf16[4096,1,2,64]{0,3,2,1:T(8,128)(2,1)}, bf16[4096,1,2,64]{0,3,2,1:T(8,128)(2,1)S(1)}, u32[]{:S(2)}, u32[]{:S(2)}) collective-permute-start(bf16[4096,1,2,64]{0,3,2,1:T(8,128)(2,1)} %get-tuple-element.123), channel_id=1, source_target_pairs={{480,0},{0,32},{32,64},{64,96},{96,128},{128,160},{160,192},{192,2... | collective-permute-start | bytes 3145736 | tf_op jit(solution)/shard_map/while/body/eval_jaxpr/ppermute | solution.py:12
  639.9 48.3 %collective-permute-start = (bf16[4096,1,2,64]{0,3,2,1:T(8,128)(2,1)}, bf16[4096,1,2,64]{0,3,2,1:T(8,128)(2,1)S(1)}, u32[]{:S(2)}, u32[]{:S(2)}) collective-permute-start(bf16[4096,1,2,64]{0,3,2,1:T(8,128)(2,1)} %get-tuple-element.123), channel_id=1, source_target_pairs={{480,0},{0,32},{32,64},{64,96},{96,128},{128,160},{160,192},{192,2... | collective-permute-start | bytes 3145736 | tf_op jit(solution)/shard_map/while/body/eval_jaxpr/ppermute | solution.py:12
  691.0 45.5 %collective-permute-start = (bf16[4096,1,2,64]{0,3,2,1:T(8,128)(2,1)}, bf16[4096,1,2,64]{0,3,2,1:T(8,128)(2,1)S(1)}, u32[]{:S(2)}, u32[]{:S(2)}) collective-permute-start(bf16[4096,1,2,64]{0,3,2,1:T(8,128)(2,1)} %get-tuple-element.123), channel_id=1, source_target_pairs={{480,0},{0,32},{32,64},{64,96},{96,128},{128,160},{160,192},{192,2... | collective-permute-start | bytes 3145736 | tf_op jit(solution)/shard_map/while/body/eval_jaxpr/ppermute | solution.py:12
  739.4 48.3 %collective-permute-start = (bf16[4096,1,2,64]{0,3,2,1:T(8,128)(2,1)}, bf16[4096,1,2,64]{0,3,2,1:T(8,128)(2,1)S(1)}, u32[]{:S(2)}, u32[]{:S(2)}) collective-permute-start(bf16[4096,1,2,64]{0,3,2,1:T(8,128)(2,1)} %get-tuple-element.123), channel_id=1, source_target_pairs={{480,0},{0,32},{32,64},{64,96},{96,128},{128,160},{160,192},{192,2... | collective-permute-start | bytes 3145736 | tf_op jit(solution)/shard_map/while/body/eval_jaxpr/ppermute | solution.py:12
  790.5 45.4 %collective-permute-start = (bf16[4096,1,2,64]{0,3,2,1:T(8,128)(2,1)}, bf16[4096,1,2,64]{0,3,2,1:T(8,128)(2,1)S(1)}, u32[]{:S(2)}, u32[]{:S(2)}) collective-permute-start(bf16[4096,1,2,64]{0,3,2,1:T(8,128)(2,1)} %get-tuple-element.123), channel_id=1, source_target_pairs={{480,0},{0,32},{32,64},{64,96},{96,128},{128,160},{160,192},{192,2... | collective-permute-start | bytes 3145736 | tf_op jit(solution)/shard_map/while/body/eval_jaxpr/ppermute | solution.py:12
where the time goes:
time: 870 us
  waiting for transfers between devices  733 us (84%)
  starting transfers between devices  49.5 us (6%)
  blocking collectives  29.3 us (3%)
  local copies, waits for them, and re-layouts  24.7 us (3%)
  matrix products  23.1 us (3%)
  other arithmetic  9.61 us (1%)
    ppermute x15, waiting for transfers between devices, from_behind(): return lax.ppermute(block, axis, route)  677 us
    all_to_all x1, waiting for transfers between devices, local(): lax.all_to_all(kv_send, 'uly', split_axis=0, concat_axis=0, tiled=True)  47.3 us
    all_to_all x1, blocking collectives, local(): lax.all_to_all(back_send, 'uly', split_axis=0, concat_axis=0, tiled=True)  29.3 us
    ppermute x15, starting transfers between devices, from_behind(): return lax.ppermute(block, axis, route)  28.8 us
  transfers between devices with their start and end apart: 17, of which 17 were waited for; matrix products, arithmetic and copies ran while one was open for 0% of the time, Pallas kernels for 0%

commit v1 on v0

v1 whole, which is shorter than its diff:
```python
import functools

import jax
import jax.numpy as jnp
from jax import lax
from jax.experimental import pallas as pl
from jax.experimental.pallas import tpu as pltpu
from jax.sharding import Mesh, PartitionSpec as P

HD = 64
HEADS = 16
PLANES = 16
ALL = ("y", "zh", "core", "x", "zl")
PLANE = ("y", "x")
DEPTH = ("zh", "zl")
F32 = jnp.float32
BF16 = jnp.bfloat16
VMEM = pl.BlockSpec(memory_space=pltpu.VMEM)


def lane_of(shape):
    return lax.broadcasted_iota(jnp.int32, shape, len(shape) - 1)


def pair_kv_kernel(k_ref, v_ref, out_ref):
    low = lane_of((128, 128)) < HD
    for pair in range(HEADS // 2):
        k = k_ref[:, pair * 128 : (pair + 1) * 128]
        v = v_ref[:, pair * 128 : (pair + 1) * 128]
        k_turned = pltpu.roll(k.astype(F32), HD, 1).astype(BF16)
        v_turned = pltpu.roll(v.astype(F32), HD, 1).astype(BF16)
        out_ref[2 * pair] = jnp.where(low, k, v_turned)
        out_ref[2 * pair + 1] = jnp.where(low, k_turned, v)


def pair_kv(k, v):
    return pl.pallas_call(
        pair_kv_kernel,
        out_shape=jax.ShapeDtypeStruct((HEADS, 128, 128), BF16),
        in_specs=[VMEM, VMEM],
        out_specs=VMEM,
        name="pair_kv",
    )(k, v)


def attend_kernel(q_tile, k_tile, q_ref, ka_ref, kb_ref, out_ref, va, vb):
    low = lane_of(ka_ref.shape) < HD
    va[...] = jnp.where(low, jnp.ones((), BF16), ka_ref[...])
    vb[...] = jnp.where(low, jnp.ones((), BF16), kb_ref[...])
    rows = ka_ref.shape[0]
    blocks = q_tile // 128
    low64 = lane_of((64, 128)) < HD

    def body(step, carry):
        parts = []
        for j in range(blocks):
            pair = q_ref[step * blocks + j].astype(F32) * HD**-0.5
            parts.append(jnp.where(low64, pair, 0.0))
            parts.append(jnp.where(low64, pltpu.roll(pair, HD, 1), 0.0))
        q = jnp.concatenate(parts, 0).astype(BF16)
        top, total = None, None
        for k_ref, v_ref in ((ka_ref, va), (kb_ref, vb)):
            for c in range(rows // k_tile):
                span = slice(c * k_tile, (c + 1) * k_tile)
                score = lax.dot_general(
                    q, k_ref[span], (((1,), (1,)), ((), ())), preferred_element_type=F32
                )
                here = jnp.max(score, 1, keepdims=True)
                new = here if top is None else jnp.maximum(top, here)
                weights = jnp.exp(score - new).astype(BF16)
                part = jnp.dot(weights, v_ref[span], preferred_element_type=F32)
                total = part if top is None else total * jnp.exp(top - new) + part
                top = new
        for j in range(blocks):
            span = slice(j * 128, (j + 1) * 128)
            whole = total[span]
            mixed = whole / jnp.where(lane_of(whole.shape) < HD, 1.0, pltpu.roll(whole, HD, 1))
            packed = jnp.where(low64, pltpu.roll(mixed[:64], HD, 1), mixed[64:])
            block = step * blocks + j
            out_ref[block, 0:64, :] = packed.astype(BF16)
            level = (jnp.log(whole) + top[span]).T[0:8]
            first = level.astype(BF16).astype(F32)
            second = (level - first).astype(BF16).astype(F32)
            third = level - first - second
            row = lax.broadcasted_iota(jnp.int32, (8, 128), 0)
            terms = jnp.where(row == 0, first, jnp.where(row == 1, second, third))
            out_ref[block, 64:80, :] = jnp.concatenate([terms, terms], 0).astype(BF16)
        return carry

    lax.fori_loop(0, q_ref.shape[0] // blocks, body, 0)


def attend(q, ka, kb, q_tile=1024, k_tile=512):
    n = q.shape[0]
    rows = ka.shape[0]
    return pl.pallas_call(
        functools.partial(attend_kernel, q_tile, k_tile),
        out_shape=jax.ShapeDtypeStruct((n, 80, 128), BF16),
        in_specs=[VMEM, VMEM, VMEM],
        out_specs=VMEM,
        scratch_shapes=[pltpu.VMEM(ka.shape, BF16), pltpu.VMEM(kb.shape, BF16)],
        compiler_params=pltpu.CompilerParams(vmem_limit_bytes=48 * 2**20),
        cost_estimate=pl.CostEstimate(
            flops=8 * n * 128 * rows * 128,
            bytes_accessed=2**21,
            transcendentals=2 * n * 128 * rows,
        ),
        name="attend",
    )(q, ka, kb)


def combine_kernel(part_ref, out_ref):
    n = part_ref.shape[0]
    levels = []
    for z in range(n):
        terms = part_ref[z, 64:80, :].astype(F32)
        levels.append(terms[0:1] + terms[1:2] + terms[2:3])
    level = jnp.concatenate(levels, 0)
    weight = jnp.exp(level - jnp.max(level, 0, keepdims=True))
    weight = weight / jnp.sum(weight, 0, keepdims=True)
    weight = jnp.concatenate([weight, jnp.zeros((128 - n, 128), F32)], 0).T
    low64 = lane_of((64, 128)) < HD
    total = jnp.zeros((64, 128), F32)
    for z in range(n):
        column = weight[:, z : z + 1]
        total += jnp.where(low64, column[:64], column[64:]) * part_ref[z, 0:64, :].astype(F32)
    out_ref[...] = total.astype(BF16)


def combine(parts):
    return pl.pallas_call(
        combine_kernel,
        out_shape=jax.ShapeDtypeStruct((64, 128), BF16),
        in_specs=[VMEM],
        out_specs=VMEM,
        name="combine",
    )(parts)


def exchange(blocks, axes):
    return lax.all_to_all(blocks, axes, split_axis=0, concat_axis=0, tiled=True)


def local(queries, keys, values, w_out):
    q_send = queries.reshape(2, 4, HEADS, HD).transpose(2, 1, 0, 3).reshape(HEADS, 4, 128)
    q_plane = exchange(q_send, PLANE).reshape(64, 128)
    q_all = exchange(jnp.broadcast_to(q_plane, (PLANES, 64, 128)), DEPTH)
    kv = exchange(pair_kv(keys, values), PLANE).reshape(HEADS * 128, 128)
    kv_other = lax.ppermute(kv, "core", [(0, 1), (1, 0)])
    parts = exchange(attend(q_all, kv, kv_other), DEPTH)
    attended = combine(parts).reshape(HEADS, 4, 128)
    rows = exchange(attended, PLANE).reshape(HEADS, 4, 2, HD)
    rows = rows.transpose(2, 1, 0, 3).reshape(8, HEADS * HD)
    return jnp.dot(rows, w_out, preferred_element_type=F32).astype(BF16)


def solution(mesh):
    split = Mesh(mesh.devices.reshape(4, 2, 2, 4, 8), ALL)
    return jax.shard_map(
        local,
        mesh=split,
        in_specs=(P(ALL, None), P(ALL, None), P(ALL, None), P()),
        out_specs=P(ALL, None),
        check_vma=False,
    )
```

time: 870 us -> 112 us (0.13)
  the two profiles are of different devices: /device:TPU:2 before, /device:TPU:32 now
where the time goes in v1:
time: 112 us
  blocking collectives  49.1 us (44%)
  starting transfers between devices  24.2 us (22%)
  waiting for transfers between devices  19.8 us (18%)
  Pallas kernels  15 us (13%)
  local copies, waits for them, and re-layouts  2.66 us (2%)
    all_to_all x3, blocking collectives, exchange(): return lax.all_to_all(blocks, axes, split_axis=0, concat_axis=0, tiled=True)  49.1 us
    all_to_all x2, starting transfers between devices, exchange(): return lax.all_to_all(blocks, axes, split_axis=0, concat_axis=0, tiled=True)  22.2 us
    all_to_all x2, waiting for transfers between devices, exchange(): return lax.all_to_all(blocks, axes, split_axis=0, concat_axis=0, tiled=True)  19.8 us
    pallas_call x1, Pallas kernels, attend(): pl.pallas_call(functools.partial(attend_kernel, q_tile, k_tile), out_shap...  10.9 us
  transfers between devices with their start and end apart: 3, of which 2 were waited for; matrix products, arithmetic and copies ran while one was open for 0% of the time, Pallas kernels for 2%

profile of v1, /device:TPU:32, one launch (start us, length us, event | category | flops | bytes accessed | tf_op | source)
XLA Modules:
  0.0 111.7 jit_solution(10046103487188357490)
XLA Ops:
  0.0 0.0 copy-start
  0.0 1.0 reshape.21
  1.0 0.1 reshape.22
  1.1 0.6 copy.11
  1.7 7.0 %all-to-all-start = ((bf16[16,4,128]{2,1,0:T(4,128)(2,1)}), bf16[16,4,128]{2,1,0:T(4,128)(2,1)S(1)}, u32[]{:S(2)}, u32[]{:S(2)}) async-start(bf16[16,4,128]{2,1,0:T(4,128)(2,1)} %copy.11), calls=%async_computation | async-start | bytes 32768 | tf_op jit(solution)/shard_map/all_to_all | solution.py:141
  8.8 2.0 %pair_kv.1 = bf16[16,128,128]{2,1,0:T(8,128)(2,1)} custom-call(bf16[128,1024]{1,0:T(8,128)(2,1)} %k_ref.1, bf16[128,1024]{1,0:T(8,128)(2,1)} %v_ref.1), custom_call_target="tpu_custom_call" | custom-call | tf_op jit(solution)/shard_map/pair_kv/pallas_call | solution.py:37
  10.8 5.6 %all-to-all-done = bf16[16,4,128]{2,1,0:T(4,128)(2,1)S(1)} async-done(((bf16[16,4,128]{2,1,0:T(4,128)(2,1)}), bf16[16,4,128]{2,1,0:T(4,128)(2,1)S(1)}, u32[]{:S(2)}, u32[]{:S(2)}) %all-to-all-start) | async-done | bytes 16416 | tf_op jit(solution)/shard_map/all_to_all | solution.py:141
  16.3 14.0 %all_to_all.25 = bf16[16,128,128]{2,1,0:T(8,128)(2,1)S(1)} all-to-all(bf16[16,128,128]{2,1,0:T(8,128)(2,1)} %pair_kv.1), channel_id=1, replica_groups=mesh['y'=4,'zh'=2,'core'=2,'x'=4,'zl'=8] {'y','x'}, dimensions={0} | all-to-all | bytes 1048576 | tf_op jit(solution)/shard_map/all_to_all | solution.py:141
  30.3 0.7 broadcast_in_dim.3
  31.0 15.2 %all-to-all-start.1 = ((bf16[16,64,128]{2,1,0:T(8,128)(2,1)}), bf16[16,64,128]{2,1,0:T(8,128)(2,1)S(1)}, u32[]{:S(2)}, u32[]{:S(2)}) async-start(bf16[16,64,128]{2,1,0:T(8,128)(2,1)} %broadcast_in_dim.3), calls=%async_computation.1 | async-start | bytes 524288 | tf_op jit(solution)/shard_map/all_to_all | solution.py:141
  46.3 1.9 %collective-permute-start = (bf16[2048,128]{1,0:T(8,128)(2,1)S(1)}, bf16[2048,128]{1,0:T(8,128)(2,1)S(1)}, u32[]{:S(2)}, u32[]{:S(2)}) collective-permute-start(bf16[2048,128]{1,0:T(8,128)(2,1)S(1)} %bitcast.15), channel_id=1, source_target_pairs={{0,32},{32,0},{1,33},{33,1},{2,34},{34,2},{3,35},{35,3},{4,36},{36... | collective-permute-start | bytes 1572872 | tf_op jit(solution)/shard_map/ppermute | solution.py:149
  48.2 14.2 %all-to-all-done.1.q_ref = bf16[16,64,128]{2,1,0:T(8,128)(2,1)S(1)} async-done(((bf16[16,64,128]{2,1,0:T(8,128)(2,1)}), bf16[16,64,128]{2,1,0:T(8,128)(2,1)S(1)}, u32[]{:S(2)}, u32[]{:S(2)}) %all-to-all-start.1) | async-done | bytes 262176 | tf_op jit(solution)/shard_map/all_to_all | solution.py:141
  62.4 0.0 collective-permute-done.kb_ref
  62.4 10.9 %attend.1 = bf16[16,80,128]{2,1,0:T(8,128)(2,1)S(1)} custom-call(bf16[16,64,128]{2,1,0:T(8,128)(2,1)S(1)} %all-to-all-done.1.q_ref, bf16[2048,128]{1,0:T(8,128)(2,1)S(1)} %bitcast.16, bf16[2048,128]{1,0:T(8,128)(2,1)S(1)} %collective-permute-done.kb_ref), custom_call_target="tpu_custom_call" | custom-call | flops 4294967296 | bytes 2097152 | tf_op jit(solution)/shard_map/attend/pallas_call | solution.py:96
  73.2 24.1 %all_to_all.26.part_ref = bf16[16,80,128]{2,1,0:T(8,128)(2,1)} all-to-all(bf16[16,80,128]{2,1,0:T(8,128)(2,1)S(1)} %attend.1), channel_id=1, replica_groups=mesh['y'=4,'zh'=2,'core'=2,'x'=4,'zl'=8] {'zh','zl'}, dimensions={0} | all-to-all | bytes 655360 | tf_op jit(solution)/shard_map/all_to_all | solution.py:141
  97.4 2.1 %combine.1 = bf16[64,128]{1,0:T(8,128)(2,1)} custom-call(bf16[16,80,128]{2,1,0:T(8,128)(2,1)} %all_to_all.26.part_ref), custom_call_target="tpu_custom_call" | custom-call | tf_op jit(solution)/shard_map/combine/pallas_call | solution.py:131
  99.5 11.0 %all_to_all.27 = bf16[16,4,128]{2,1,0:T(4,128)(2,1)S(1)} all-to-all(bf16[16,4,128]{2,1,0:T(4,128)(2,1)} %bitcast.20), channel_id=1, replica_groups=mesh['y'=4,'zh'=2,'core'=2,'x'=4,'zl'=8] {'y','x'}, dimensions={0} | all-to-all | bytes 32768 | tf_op jit(solution)/shard_map/all_to_all | solution.py:141
  110.5 0.1 reshape.26
  110.6 0.1 reshape.27
  110.7 0.0 copy-done
  110.7 1.0 convolution_convert_fusion
  (3 shorter events, 0.1 us)
Async XLA Ops:
  0.0 110.7 %copy-start = (bf16[1024,1024]{1,0:T(8,128)(2,1)S(1)}, bf16[1024,1024]{1,0:T(8,128)(2,1)}, u32[]{:S(2)}) copy-start(bf16[1024,1024]{1,0:T(8,128)(2,1)} %param.7) | copy-start | bytes 6291460
  1.7 14.6 %all-to-all-start = ((bf16[16,4,128]{2,1,0:T(4,128)(2,1)}), bf16[16,4,128]{2,1,0:T(4,128)(2,1)S(1)}, u32[]{:S(2)}, u32[]{:S(2)}) async-start(bf16[16,4,128]{2,1,0:T(4,128)(2,1)} %copy.11), calls=%async_computation | async-start | bytes 32768 | tf_op jit(solution)/shard_map/all_to_all | solution.py:141
  31.0 31.3 %all-to-all-start.1 = ((bf16[16,64,128]{2,1,0:T(8,128)(2,1)}), bf16[16,64,128]{2,1,0:T(8,128)(2,1)S(1)}, u32[]{:S(2)}, u32[]{:S(2)}) async-start(bf16[16,64,128]{2,1,0:T(8,128)(2,1)} %broadcast_in_dim.3), calls=%async_computation.1 | async-start | bytes 524288 | tf_op jit(solution)/shard_map/all_to_all | solution.py:141
  46.3 16.1 %collective-permute-start = (bf16[2048,128]{1,0:T(8,128)(2,1)S(1)}, bf16[2048,128]{1,0:T(8,128)(2,1)S(1)}, u32[]{:S(2)}, u32[]{:S(2)}) collective-permute-start(bf16[2048,128]{1,0:T(8,128)(2,1)S(1)} %bitcast.15), channel_id=1, source_target_pairs={{0,32},{32,0},{1,33},{33,1},{2,34},{34,2},{3,35},{35,3},{4,36},{36... | collective-permute-start | bytes 1572872 | tf_op jit(solution)/shard_map/ppermute | solution.py:149

commit v2 on v1

--- a/solution.py
+++ b/solution.py
@@ -22,31 +22,44 @@
     return lax.broadcasted_iota(jnp.int32, shape, len(shape) - 1)
 
 
-def pair_kv_kernel(k_ref, v_ref, out_ref):
+def pack_kernel(q_ref, k_ref, v_ref, out_ref):
     low = lane_of((128, 128)) < HD
+    low4 = lane_of((4, 128)) < HD
+    rest = jnp.zeros((12, 128), F32)
     for pair in range(HEADS // 2):
-        k = k_ref[:, pair * 128 : (pair + 1) * 128]
-        v = v_ref[:, pair * 128 : (pair + 1) * 128]
+        span = slice(pair * 128, (pair + 1) * 128)
+        k = k_ref[:, span]
+        v = v_ref[:, span]
         k_turned = pltpu.roll(k.astype(F32), HD, 1).astype(BF16)
         v_turned = pltpu.roll(v.astype(F32), HD, 1).astype(BF16)
-        out_ref[2 * pair] = jnp.where(low, k, v_turned)
-        out_ref[2 * pair + 1] = jnp.where(low, k_turned, v)
+        out_ref[2 * pair, 0:128, :] = jnp.where(low, k, v_turned)
+        out_ref[2 * pair + 1, 0:128, :] = jnp.where(low, k_turned, v)
+        q = q_ref[:, span].astype(F32)
+        q_turned = pltpu.roll(q, HD, 1)
+        even = jnp.where(low4, q[0:4], q_turned[4:8])
+        odd = jnp.where(low4, q_turned[0:4], q[4:8])
+        out_ref[2 * pair, 128:144, :] = jnp.concatenate([even, rest], 0).astype(BF16)
+        out_ref[2 * pair + 1, 128:144, :] = jnp.concatenate([odd, rest], 0).astype(BF16)
 
 
-def pair_kv(k, v):
+def pack(q, k, v):
     return pl.pallas_call(
-        pair_kv_kernel,
-        out_shape=jax.ShapeDtypeStruct((HEADS, 128, 128), BF16),
-        in_specs=[VMEM, VMEM],
+        pack_kernel,
+        out_shape=jax.ShapeDtypeStruct((HEADS, 144, 128), BF16),
+        in_specs=[VMEM, VMEM, VMEM],
         out_specs=VMEM,
-        name="pair_kv",
-    )(k, v)
+        name="pack",
+    )(q, k, v)
 
 
-def attend_kernel(q_tile, k_tile, q_ref, ka_ref, kb_ref, out_ref, va, vb):
-    low = lane_of(ka_ref.shape) < HD
-    va[...] = jnp.where(low, jnp.ones((), BF16), ka_ref[...])
-    vb[...] = jnp.where(low, jnp.ones((), BF16), kb_ref[...])
+def attend_kernel(q_tile, k_tile, q_ref, kva_ref, kvb_ref, out_ref, ka_ref, va, kb_ref, vb):
+    low = lane_of((128, 128)) < HD
+    for source in range(HEADS):
+        span = slice(source * 128, (source + 1) * 128)
+        for kv_ref, k_ref, v_ref in ((kva_ref, ka_ref, va), (kvb_ref, kb_ref, vb)):
+            block = kv_ref[source, 0:128, :]
+            k_ref[span] = block
+            v_ref[span] = jnp.where(low, jnp.ones((), BF16), block)
     rows = ka_ref.shape[0]
     blocks = q_tile // 128
     low64 = lane_of((64, 128)) < HD
@@ -90,15 +103,15 @@
     lax.fori_loop(0, q_ref.shape[0] // blocks, body, 0)
 
 
-def attend(q, ka, kb, q_tile=1024, k_tile=512):
+def attend(q, kva, kvb, q_tile=1024, k_tile=512):
     n = q.shape[0]
-    rows = ka.shape[0]
+    rows = HEADS * 128
     return pl.pallas_call(
         functools.partial(attend_kernel, q_tile, k_tile),
         out_shape=jax.ShapeDtypeStruct((n, 80, 128), BF16),
         in_specs=[VMEM, VMEM, VMEM],
         out_specs=VMEM,
-        scratch_shapes=[pltpu.VMEM(ka.shape, BF16), pltpu.VMEM(kb.shape, BF16)],
+        scratch_shapes=[pltpu.VMEM((rows, 128), BF16)] * 4,
         compiler_params=pltpu.CompilerParams(vmem_limit_bytes=48 * 2**20),
         cost_estimate=pl.CostEstimate(
             flops=8 * n * 128 * rows * 128,
@@ -106,7 +119,7 @@
             transcendentals=2 * n * 128 * rows,
         ),
         name="attend",
-    )(q, ka, kb)
+    )(q, kva, kvb)
 
 
 def combine_kernel(part_ref, out_ref):
@@ -142,12 +155,11 @@
 
 
 def local(queries, keys, values, w_out):
-    q_send = queries.reshape(2, 4, HEADS, HD).transpose(2, 1, 0, 3).reshape(HEADS, 4, 128)
-    q_plane = exchange(q_send, PLANE).reshape(64, 128)
+    held = exchange(pack(queries, keys, values), PLANE)
+    held_other = lax.ppermute(held, "core", [(0, 1), (1, 0)])
+    q_plane = held[:, 128:132, :].reshape(1, 64, 128)
     q_all = exchange(jnp.broadcast_to(q_plane, (PLANES, 64, 128)), DEPTH)
-    kv = exchange(pair_kv(keys, values), PLANE).reshape(HEADS * 128, 128)
-    kv_other = lax.ppermute(kv, "core", [(0, 1), (1, 0)])
-    parts = exchange(attend(q_all, kv, kv_other), DEPTH)
+    parts = exchange(attend(q_all, held, held_other), DEPTH)
     attended = combine(parts).reshape(HEADS, 4, 128)
     rows = exchange(attended, PLANE).reshape(HEADS, 4, 2, HD)
     rows = rows.transpose(2, 1, 0, 3).reshape(8, HEADS * HD)

time: 112 us -> 105 us (0.938)
  the two profiles are of different devices: /device:TPU:32 before, /device:TPU:64 now
where the time goes in v2:
time: 105 us
  blocking collectives  55.9 us (53%)
  starting transfers between devices  16.7 us (16%)
  Pallas kernels  15.3 us (15%)
  waiting for transfers between devices  14.9 us (14%)
    all_to_all x3, blocking collectives, exchange(): return lax.all_to_all(blocks, axes, split_axis=0, concat_axis=0, tiled=True)  55.9 us
    all_to_all x1, starting transfers between devices, exchange(): return lax.all_to_all(blocks, axes, split_axis=0, concat_axis=0, tiled=True)  14.8 us
    all_to_all x1, waiting for transfers between devices, exchange(): return lax.all_to_all(blocks, axes, split_axis=0, concat_axis=0, tiled=True)  13 us
    pallas_call x1, Pallas kernels, attend(): pl.pallas_call(functools.partial(attend_kernel, q_tile, k_tile), out_shap...  11 us
    pallas_call x1, Pallas kernels, pack(): pl.pallas_call(pack_kernel, out_shape=jax.ShapeDtypeStruct((HEADS, 144, 1...  2.23 us
    pallas_call x1, Pallas kernels, combine(): pl.pallas_call(combine_kernel, out_shape=jax.ShapeDtypeStruct((64, 128),...  2.11 us
  transfers between devices with their start and end apart: 2, of which 2 were waited for; matrix products, arithmetic and copies ran while one was open for 0% of the time, Pallas kernels for 0%

profile of v2, /device:TPU:64, one launch (start us, length us, event | category | flops | bytes accessed | tf_op | source)
XLA Modules:
  0.0 104.8 jit_solution(8825652914987386903)
XLA Ops:
  0.0 0.0 copy-start
  0.0 2.2 %pack.1 = bf16[16,144,128]{2,1,0:T(8,128)(2,1)} custom-call(bf16[8,1024]{1,0:T(8,128)(2,1)} %q_ref.1, bf16[128,1024]{1,0:T(8,128)(2,1)} %k_ref.1, bf16[128,1024]{1,0:T(8,128)(2,1)} %v_ref.1), custom_call_target="tpu_custom_call" | custom-call | tf_op jit(solution)/shard_map/pack/pallas_call | solution.py:46
  2.2 19.3 %all_to_all.20.kva_ref = bf16[16,144,128]{2,1,0:T(8,128)(2,1)S(1)} all-to-all(bf16[16,144,128]{2,1,0:T(8,128)(2,1)} %pack.1), channel_id=1, replica_groups=mesh['y'=4,'zh'=2,'core'=2,'x'=4,'zl'=8] {'y','x'}, dimensions={0} | all-to-all | bytes 1179648 | tf_op jit(solution)/shard_map/all_to_all | solution.py:154
  21.5 0.7 broadcast_in_dim.8
  22.3 14.8 %all-to-all-start.1 = ((bf16[16,64,128]{2,1,0:T(8,128)(2,1)}), bf16[16,64,128]{2,1,0:T(8,128)(2,1)S(1)}, u32[]{:S(2)}, u32[]{:S(2)}) async-start(bf16[16,64,128]{2,1,0:T(8,128)(2,1)} %broadcast_in_dim.8), calls=%async_computation.1 | async-start | bytes 524288 | tf_op jit(solution)/shard_map/all_to_all | solution.py:154
  37.0 1.9 %collective-permute-start = (bf16[16,144,128]{2,1,0:T(8,128)(2,1)S(1)}, bf16[16,144,128]{2,1,0:T(8,128)(2,1)S(1)}, u32[]{:S(2)}, u32[]{:S(2)}) collective-permute-start(bf16[16,144,128]{2,1,0:T(8,128)(2,1)S(1)} %all_to_all.20.kva_ref), channel_id=1, source_target_pairs={{0,32},{32,0},{1,33},{33,1},{2,34},{34,2},{3,35},{35,3},{4,36},{36... | collective-permute-start | bytes 1769480 | tf_op jit(solution)/shard_map/ppermute | solution.py:159
  39.0 2.0 %collective-permute-done.kvb_ref = bf16[16,144,128]{2,1,0:T(8,128)(2,1)S(1)} collective-permute-done((bf16[16,144,128]{2,1,0:T(8,128)(2,1)S(1)}, bf16[16,144,128]{2,1,0:T(8,128)(2,1)S(1)}, u32[]{:S(2)}, u32[]{:S(2)}) %collective-permute-start) | collective-permute-done | bytes 589856 | tf_op jit(solution)/shard_map/ppermute | solution.py:159
  40.9 13.0 %all-to-all-done.1.q_ref = bf16[16,64,128]{2,1,0:T(8,128)(2,1)S(1)} async-done(((bf16[16,64,128]{2,1,0:T(8,128)(2,1)}), bf16[16,64,128]{2,1,0:T(8,128)(2,1)S(1)}, u32[]{:S(2)}, u32[]{:S(2)}) %all-to-all-start.1) | async-done | bytes 262176 | tf_op jit(solution)/shard_map/all_to_all | solution.py:154
  53.9 11.0 %attend.1 = bf16[16,80,128]{2,1,0:T(8,128)(2,1)S(1)} custom-call(bf16[16,64,128]{2,1,0:T(8,128)(2,1)S(1)} %all-to-all-done.1.q_ref, bf16[16,144,128]{2,1,0:T(8,128)(2,1)S(1)} %all_to_all.20.kva_ref, bf16[16,144,128]{2,1,0:T(8,128)(2,1)S(1)} %collective-permute-done.kvb_ref), custom_call_target="tpu_custom_call" | custom-call | flops 4294967296 | bytes 2097152 | tf_op jit(solution)/shard_map/attend/pallas_call | solution.py:109
  64.9 25.1 %all_to_all.21.part_ref = bf16[16,80,128]{2,1,0:T(8,128)(2,1)} all-to-all(bf16[16,80,128]{2,1,0:T(8,128)(2,1)S(1)} %attend.1), channel_id=1, replica_groups=mesh['y'=4,'zh'=2,'core'=2,'x'=4,'zl'=8] {'zh','zl'}, dimensions={0} | all-to-all | bytes 655360 | tf_op jit(solution)/shard_map/all_to_all | solution.py:154
  90.0 2.1 %combine.1 = bf16[64,128]{1,0:T(8,128)(2,1)} custom-call(bf16[16,80,128]{2,1,0:T(8,128)(2,1)} %all_to_all.21.part_ref), custom_call_target="tpu_custom_call" | custom-call | tf_op jit(solution)/shard_map/combine/pallas_call | solution.py:144
  92.1 11.5 %all_to_all.22 = bf16[16,4,128]{2,1,0:T(4,128)(2,1)S(1)} all-to-all(bf16[16,4,128]{2,1,0:T(4,128)(2,1)} %bitcast.11), channel_id=1, replica_groups=mesh['y'=4,'zh'=2,'core'=2,'x'=4,'zl'=8] {'y','x'}, dimensions={0} | all-to-all | bytes 32768 | tf_op jit(solution)/shard_map/all_to_all | solution.py:154
  103.6 0.1 reshape.12
  103.7 0.1 reshape.13
  103.8 0.0 copy-done
  103.8 1.0 convolution_convert_fusion
  (3 shorter events, 0.0 us)
Async XLA Ops:
  0.0 103.8 %copy-start = (bf16[1024,1024]{1,0:T(8,128)(2,1)S(1)}, bf16[1024,1024]{1,0:T(8,128)(2,1)}, u32[]{:S(2)}) copy-start(bf16[1024,1024]{1,0:T(8,128)(2,1)} %param.7) | copy-start | bytes 6291460
  22.3 31.6 %all-to-all-start.1 = ((bf16[16,64,128]{2,1,0:T(8,128)(2,1)}), bf16[16,64,128]{2,1,0:T(8,128)(2,1)S(1)}, u32[]{:S(2)}, u32[]{:S(2)}) async-start(bf16[16,64,128]{2,1,0:T(8,128)(2,1)} %broadcast_in_dim.8), calls=%async_computation.1 | async-start | bytes 524288 | tf_op jit(solution)/shard_map/all_to_all | solution.py:154
  37.0 3.9 %collective-permute-start = (bf16[16,144,128]{2,1,0:T(8,128)(2,1)S(1)}, bf16[16,144,128]{2,1,0:T(8,128)(2,1)S(1)}, u32[]{:S(2)}, u32[]{:S(2)}) collective-permute-start(bf16[16,144,128]{2,1,0:T(8,128)(2,1)S(1)} %all_to_all.20.kva_ref), channel_id=1, source_target_pairs={{0,32},{32,0},{1,33},{33,1},{2,34},{34,2},{3,35},{35,3},{4,36},{36... | collective-permute-start | bytes 1769480 | tf_op jit(solution)/shard_map/ppermute | solution.py:159

commit v3 on v2

v3 whole, which is shorter than its diff:
```python
import functools

import jax
import jax.numpy as jnp
from jax import lax
from jax.experimental import pallas as pl
from jax.experimental.pallas import tpu as pltpu
from jax.sharding import Mesh, PartitionSpec as P

HD = 64
HEADS = 16
STEPS = 8
ALL = ("y", "zh", "core", "xa", "xb", "zq", "zo")
PLACE = ("y", "xa", "zo")
DEPTH = ("zh", "zq")
F32 = jnp.float32
BF16 = jnp.bfloat16
VMEM = pl.BlockSpec(memory_space=pltpu.VMEM)


def iota(shape, dim):
    return lax.broadcasted_iota(jnp.int32, shape, dim)


def pack_kernel(q_ref, k_ref, v_ref, out_ref):
    low = iota((128, 128), 1) < HD
    low4 = iota((4, 128), 1) < HD
    rest = jnp.zeros((12, 128), F32)
    for pair in range(HEADS // 2):
        span = slice(pair * 128, (pair + 1) * 128)
        k = k_ref[:, span]
        v = v_ref[:, span]
        k_turned = pltpu.roll(k.astype(F32), HD, 1).astype(BF16)
        v_turned = pltpu.roll(v.astype(F32), HD, 1).astype(BF16)
        out_ref[2 * pair, 0:128, :] = jnp.where(low, k, v_turned)
        out_ref[2 * pair + 1, 0:128, :] = jnp.where(low, k_turned, v)
        q = q_ref[:, span].astype(F32)
        q_turned = pltpu.roll(q, HD, 1)
        even = jnp.where(low4, q[0:4], q_turned[4:8])
        odd = jnp.where(low4, q_turned[0:4], q[4:8])
        out_ref[2 * pair, 128:144, :] = jnp.concatenate([even, rest], 0).astype(BF16)
        out_ref[2 * pair + 1, 128:144, :] = jnp.concatenate([odd, rest], 0).astype(BF16)


def pack(q, k, v):
    return pl.pallas_call(
        pack_kernel,
        out_shape=jax.ShapeDtypeStruct((HEADS, 144, 128), BF16),
        in_specs=[VMEM, VMEM, VMEM],
        out_specs=VMEM,
        name="pack",
    )(q, k, v)


def attend_kernel(group, q_ref, *refs):
    kv_refs, out_ref = refs[:4], refs[4]
    low64 = iota((64, 128), 1) < HD
    rows = group * 128
    low = iota((rows, 128), 1) < HD
    parts = []
    for step in range(STEPS):
        pair = q_ref[step].astype(F32) * HD**-0.5
        parts.append(jnp.where(low64, pair, 0.0))
        parts.append(jnp.where(low64, pltpu.roll(pair, HD, 1), 0.0))
    q = jnp.concatenate(parts, 0).astype(BF16)
    top, total = None, None
    for kv_ref in kv_refs:
        for c in range(HEADS // group):
            kv = kv_ref[c * group : (c + 1) * group, 0:128, :].reshape(rows, 128)
            score = lax.dot_general(
                q, kv, (((1,), (1,)), ((), ())), preferred_element_type=F32
            )
            here = jnp.max(score, 1, keepdims=True)
            new = here if top is None else jnp.maximum(top, here)
            weights = jnp.exp(score - new).astype(BF16)
            marked = jnp.where(low, jnp.ones((), BF16), kv)
            part = jnp.dot(weights, marked, preferred_element_type=F32)
            total = part if top is None else total * jnp.exp(top - new) + part
            top = new
    sub = iota((64, 128), 0) % 8 < 4
    first_half = iota((64, 128), 1) % HD < HD // 2
    for step in range(STEPS):
        a = total[step * 128 : step * 128 + 64]
        b = total[step * 128 + 64 : step * 128 + 128]
        weight = jnp.where(low64, a, pltpu.roll(b, HD, 1))
        mixed = jnp.where(low64, pltpu.roll(a, HD, 1), b) / weight
        highest = jnp.where(
            low64, top[step * 128 : step * 128 + 64], top[step * 128 + 64 : step * 128 + 128]
        )
        level = jnp.log(weight) + highest
        first = level.astype(BF16).astype(F32)
        level = jnp.where(first_half, first, level - first)
        mixed_turned = pltpu.roll(mixed.reshape(8, 8, 128), 4, 1).reshape(64, 128)
        level_turned = pltpu.roll(level.reshape(8, 8, 128), 4, 1).reshape(64, 128)
        even = jnp.where(sub, mixed, level_turned).reshape(8, 8, 128)
        odd = jnp.where(sub, mixed_turned, level).reshape(8, 8, 128)
        both = jnp.stack([even, odd], 1).reshape(128, 128)
        out_ref[step * 128 : (step + 1) * 128, :] = both.astype(BF16)


def attend(q, kvs, group=2):
    rows = len(kvs) * HEADS * 128
    return pl.pallas_call(
        functools.partial(attend_kernel, group),
        out_shape=jax.ShapeDtypeStruct((STEPS * 128, 128), BF16),
        in_specs=[VMEM] * (1 + len(kvs)),
        out_specs=VMEM,
        compiler_params=pltpu.CompilerParams(vmem_limit_bytes=48 * 2**20),
        cost_estimate=pl.CostEstimate(
            flops=4 * STEPS * 128 * rows * 128,
            bytes_accessed=2**22,
            transcendentals=STEPS * 128 * rows,
        ),
        name="attend",
    )(q, *kvs)


def finish_kernel(part_ref, w_ref, out_ref):
    near = iota((HEADS * 8, 128), 1) % HD < HD // 2
    blocks, levels = [], []
    for step in range(STEPS):
        block = part_ref[step * HEADS * 8 : (step + 1) * HEADS * 8, :].astype(F32)
        other = jnp.where(near, pltpu.roll(block, 96, 1), pltpu.roll(block, 32, 1))
        level = (block + other).reshape(HEADS, 8, 128)
        blocks.append(block.reshape(HEADS, 8, 128))
        levels.append(pltpu.roll(level, 4, 1))
    top = functools.reduce(jnp.maximum, levels)
    weights = [jnp.exp(level - top) for level in levels]
    mixed = sum(w * b for w, b in zip(weights, blocks)) / sum(weights)
    turned = pltpu.roll(mixed, HD, 2)
    low = iota((8, 128), 1) < HD
    upper = iota((8, 128), 0) < 4
    tiles = []
    for pair in range(HEADS // 2):
        head = jnp.where(low, mixed[2 * pair], turned[2 * pair + 1])
        tail = jnp.where(low, turned[2 * pair], mixed[2 * pair + 1])
        tiles.append(jnp.where(upper, head, pltpu.roll(tail, 4, 0)))
    rows = jnp.concatenate(tiles, 1).astype(BF16)
    out_ref[...] = jnp.dot(rows, w_ref[...], preferred_element_type=F32).astype(BF16)


def finish(parts, w_out):
    return pl.pallas_call(
        finish_kernel,
        out_shape=jax.ShapeDtypeStruct((8, HEADS * HD), BF16),
        in_specs=[VMEM, VMEM],
        out_specs=VMEM,
        name="finish",
    )(parts, w_out)


def exchange(blocks, axes):
    return lax.all_to_all(blocks, axes, split_axis=0, concat_axis=0, tiled=True)


def swap(block, axis):
    return lax.ppermute(block, axis, [(0, 1), (1, 0)])


def local(queries, keys, values, w_out):
    held = exchange(pack(queries, keys, values), PLACE)
    held_x = swap(held, "xb")
    held_core = swap(held, "core")
    q_place = held[:, 128:132, :].reshape(1, 64, 128)
    q_all = exchange(jnp.broadcast_to(q_place, (STEPS, 64, 128)), DEPTH)
    held_x, q_all = lax.optimization_barrier((held_x, q_all))
    held_both = swap(held_x, "core")
    parts = attend(q_all, (held, held_core, held_x, held_both))
    parts = exchange(parts.reshape(STEPS * HEADS, 8, 128), DEPTH + PLACE)
    return finish(parts.reshape(STEPS * HEADS * 8, 128), w_out)


def solution(mesh):
    split = Mesh(mesh.devices.reshape(4, 2, 2, 2, 2, 4, 2), ALL)
    return jax.shard_map(
        local,
        mesh=split,
        in_specs=(P(ALL, None), P(ALL, None), P(ALL, None), P()),
        out_specs=P(ALL, None),
        check_vma=False,
    )
```

time: 105 us -> 104 us (level)
  the two profiles are of different devices: /device:TPU:64 before, /device:TPU:2 now
where the time goes in v3:
time: 104 us
  blocking collectives  52.9 us (51%)
  starting transfers between devices  21.3 us (20%)
  Pallas kernels  14.4 us (14%)
  waiting for transfers between devices  14.1 us (14%)
    all_to_all x2, blocking collectives, exchange(): return lax.all_to_all(blocks, axes, split_axis=0, concat_axis=0, tiled=True)  52.9 us
    all_to_all x1, starting transfers between devices, exchange(): return lax.all_to_all(blocks, axes, split_axis=0, concat_axis=0, tiled=True)  14.2 us
    all_to_all x1, waiting for transfers between devices, exchange(): return lax.all_to_all(blocks, axes, split_axis=0, concat_axis=0, tiled=True)  12.2 us
    pallas_call x1, Pallas kernels, attend(): pl.pallas_call(functools.partial(attend_kernel, group), out_shape=jax.Sha...  9.38 us
    ppermute x3, starting transfers between devices, swap(): return lax.ppermute(block, axis, [(0, 1), (1, 0)])  7.15 us
    pallas_call x1, Pallas kernels, finish(): pl.pallas_call(finish_kernel, out_shape=jax.ShapeDtypeStruct((8, HEADS *...  2.97 us
    pallas_call x1, Pallas kernels, pack(): pl.pallas_call(pack_kernel, out_shape=jax.ShapeDtypeStruct((HEADS, 144, 1...  2.09 us
  transfers between devices with their start and end apart: 4, of which 2 were waited for; matrix products, arithmetic and copies ran while one was open for 1% of the time, Pallas kernels for 0%

profile of v3, /device:TPU:2, one launch (start us, length us, event | category | flops | bytes accessed | tf_op | source)
XLA Modules:
  0.0 103.6 jit_solution(13279695457495380023)
XLA Ops:
  0.0 2.1 %pack.1 = bf16[16,144,128]{2,1,0:T(8,128)(2,1)} custom-call(bf16[8,1024]{1,0:T(8,128)(2,1)} %q_ref.1, bf16[128,1024]{1,0:T(8,128)(2,1)} %k_ref.1, bf16[128,1024]{1,0:T(8,128)(2,1)} %v_ref.1), custom_call_target="tpu_custom_call" | custom-call | tf_op jit(solution)/shard_map/pack/pallas_call | solution.py:46
  2.1 20.7 %all_to_all.15.refs_0_ = bf16[16,144,128]{2,1,0:T(8,128)(2,1)S(1)} all-to-all(bf16[16,144,128]{2,1,0:T(8,128)(2,1)} %pack.1), channel_id=1, replica_groups=mesh['y'=4,'zh'=2,'core'=2,'xa'=2,'xb'=2,'zq'=4,'zo'=2] {'y','xa','zo'}, dimensions={0} | all-to-all | bytes 1179648 | tf_op jit(solution)/shard_map/all_to_all | solution.py:153
  22.7 3.3 %collective-permute-start = (bf16[16,144,128]{2,1,0:T(8,128)(2,1)S(1)}, bf16[16,144,128]{2,1,0:T(8,128)(2,1)S(1)}, u32[]{:S(2)}, u32[]{:S(2)}) collective-permute-start(bf16[16,144,128]{2,1,0:T(8,128)(2,1)S(1)} %all_to_all.15.refs_0_), channel_id=1, source_target_pairs={{0,8},{8,0},{1,9},{9,1},{2,10},{10,2},{3,11},{11,3},{4,12},{12,4},... | collective-permute-start | bytes 1769480 | tf_op jit(solution)/shard_map/ppermute | solution.py:157
  26.1 0.7 broadcast_in_dim.8
  26.8 14.2 %all-to-all-start.1 = ((bf16[8,64,128]{2,1,0:T(8,128)(2,1)}), bf16[8,64,128]{2,1,0:T(8,128)(2,1)S(1)}, u32[]{:S(2)}, u32[]{:S(2)}) async-start(bf16[8,64,128]{2,1,0:T(8,128)(2,1)} %broadcast_in_dim.8), calls=%async_computation.1 | async-start | bytes 262144 | tf_op jit(solution)/shard_map/all_to_all | solution.py:153
  41.0 1.9 %collective-permute-start.1 = (bf16[16,144,128]{2,1,0:T(8,128)(2,1)S(1)}, bf16[16,144,128]{2,1,0:T(8,128)(2,1)S(1)}, u32[]{:S(2)}, u32[]{:S(2)}) collective-permute-start(bf16[16,144,128]{2,1,0:T(8,128)(2,1)S(1)} %all_to_all.15.refs_0_), channel_id=1, source_target_pairs={{0,32},{32,0},{1,33},{33,1},{2,34},{34,2},{3,35},{35,3},{4,36},{36... | collective-permute-start | bytes 1769480 | tf_op jit(solution)/shard_map/ppermute | solution.py:157
  42.9 12.2 %all-to-all-done.1.q_ref = bf16[8,64,128]{2,1,0:T(8,128)(2,1)S(1)} async-done(((bf16[8,64,128]{2,1,0:T(8,128)(2,1)}), bf16[8,64,128]{2,1,0:T(8,128)(2,1)S(1)}, u32[]{:S(2)}, u32[]{:S(2)}) %all-to-all-start.1) | async-done | bytes 131104 | tf_op jit(solution)/shard_map/all_to_all | solution.py:153
  55.1 0.0 collective-permute-done.refs_2_
  55.1 1.9 %collective-permute-start.2 = (bf16[16,144,128]{2,1,0:T(8,128)(2,1)S(1)}, bf16[16,144,128]{2,1,0:T(8,128)(2,1)S(1)}, u32[]{:S(2)}, u32[]{:S(2)}) collective-permute-start(bf16[16,144,128]{2,1,0:T(8,128)(2,1)S(1)} %collective-permute-done.refs_2_), channel_id=1, source_target_pairs={{0,32},{32,0},{1,33},{33,1},{2,34},{34,2},{3,35},{35,3},{4,36},{36... | collective-permute-start | bytes 1769480 | tf_op jit(solution)/shard_map/ppermute | solution.py:157
  57.0 0.0 collective-permute-done.1.refs_1_
  57.0 2.0 %collective-permute-done.2.refs_3_ = bf16[16,144,128]{2,1,0:T(8,128)(2,1)S(1)} collective-permute-done((bf16[16,144,128]{2,1,0:T(8,128)(2,1)S(1)}, bf16[16,144,128]{2,1,0:T(8,128)(2,1)S(1)}, u32[]{:S(2)}, u32[]{:S(2)}) %collective-permute-start.2) | collective-permute-done | bytes 589856 | tf_op jit(solution)/shard_map/ppermute | solution.py:157
  58.9 9.4 %attend.1 = bf16[1024,128]{1,0:T(8,128)(2,1)S(1)} custom-call(bf16[8,64,128]{2,1,0:T(8,128)(2,1)S(1)} %all-to-all-done.1.q_ref, bf16[16,144,128]{2,1,0:T(8,128)(2,1)S(1)} %all_to_all.15.refs_0_, bf16[16,144,128]{2,1,0:T(8,128)(2,1)S(1)} %collective-permute-done.1.refs_1_, bf16[16,144,128]{2,1,0:T(8,128)(2,1)S(1)} %collective-permute-done.refs_2_, ...), custom_call_target="tpu_custom_call" | custom-call | flops 4294967296 | bytes 4194304 | tf_op jit(solution)/shard_map/attend/pallas_call | solution.py:103
  68.3 32.3 %all_to_all.16 = bf16[128,8,128]{2,1,0:T(8,128)(2,1)} all-to-all(bf16[128,8,128]{2,1,0:T(8,128)(2,1)S(1)} %bitcast.3), channel_id=1, replica_groups=mesh['y'=4,'zh'=2,'core'=2,'xa'=2,'xb'=2,'zq'=4,'zo'=2] {'zh','zq','y','..., dimensions={0} | all-to-all | bytes 524288 | tf_op jit(solution)/shard_map/all_to_all | solution.py:153
  100.6 3.0 %finish.1 = bf16[8,1024]{1,0:T(8,128)(2,1)} custom-call(bf16[1024,128]{1,0:T(8,128)(2,1)} %bitcast.4, bf16[1024,1024]{1,0:T(8,128)(2,1)} %w_ref.1), custom_call_target="tpu_custom_call" | custom-call | tf_op jit(solution)/shard_map/finish/pallas_call | solution.py:143
  (1 shorter events, 0.0 us)
Async XLA Ops:
  22.7 32.3 %collective-permute-start = (bf16[16,144,128]{2,1,0:T(8,128)(2,1)S(1)}, bf16[16,144,128]{2,1,0:T(8,128)(2,1)S(1)}, u32[]{:S(2)}, u32[]{:S(2)}) collective-permute-start(bf16[16,144,128]{2,1,0:T(8,128)(2,1)S(1)} %all_to_all.15.refs_0_), channel_id=1, source_target_pairs={{0,8},{8,0},{1,9},{9,1},{2,10},{10,2},{3,11},{11,3},{4,12},{12,4},... | collective-permute-start | bytes 1769480 | tf_op jit(solution)/shard_map/ppermute | solution.py:157
  26.8 28.3 %all-to-all-start.1 = ((bf16[8,64,128]{2,1,0:T(8,128)(2,1)}), bf16[8,64,128]{2,1,0:T(8,128)(2,1)S(1)}, u32[]{:S(2)}, u32[]{:S(2)}) async-start(bf16[8,64,128]{2,1,0:T(8,128)(2,1)} %broadcast_in_dim.8), calls=%async_computation.1 | async-start | bytes 262144 | tf_op jit(solution)/shard_map/all_to_all | solution.py:153
  41.0 16.0 %collective-permute-start.1 = (bf16[16,144,128]{2,1,0:T(8,128)(2,1)S(1)}, bf16[16,144,128]{2,1,0:T(8,128)(2,1)S(1)}, u32[]{:S(2)}, u32[]{:S(2)}) collective-permute-start(bf16[16,144,128]{2,1,0:T(8,128)(2,1)S(1)} %all_to_all.15.refs_0_), channel_id=1, source_target_pairs={{0,32},{32,0},{1,33},{33,1},{2,34},{34,2},{3,35},{35,3},{4,36},{36... | collective-permute-start | bytes 1769480 | tf_op jit(solution)/shard_map/ppermute | solution.py:157
  55.1 3.9 %collective-permute-start.2 = (bf16[16,144,128]{2,1,0:T(8,128)(2,1)S(1)}, bf16[16,144,128]{2,1,0:T(8,128)(2,1)S(1)}, u32[]{:S(2)}, u32[]{:S(2)}) collective-permute-start(bf16[16,144,128]{2,1,0:T(8,128)(2,1)S(1)} %collective-permute-done.refs_2_), channel_id=1, source_target_pairs={{0,32},{32,0},{1,33},{33,1},{2,34},{34,2},{3,35},{35,3},{4,36},{36... | collective-permute-start | bytes 1769480 | tf_op jit(solution)/shard_map/ppermute | solution.py:157

commit v4 on v3

v4 whole, which is shorter than its diff:
```python
import functools

import jax
import jax.numpy as jnp
from jax import lax
from jax.experimental import pallas as pl
from jax.experimental.pallas import tpu as pltpu
from jax.sharding import Mesh, PartitionSpec as P

HD = 64
HEADS = 16
NEAR = 4
FAR = 4
ALL = ("y", "far_a", "core", "x", "far_b", "near")
PLACE = ("x", "y")
DEPTH = ("near", "far_a", "far_b")
F32 = jnp.float32
BF16 = jnp.bfloat16
VMEM = pl.BlockSpec(memory_space=pltpu.VMEM)


def iota(shape, dim):
    return lax.broadcasted_iota(jnp.int32, shape, dim)


def pack_kernel(q_ref, k_ref, v_ref, out_ref):
    low = iota((128, 128), 1) < HD
    low4 = iota((4, 128), 1) < HD
    rest = jnp.zeros((12, 128), F32)
    for pair in range(HEADS // 2):
        span = slice(pair * 128, (pair + 1) * 128)
        k = k_ref[:, span]
        v = v_ref[:, span]
        k_turned = pltpu.roll(k.astype(F32), HD, 1).astype(BF16)
        v_turned = pltpu.roll(v.astype(F32), HD, 1).astype(BF16)
        out_ref[2 * pair, 0:128, :] = jnp.where(low, k, v_turned)
        out_ref[2 * pair + 1, 0:128, :] = jnp.where(low, k_turned, v)
        q = q_ref[:, span].astype(F32)
        q_turned = pltpu.roll(q, HD, 1)
        even = jnp.where(low4, q[0:4], q_turned[4:8])
        odd = jnp.where(low4, q_turned[0:4], q[4:8])
        out_ref[2 * pair, 128:144, :] = jnp.concatenate([even, rest], 0).astype(BF16)
        out_ref[2 * pair + 1, 128:144, :] = jnp.concatenate([odd, rest], 0).astype(BF16)


def pack(q, k, v):
    return pl.pallas_call(
        pack_kernel,
        out_shape=jax.ShapeDtypeStruct((HEADS, 144, 128), BF16),
        in_specs=[VMEM, VMEM, VMEM],
        out_specs=VMEM,
        name="pack",
    )(q, k, v)


def packed_stats(level):
    level = level.T[0:8]
    first = level.astype(BF16).astype(F32)
    second = (level - first).astype(BF16).astype(F32)
    third = level - first - second
    row = iota((8, 128), 0)
    terms = jnp.where(row == 0, first, jnp.where(row == 1, second, third))
    return jnp.concatenate([terms, terms], 0).astype(BF16)


def attend_kernel(blocks, group, q_ref, kva_ref, kvb_ref, out_ref):
    low16 = iota((16, 128), 1) < HD
    low64 = iota((64, 128), 1) < HD
    rows = group * 128
    low = iota((rows, 128), 1) < HD

    def body(step, carry):
        parts = []
        for j in range(blocks):
            x = step * (blocks // NEAR) + j // NEAR
            near = j % NEAR
            first, second = [], []
            for far in range(FAR):
                span = pl.ds(pl.multiple_of(x * 16, 16), 16)
                pair = q_ref[near * FAR + far, span, :].astype(F32) * HD**-0.5
                first.append(jnp.where(low16, pair, 0.0))
                second.append(jnp.where(low16, pltpu.roll(pair, HD, 1), 0.0))
            parts += first + second
        q = jnp.concatenate(parts, 0).astype(BF16)
        top, total = None, None
        for kv_ref in (kva_ref, kvb_ref):
            for c in range(HEADS // group):
                kv = kv_ref[c * group : (c + 1) * group, 0:128, :].reshape(rows, 128)
                score = lax.dot_general(
                    q, kv, (((1,), (1,)), ((), ())), preferred_element_type=F32
                )
                here = jnp.max(score, 1, keepdims=True)
                new = here if top is None else jnp.maximum(top, here)
                weights = jnp.exp(score - new).astype(BF16)
                marked = jnp.where(low, jnp.ones((), BF16), kv)
                part = jnp.dot(weights, marked, preferred_element_type=F32)
                total = part if top is None else total * jnp.exp(top - new) + part
                top = new
        for j in range(blocks):
            span = slice(j * 128, (j + 1) * 128)
            whole = total[span]
            mixed = whole / jnp.where(iota((128, 128), 1) < HD, 1.0, pltpu.roll(whole, HD, 1))
            packed = jnp.where(low64, pltpu.roll(mixed[:64], HD, 1), mixed[64:])
            block = step * blocks + j
            out_ref[block, 0:64, :] = packed.astype(BF16)
            out_ref[block, 64:80, :] = packed_stats(jnp.log(whole) + top[span])
        return carry

    lax.fori_loop(0, 16 // blocks, body, 0)


def attend(q, kva, kvb, blocks=8, group=2):
    rows = 2 * HEADS * 128
    return pl.pallas_call(
        functools.partial(attend_kernel, blocks, group),
        out_shape=jax.ShapeDtypeStruct((16, 80, 128), BF16),
        in_specs=[VMEM] * 3,
        out_specs=VMEM,
        compiler_params=pltpu.CompilerParams(vmem_limit_bytes=48 * 2**20),
        cost_estimate=pl.CostEstimate(
            flops=4 * 2048 * rows * 128, bytes_accessed=2**21, transcendentals=2048 * rows
        ),
        name="attend",
    )(q, kva, kvb)


def gather_near_kernel(part_ref, out_ref):
    rows, sums = [], []
    for x in range(4):
        levels = []
        for near in range(NEAR):
            terms = part_ref[x * NEAR + near, 64:80, :].astype(F32)
            levels.append(terms[0:1] + terms[1:2] + terms[2:3])
        top = functools.reduce(jnp.maximum, levels)
        weights = [jnp.exp(level - top) for level in levels]
        whole = sum(weights)
        rows += [weight / whole for weight in weights]
        sums.append(top + jnp.log(whole))
    table = jnp.concatenate(rows + sums + [jnp.zeros((108, 128), F32)], 0).T
    low64 = iota((64, 128), 1) < HD
    sub = iota((64, 128), 0) % 8 < 4
    first_half = iota((64, 128), 1) % HD < HD // 2

    def column(n):
        c = table[:, n : n + 1]
        return jnp.where(low64, c[:64], c[64:])

    heads = []
    for x in range(4):
        mixed = sum(
            column(x * NEAR + near) * part_ref[x * NEAR + near, 0:64, :].astype(F32)
            for near in range(NEAR)
        )
        level = column(16 + x)
        first = level.astype(BF16).astype(F32)
        level = jnp.where(first_half, first, level - first)
        mixed_turned = pltpu.roll(mixed.reshape(8, 8, 128), 4, 1).reshape(64, 128)
        level_turned = pltpu.roll(level.reshape(8, 8, 128), 4, 1).reshape(64, 128)
        even = jnp.where(sub, mixed, level_turned)
        odd = jnp.where(sub, mixed_turned, level)
        heads.append((even, odd))
    for owner in range(16):
        span = slice(owner // 2 * 8, owner // 2 * 8 + 8)
        tiles = [heads[x][owner % 2][span] for x in range(4)]
        out_ref[owner] = jnp.concatenate(tiles, 0).astype(BF16)


def gather_near(parts):
    return pl.pallas_call(
        gather_near_kernel,
        out_shape=jax.ShapeDtypeStruct((16, 32, 128), BF16),
        in_specs=[VMEM],
        out_specs=VMEM,
        name="gather_near",
    )(parts)


def finish_kernel(part_ref, w_hbm, out_ref, w_ref, sem):
    copy = pltpu.make_async_copy(w_hbm, w_ref, sem)
    copy.start()
    near = iota((HEADS * 8, 128), 1) % HD < HD // 2
    blocks, levels = [], []
    for far in range(FAR):
        block = part_ref[far * 4 : (far + 1) * 4].reshape(HEADS * 8, 128).astype(F32)
        other = jnp.where(near, pltpu.roll(block, 96, 1), pltpu.roll(block, 32, 1))
        level = (block + other).reshape(HEADS, 8, 128)
        blocks.append(block.reshape(HEADS, 8, 128))
        levels.append(pltpu.roll(level, 4, 1))
    top = functools.reduce(jnp.maximum, levels)
    weights = [jnp.exp(level - top) for level in levels]
    mixed = sum(w * b for w, b in zip(weights, blocks)) / sum(weights)
    turned = pltpu.roll(mixed, HD, 2)
    low = iota((8, 128), 1) < HD
    upper = iota((8, 128), 0) < 4
    tiles = []
    for pair in range(HEADS // 2):
        a, b = (h % 4 * 4 + h // 4 for h in (2 * pair, 2 * pair + 1))
        head = jnp.where(low, mixed[a], turned[b])
        tail = jnp.where(low, turned[a], mixed[b])
        tiles.append(jnp.where(upper, head, pltpu.roll(tail, 4, 0)))
    rows = jnp.concatenate(tiles, 1).astype(BF16)
    copy.wait()
    out_ref[...] = jnp.dot(rows, w_ref[...], preferred_element_type=F32).astype(BF16)


def finish(parts, w_out):
    return pl.pallas_call(
        finish_kernel,
        out_shape=jax.ShapeDtypeStruct((8, HEADS * HD), BF16),
        in_specs=[VMEM, pl.BlockSpec(memory_space=pl.ANY)],
        out_specs=VMEM,
        scratch_shapes=[pltpu.VMEM(w_out.shape, BF16), pltpu.SemaphoreType.DMA],
        name="finish",
    )(parts, w_out)


def exchange(blocks, axes):
    return lax.all_to_all(blocks, axes, split_axis=0, concat_axis=0, tiled=True)


def local(queries, keys, values, w_out):
    held = exchange(pack(queries, keys, values), PLACE)
    held_core = lax.ppermute(held, "core", [(0, 1), (1, 0)])
    q_place = held[:, 128:132, :].reshape(1, 64, 128)
    q_all = exchange(jnp.broadcast_to(q_place, (16, 64, 128)), DEPTH)
    parts = exchange(attend(q_all, held, held_core), ("x", "near"))
    parts = exchange(gather_near(parts), ("far_a", "far_b", "y"))
    return finish(parts, w_out)


def solution(mesh):
    split = Mesh(mesh.devices.reshape(4, 2, 2, 4, 2, 4), ALL)
    return jax.shard_map(
        local,
        mesh=split,
        in_specs=(P(ALL, None), P(ALL, None), P(ALL, None), P()),
        out_specs=P(ALL, None),
        check_vma=False,
    )
```

time: 104 us -> 109 us (1.048)
  the two profiles are of different devices: /device:TPU:2 before, /device:TPU:32 now
where the time goes in v4:
time: 109 us
  blocking collectives  55.6 us (51%)
  Pallas kernels  18.9 us (17%)
  starting transfers between devices  17.1 us (16%)
  waiting for transfers between devices  16.3 us (15%)
    all_to_all x3, blocking collectives, exchange(): return lax.all_to_all(blocks, axes, split_axis=0, concat_axis=0, tiled=True)  55.6 us
    all_to_all x1, starting transfers between devices, exchange(): return lax.all_to_all(blocks, axes, split_axis=0, concat_axis=0, tiled=True)  15.2 us
    all_to_all x1, waiting for transfers between devices, exchange(): return lax.all_to_all(blocks, axes, split_axis=0, concat_axis=0, tiled=True)  14.3 us
    pallas_call x1, Pallas kernels, attend(): pl.pallas_call(functools.partial(attend_kernel, blocks, group), out_shape...  11.1 us
    pallas_call x1, Pallas kernels, finish(): pl.pallas_call(finish_kernel, out_shape=jax.ShapeDtypeStruct((8, HEADS *...  3.5 us
    pallas_call x1, Pallas kernels, gather_near(): pl.pallas_call(gather_near_kernel, out_shape=jax.ShapeDtypeStruct((16, 32...  2.23 us
  transfers between devices with their start and end apart: 2, of which 2 were waited for; matrix products, arithmetic and copies ran while one was open for 0% of the time, Pallas kernels for 0%

profile of v4, /device:TPU:32, one launch (start us, length us, event | category | flops | bytes accessed | tf_op | source)
XLA Modules:
  0.0 108.8 jit_solution(15897929151582803497)
XLA Ops:
  0.0 2.1 %pack.1 = bf16[16,144,128]{2,1,0:T(8,128)(2,1)} custom-call(bf16[8,1024]{1,0:T(8,128)(2,1)} %q_ref.1, bf16[128,1024]{1,0:T(8,128)(2,1)} %k_ref.1, bf16[128,1024]{1,0:T(8,128)(2,1)} %v_ref.1), custom_call_target="tpu_custom_call" | custom-call | tf_op jit(solution)/shard_map/pack/pallas_call | solution.py:47
  2.1 19.3 %all_to_all.20.kva_ref = bf16[16,144,128]{2,1,0:T(8,128)(2,1)S(1)} all-to-all(bf16[16,144,128]{2,1,0:T(8,128)(2,1)} %pack.1), channel_id=1, replica_groups=mesh['y'=4,'far_a'=2,'core'=2,'x'=4,'far_b'=2,'near'=4] {'x','y'}, dimensions={0} | all-to-all | bytes 1179648 | tf_op jit(solution)/shard_map/all_to_all | solution.py:218
  21.3 0.7 broadcast_in_dim.8
  22.1 15.2 %all-to-all-start.1 = ((bf16[16,64,128]{2,1,0:T(8,128)(2,1)}), bf16[16,64,128]{2,1,0:T(8,128)(2,1)S(1)}, u32[]{:S(2)}, u32[]{:S(2)}) async-start(bf16[16,64,128]{2,1,0:T(8,128)(2,1)} %broadcast_in_dim.8), calls=%async_computation.1 | async-start | bytes 524288 | tf_op jit(solution)/shard_map/all_to_all | solution.py:218
  37.3 1.9 %collective-permute-start = (bf16[16,144,128]{2,1,0:T(8,128)(2,1)S(1)}, bf16[16,144,128]{2,1,0:T(8,128)(2,1)S(1)}, u32[]{:S(2)}, u32[]{:S(2)}) collective-permute-start(bf16[16,144,128]{2,1,0:T(8,128)(2,1)S(1)} %all_to_all.20.kva_ref), channel_id=1, source_target_pairs={{0,32},{32,0},{1,33},{33,1},{2,34},{34,2},{3,35},{35,3},{4,36},{36... | collective-permute-start | bytes 1769480 | tf_op jit(solution)/shard_map/ppermute | solution.py:223
  39.2 2.0 %collective-permute-done.kvb_ref = bf16[16,144,128]{2,1,0:T(8,128)(2,1)S(1)} collective-permute-done((bf16[16,144,128]{2,1,0:T(8,128)(2,1)S(1)}, bf16[16,144,128]{2,1,0:T(8,128)(2,1)S(1)}, u32[]{:S(2)}, u32[]{:S(2)}) %collective-permute-start) | collective-permute-done | bytes 589856 | tf_op jit(solution)/shard_map/ppermute | solution.py:223
  41.2 14.3 %all-to-all-done.1.q_ref = bf16[16,64,128]{2,1,0:T(8,128)(2,1)S(1)} async-done(((bf16[16,64,128]{2,1,0:T(8,128)(2,1)}), bf16[16,64,128]{2,1,0:T(8,128)(2,1)S(1)}, u32[]{:S(2)}, u32[]{:S(2)}) %all-to-all-start.1) | async-done | bytes 262176 | tf_op jit(solution)/shard_map/all_to_all | solution.py:218
  55.5 11.1 %attend.1 = bf16[16,80,128]{2,1,0:T(8,128)(2,1)S(1)} custom-call(bf16[16,64,128]{2,1,0:T(8,128)(2,1)S(1)} %all-to-all-done.1.q_ref, bf16[16,144,128]{2,1,0:T(8,128)(2,1)S(1)} %all_to_all.20.kva_ref, bf16[16,144,128]{2,1,0:T(8,128)(2,1)S(1)} %collective-permute-done.kvb_ref), custom_call_target="tpu_custom_call" | custom-call | flops 4294967296 | bytes 2097152 | tf_op jit(solution)/shard_map/attend/pallas_call | solution.py:114
  66.7 14.0 %all_to_all.21.part_ref = bf16[16,80,128]{2,1,0:T(8,128)(2,1)} all-to-all(bf16[16,80,128]{2,1,0:T(8,128)(2,1)S(1)} %attend.1), channel_id=1, replica_groups=mesh['y'=4,'far_a'=2,'core'=2,'x'=4,'far_b'=2,'near'=4] {'x','near'}, dimensions={0} | all-to-all | bytes 655360 | tf_op jit(solution)/shard_map/all_to_all | solution.py:218
  80.7 2.2 %gather_near.1 = bf16[16,32,128]{2,1,0:T(8,128)(2,1)} custom-call(bf16[16,80,128]{2,1,0:T(8,128)(2,1)} %all_to_all.21.part_ref), custom_call_target="tpu_custom_call" | custom-call | tf_op jit(solution)/shard_map/gather_near/pallas_call | solution.py:169
  82.9 22.4 %all_to_all.22.part_ref = bf16[16,32,128]{2,1,0:T(8,128)(2,1)} all-to-all(bf16[16,32,128]{2,1,0:T(8,128)(2,1)} %gather_near.1), channel_id=1, replica_groups=mesh['y'=4,'far_a'=2,'core'=2,'x'=4,'far_b'=2,'near'=4] {'far_a','far_b'..., dimensions={0} | all-to-all | bytes 262144 | tf_op jit(solution)/shard_map/all_to_all | solution.py:218
  105.3 3.5 %finish.1 = bf16[8,1024]{1,0:T(8,128)(2,1)} custom-call(bf16[16,32,128]{2,1,0:T(8,128)(2,1)} %all_to_all.22.part_ref, bf16[1024,1024]{1,0:T(8,128)(2,1)} %w_hbm.1), custom_call_target="tpu_custom_call" | custom-call | tf_op jit(solution)/shard_map/finish/pallas_call | solution.py:207
  (1 shorter events, 0.0 us)
Async XLA Ops:
  22.1 33.4 %all-to-all-start.1 = ((bf16[16,64,128]{2,1,0:T(8,128)(2,1)}), bf16[16,64,128]{2,1,0:T(8,128)(2,1)S(1)}, u32[]{:S(2)}, u32[]{:S(2)}) async-start(bf16[16,64,128]{2,1,0:T(8,128)(2,1)} %broadcast_in_dim.8), calls=%async_computation.1 | async-start | bytes 524288 | tf_op jit(solution)/shard_map/all_to_all | solution.py:218
  37.3 3.9 %collective-permute-start = (bf16[16,144,128]{2,1,0:T(8,128)(2,1)S(1)}, bf16[16,144,128]{2,1,0:T(8,128)(2,1)S(1)}, u32[]{:S(2)}, u32[]{:S(2)}) collective-permute-start(bf16[16,144,128]{2,1,0:T(8,128)(2,1)S(1)} %all_to_all.20.kva_ref), channel_id=1, source_target_pairs={{0,32},{32,0},{1,33},{33,1},{2,34},{34,2},{3,35},{35,3},{4,36},{36... | collective-permute-start | bytes 1769480 | tf_op jit(solution)/shard_map/ppermute | solution.py:223

commit v5 on v3

--- a/solution.py
+++ b/solution.py
@@ -11,6 +11,7 @@
 HEADS = 16
 STEPS = 8
 ALL = ("y", "zh", "core", "xa", "xb", "zq", "zo")
+SPREAD = ("y", "xa", "zo", "xb")
 PLACE = ("y", "xa", "zo")
 DEPTH = ("zh", "zq")
 F32 = jnp.float32
@@ -32,20 +33,25 @@
         v = v_ref[:, span]
         k_turned = pltpu.roll(k.astype(F32), HD, 1).astype(BF16)
         v_turned = pltpu.roll(v.astype(F32), HD, 1).astype(BF16)
-        out_ref[2 * pair, 0:128, :] = jnp.where(low, k, v_turned)
-        out_ref[2 * pair + 1, 0:128, :] = jnp.where(low, k_turned, v)
+        even_kv = jnp.where(low, k, v_turned)
+        odd_kv = jnp.where(low, k_turned, v)
         q = q_ref[:, span].astype(F32)
         q_turned = pltpu.roll(q, HD, 1)
         even = jnp.where(low4, q[0:4], q_turned[4:8])
         odd = jnp.where(low4, q_turned[0:4], q[4:8])
-        out_ref[2 * pair, 128:144, :] = jnp.concatenate([even, rest], 0).astype(BF16)
-        out_ref[2 * pair + 1, 128:144, :] = jnp.concatenate([odd, rest], 0).astype(BF16)
+        even = jnp.concatenate([even, rest], 0).astype(BF16)
+        odd = jnp.concatenate([odd, rest], 0).astype(BF16)
+        for half in range(2):
+            out_ref[4 * pair + half, 0:128, :] = even_kv
+            out_ref[4 * pair + half, 128:144, :] = even
+            out_ref[4 * pair + 2 + half, 0:128, :] = odd_kv
+            out_ref[4 * pair + 2 + half, 128:144, :] = odd
 
 
 def pack(q, k, v):
     return pl.pallas_call(
         pack_kernel,
-        out_shape=jax.ShapeDtypeStruct((HEADS, 144, 128), BF16),
+        out_shape=jax.ShapeDtypeStruct((2 * HEADS, 144, 128), BF16),
         in_specs=[VMEM, VMEM, VMEM],
         out_specs=VMEM,
         name="pack",
@@ -53,7 +59,7 @@
 
 
 def attend_kernel(group, q_ref, *refs):
-    kv_refs, out_ref = refs[:4], refs[4]
+    kv_refs, out_ref = refs[:-1], refs[-1]
     low64 = iota((64, 128), 1) < HD
     rows = group * 128
     low = iota((rows, 128), 1) < HD
@@ -65,7 +71,7 @@
     q = jnp.concatenate(parts, 0).astype(BF16)
     top, total = None, None
     for kv_ref in kv_refs:
-        for c in range(HEADS // group):
+        for c in range(kv_ref.shape[0] // group):
             kv = kv_ref[c * group : (c + 1) * group, 0:128, :].reshape(rows, 128)
             score = lax.dot_general(
                 q, kv, (((1,), (1,)), ((), ())), preferred_element_type=F32
@@ -99,13 +105,13 @@
 
 
 def attend(q, kvs, group=2):
-    rows = len(kvs) * HEADS * 128
+    rows = 128 * sum(kv.shape[0] for kv in kvs)
     return pl.pallas_call(
         functools.partial(attend_kernel, group),
         out_shape=jax.ShapeDtypeStruct((STEPS * 128, 128), BF16),
         in_specs=[VMEM] * (1 + len(kvs)),
         out_specs=VMEM,
-        compiler_params=pltpu.CompilerParams(vmem_limit_bytes=48 * 2**20),
+        compiler_params=pltpu.CompilerParams(vmem_limit_bytes=32 * 2**20),
         cost_estimate=pl.CostEstimate(
             flops=4 * STEPS * 128 * rows * 128,
             bytes_accessed=2**22,
@@ -115,7 +121,7 @@
     )(q, *kvs)
 
 
-def finish_kernel(part_ref, w_ref, out_ref):
+def finish_kernel(part_ref, out_ref):
     near = iota((HEADS * 8, 128), 1) % HD < HD // 2
     blocks, levels = [], []
     for step in range(STEPS):
@@ -135,39 +141,34 @@
         head = jnp.where(low, mixed[2 * pair], turned[2 * pair + 1])
         tail = jnp.where(low, turned[2 * pair], mixed[2 * pair + 1])
         tiles.append(jnp.where(upper, head, pltpu.roll(tail, 4, 0)))
-    rows = jnp.concatenate(tiles, 1).astype(BF16)
-    out_ref[...] = jnp.dot(rows, w_ref[...], preferred_element_type=F32).astype(BF16)
+    out_ref[...] = jnp.concatenate(tiles, 1).astype(BF16)
 
 
-def finish(parts, w_out):
+def finish(parts):
     return pl.pallas_call(
         finish_kernel,
         out_shape=jax.ShapeDtypeStruct((8, HEADS * HD), BF16),
-        in_specs=[VMEM, VMEM],
+        in_specs=[VMEM],
         out_specs=VMEM,
         name="finish",
-    )(parts, w_out)
+    )(parts)
 
 
 def exchange(blocks, axes):
     return lax.all_to_all(blocks, axes, split_axis=0, concat_axis=0, tiled=True)
 
 
-def swap(block, axis):
-    return lax.ppermute(block, axis, [(0, 1), (1, 0)])
-
-
 def local(queries, keys, values, w_out):
-    held = exchange(pack(queries, keys, values), PLACE)
-    held_x = swap(held, "xb")
-    held_core = swap(held, "core")
-    q_place = held[:, 128:132, :].reshape(1, 64, 128)
-    q_all = exchange(jnp.broadcast_to(q_place, (STEPS, 64, 128)), DEPTH)
-    held_x, q_all = lax.optimization_barrier((held_x, q_all))
-    held_both = swap(held_x, "core")
-    parts = attend(q_all, (held, held_core, held_x, held_both))
+    held = exchange(pack(queries, keys, values), SPREAD)
+    held_core = lax.ppermute(held, "core", [(0, 1), (1, 0)])
+    own = lax.dynamic_slice(
+        held.reshape(HEADS, 2, 144, 128), (0, lax.axis_index("xb"), 128, 0), (HEADS, 1, 4, 128)
+    )
+    q_all = exchange(jnp.broadcast_to(own.reshape(1, 64, 128), (STEPS, 64, 128)), DEPTH)
+    parts = attend(q_all, (held, held_core))
     parts = exchange(parts.reshape(STEPS * HEADS, 8, 128), DEPTH + PLACE)
-    return finish(parts.reshape(STEPS * HEADS * 8, 128), w_out)
+    attended = finish(parts.reshape(STEPS * HEADS * 8, 128))
+    return jnp.dot(attended, w_out, preferred_element_type=F32).astype(BF16)
 
 
 def solution(mesh):

time: 104 us -> 109 us (1.048)
  blocking collectives: 52.9 us -> 89.5 us
  starting transfers between devices: 21.3 us -> 1.91 us
  waiting for transfers between devices: 14.1 us -> 0.01 us
  matrix products: 0 us -> 1.71 us
    all_to_all x2 -> x3, blocking collectives: 52.9 us -> 89.5 us  [exchange(): return lax.all_to_all(blocks, axes, split_axis=0, concat_axis=0, tiled=True)]
    all_to_all x1 -> x0, starting transfers between devices: 14.2 us -> none  [exchange(): return lax.all_to_all(blocks, axes, split_axis=0, concat_axis=0, tiled=True)]
    all_to_all x1 -> x0, waiting for transfers between devices: 12.2 us -> none  [exchange(): return lax.all_to_all(blocks, axes, split_axis=0, concat_axis=0, tiled=True)]
    ppermute x3 -> x1, starting transfers between devices: 7.15 us -> 1.91 us  [local(): held_core = lax.ppermute(held, 'core', [(0, 1), (1, 0)])]
    ppermute x3 -> x1, waiting for transfers between devices: 1.96 us -> 0.01 us  [local(): held_core = lax.ppermute(held, 'core', [(0, 1), (1, 0)])]
    dot_general x0 -> x1, matrix products: none -> 1.71 us  [local(): return jnp.dot(attended, w_out, preferred_element_type=F32).astype(BF16)]
    pallas_call x1, Pallas kernels: 9.38 us -> 10.6 us  [attend(): pl.pallas_call(functools.partial(attend_kernel, group), out_shape=jax.Sha...]
  transfers between devices with their start and end apart: 4 -> 1, of which waited for: 2 -> 0; matrix products, arithmetic and copies ran while one was open for 1% -> 0% of each run, Pallas kernels for 0% -> 0%
where the time goes in v5:
time: 109 us; the launch traced here: 108 us
  blocking collectives  89.5 us (82%)
  Pallas kernels  15 us (14%)
  starting transfers between devices  1.91 us (2%)
  matrix products  1.71 us (2%)
    all_to_all x3, blocking collectives, exchange(): return lax.all_to_all(blocks, axes, split_axis=0, concat_axis=0, tiled=True)  89.5 us
    pallas_call x1, Pallas kernels, attend(): pl.pallas_call(functools.partial(attend_kernel, group), out_shape=jax.Sha...  10.6 us
    pallas_call x1, Pallas kernels, pack(): pl.pallas_call(pack_kernel, out_shape=jax.ShapeDtypeStruct((2 * HEADS, 14...  2.43 us
  transfers between devices with their start and end apart: 1, of which 0 were waited for; matrix products, arithmetic and copies ran while one was open for 0% of the time, Pallas kernels for 0%

profile of v5, /device:TPU:2, one launch (start us, length us, event | category | flops | bytes accessed | tf_op | source)
XLA Modules:
  0.0 108.2 jit_solution(16296067266318467665)
XLA Ops:
  0.0 0.0 copy-start
  0.0 2.4 %pack.1 = bf16[32,144,128]{2,1,0:T(8,128)(2,1)} custom-call(bf16[8,1024]{1,0:T(8,128)(2,1)} %q_ref.1, bf16[128,1024]{1,0:T(8,128)(2,1)} %k_ref.1, bf16[128,1024]{1,0:T(8,128)(2,1)} %v_ref.1), custom_call_target="tpu_custom_call" | custom-call | tf_op jit(solution)/shard_map/pack/pallas_call | solution.py:52
  2.4 27.0 %all_to_all.15.refs_0_ = bf16[32,144,128]{2,1,0:T(8,128)(2,1)S(1)} all-to-all(bf16[32,144,128]{2,1,0:T(8,128)(2,1)} %pack.1), channel_id=1, replica_groups=mesh['y'=4,'zh'=2,'core'=2,'xa'=2,'xb'=2,'zq'=4,'zo'=2] {'y','xa','zo','..., dimensions={0} | all-to-all | bytes 2359296 | tf_op jit(solution)/shard_map/all_to_all | solution.py:158
  29.5 1.9 %collective-permute-start = (bf16[32,144,128]{2,1,0:T(8,128)(2,1)S(1)}, bf16[32,144,128]{2,1,0:T(8,128)(2,1)}, u32[]{:S(2)}, u32[]{:S(2)}) collective-permute-start(bf16[32,144,128]{2,1,0:T(8,128)(2,1)S(1)} %all_to_all.15.refs_0_), channel_id=1, source_target_pairs={{0,32},{32,0},{1,33},{33,1},{2,34},{34,2},{3,35},{35,3},{4,36},{36... | collective-permute-start | bytes 3538952 | tf_op jit(solution)/shard_map/ppermute | solution.py:163
  31.4 30.1 %all_to_all.16.q_ref = bf16[8,64,128]{2,1,0:T(8,128)(2,1)S(1)} all-to-all(bf16[8,64,128]{2,1,0:T(8,128)(2,1)S(1)} %broadcast_in_dim.8), channel_id=1, replica_groups=mesh['y'=4,'zh'=2,'core'=2,'xa'=2,'xb'=2,'zq'=4,'zo'=2] {'zh','zq'}, dimensions={0} | all-to-all | bytes 262144 | tf_op jit(solution)/shard_map/all_to_all | solution.py:158
  61.5 0.0 collective-permute-done.refs_1_
  61.5 10.6 %attend.1 = bf16[1024,128]{1,0:T(8,128)(2,1)S(1)} custom-call(bf16[8,64,128]{2,1,0:T(8,128)(2,1)S(1)} %all_to_all.16.q_ref, bf16[32,144,128]{2,1,0:T(8,128)(2,1)S(1)} %all_to_all.15.refs_0_, bf16[32,144,128]{2,1,0:T(8,128)(2,1)} %collective-permute-done.refs_1_), custom_call_target="tpu_custom_call" | custom-call | flops 4294967296 | bytes 4194304 | tf_op jit(solution)/shard_map/attend/pallas_call | solution.py:109
  72.2 32.4 %all_to_all.17 = bf16[128,8,128]{2,1,0:T(8,128)(2,1)} all-to-all(bf16[128,8,128]{2,1,0:T(8,128)(2,1)S(1)} %bitcast.7), channel_id=1, replica_groups=mesh['y'=4,'zh'=2,'core'=2,'xa'=2,'xb'=2,'zq'=4,'zo'=2] {'zh','zq','y','..., dimensions={0} | all-to-all | bytes 524288 | tf_op jit(solution)/shard_map/all_to_all | solution.py:158
  104.6 2.0 %finish.1 = bf16[8,1024]{1,0:T(8,128)(2,1)} custom-call(bf16[1024,128]{1,0:T(8,128)(2,1)} %bitcast.8), custom_call_target="tpu_custom_call" | custom-call | tf_op jit(solution)/shard_map/finish/pallas_call | solution.py:148
  106.5 0.0 copy-done
  106.5 1.7 %convolution_convert_fusion = bf16[8,1024]{1,0:T(8,128)(2,1)} fusion(bf16[8,1024]{1,0:T(8,128)(2,1)} %finish.1, bf16[1024,1024]{1,0:T(8,128)(2,1)S(1)} %copy-done), kind=kOutput, calls=%fused_computation | convolution fusion | flops 16785408 | bytes 2129920 | tf_op jit(solution)/shard_map/dot_general | solution.py:171
  (2 shorter events, 0.0 us)
Async XLA Ops:
  0.0 106.5 %copy-start = (bf16[1024,1024]{1,0:T(8,128)(2,1)S(1)}, bf16[1024,1024]{1,0:T(8,128)(2,1)}, u32[]{:S(2)}) copy-start(bf16[1024,1024]{1,0:T(8,128)(2,1)} %param.7) | copy-start | bytes 6291460
  29.5 32.1 %collective-permute-start = (bf16[32,144,128]{2,1,0:T(8,128)(2,1)S(1)}, bf16[32,144,128]{2,1,0:T(8,128)(2,1)}, u32[]{:S(2)}, u32[]{:S(2)}) collective-permute-start(bf16[32,144,128]{2,1,0:T(8,128)(2,1)S(1)} %all_to_all.15.refs_0_), channel_id=1, source_target_pairs={{0,32},{32,0},{1,33},{33,1},{2,34},{34,2},{3,35},{35,3},{4,36},{36... | collective-permute-start | bytes 3538952 | tf_op jit(solution)/shard_map/ppermute | solution.py:163

commit v6 on v3

v6 whole, which is shorter than its diff:
```python
import functools

import jax
import jax.numpy as jnp
from jax import lax
from jax.experimental import pallas as pl
from jax.experimental.pallas import tpu as pltpu
from jax.sharding import Mesh, PartitionSpec as P

HD = 64
HEADS = 16
STEPS = 8
ALL = ("y", "zh", "core", "xa", "xb", "zq", "zo")
PLACE = ("y", "xa", "zo")
DEPTH = ("zh", "zq")
F32 = jnp.float32
BF16 = jnp.bfloat16
VMEM = pl.BlockSpec(memory_space=pltpu.VMEM)


def iota(shape, dim):
    return lax.broadcasted_iota(jnp.int32, shape, dim)


def pack_kernel(q_ref, k_ref, v_ref, out_ref):
    low = iota((128, 128), 1) < HD
    low4 = iota((4, 128), 1) < HD
    rest = jnp.zeros((12, 128), F32)
    for pair in range(HEADS // 2):
        span = slice(pair * 128, (pair + 1) * 128)
        k = k_ref[:, span]
        v = v_ref[:, span]
        k_turned = pltpu.roll(k.astype(F32), HD, 1).astype(BF16)
        v_turned = pltpu.roll(v.astype(F32), HD, 1).astype(BF16)
        out_ref[2 * pair, 0:128, :] = jnp.where(low, k, v_turned)
        out_ref[2 * pair + 1, 0:128, :] = jnp.where(low, k_turned, v)
        q = q_ref[:, span].astype(F32)
        q_turned = pltpu.roll(q, HD, 1)
        even = jnp.where(low4, q[0:4], q_turned[4:8])
        odd = jnp.where(low4, q_turned[0:4], q[4:8])
        out_ref[2 * pair, 128:144, :] = jnp.concatenate([even, rest], 0).astype(BF16)
        out_ref[2 * pair + 1, 128:144, :] = jnp.concatenate([odd, rest], 0).astype(BF16)


def pack(q, k, v):
    return pl.pallas_call(
        pack_kernel,
        out_shape=jax.ShapeDtypeStruct((HEADS, 144, 128), BF16),
        in_specs=[VMEM, VMEM, VMEM],
        out_specs=VMEM,
        name="pack",
    )(q, k, v)


def packed_stats(level):
    level = level.T[0:8]
    first = level.astype(BF16).astype(F32)
    second = (level - first).astype(BF16).astype(F32)
    third = level - first - second
    row = iota((8, 128), 0)
    terms = jnp.where(row == 0, first, jnp.where(row == 1, second, third))
    return jnp.concatenate([terms, terms], 0).astype(BF16)


def take_queries(q_ref):
    low64 = iota((64, 128), 1) < HD
    parts = []
    for step in range(STEPS):
        pair = q_ref[step].astype(F32) * HD**-0.5
        parts.append(jnp.where(low64, pair, 0.0))
        parts.append(jnp.where(low64, pltpu.roll(pair, HD, 1), 0.0))
    return jnp.concatenate(parts, 0).astype(BF16)


def absorb(group, q, kv_refs, top, total):
    rows = group * 128
    low = iota((rows, 128), 1) < HD
    for kv_ref in kv_refs:
        for c in range(HEADS // group):
            kv = kv_ref[c * group : (c + 1) * group, 0:128, :].reshape(rows, 128)
            score = lax.dot_general(q, kv, (((1,), (1,)), ((), ())), preferred_element_type=F32)
            here = jnp.max(score, 1, keepdims=True)
            new = here if top is None else jnp.maximum(top, here)
            weights = jnp.exp(score - new).astype(BF16)
            marked = jnp.where(low, jnp.ones((), BF16), kv)
            part = jnp.dot(weights, marked, preferred_element_type=F32)
            total = part if top is None else total * jnp.exp(top - new) + part
            top = new
    return top, total


def attend_first_kernel(group, q_ref, kva_ref, kvb_ref, top_ref, total_ref):
    top, total = absorb(group, take_queries(q_ref), (kva_ref, kvb_ref), None, None)
    top_ref[...] = jnp.broadcast_to(top, top_ref.shape)
    total_ref[...] = total


def attend_second_kernel(group, q_ref, kva_ref, kvb_ref, top_ref, total_ref, out_ref):
    top, total = top_ref[:, 0:1], total_ref[...]
    top, total = absorb(group, take_queries(q_ref), (kva_ref, kvb_ref), top, total)
    low64 = iota((64, 128), 1) < HD
    for step in range(STEPS):
        span = slice(step * 128, (step + 1) * 128)
        whole = total[span]
        mixed = whole / jnp.where(iota((128, 128), 1) < HD, 1.0, pltpu.roll(whole, HD, 1))
        packed = jnp.where(low64, pltpu.roll(mixed[:64], HD, 1), mixed[64:])
        out_ref[step, 0:64, :] = packed.astype(BF16)
        out_ref[step, 64:80, :] = packed_stats(jnp.log(whole) + top[span])


def attend(kernel, shapes, q, *rest, group=2):
    queries, rows = STEPS * 128, 2 * HEADS * 128
    return pl.pallas_call(
        functools.partial(kernel, group),
        out_shape=shapes,
        in_specs=[VMEM] * (1 + len(rest)),
        out_specs=jax.tree.map(lambda shape: VMEM, shapes),
        compiler_params=pltpu.CompilerParams(vmem_limit_bytes=32 * 2**20),
        cost_estimate=pl.CostEstimate(
            flops=4 * queries * rows * 128, bytes_accessed=2**21, transcendentals=queries * rows
        ),
        name=kernel.__name__,
    )(q, *rest)


def combine_kernel(part_ref, out_ref):
    n = part_ref.shape[0]
    levels = []
    for z in range(n):
        terms = part_ref[z, 64:80, :].astype(F32)
        levels.append(terms[0:1] + terms[1:2] + terms[2:3])
    level = jnp.concatenate(levels, 0)
    weight = jnp.exp(level - jnp.max(level, 0, keepdims=True))
    weight = weight / jnp.sum(weight, 0, keepdims=True)
    weight = jnp.concatenate([weight, jnp.zeros((128 - n, 128), F32)], 0).T
    low64 = iota((64, 128), 1) < HD
    total = jnp.zeros((64, 128), F32)
    for z in range(n):
        column = weight[:, z : z + 1]
        total += jnp.where(low64, column[:64], column[64:]) * part_ref[z, 0:64, :].astype(F32)
    out_ref[...] = total.astype(BF16)


def combine(parts):
    return pl.pallas_call(
        combine_kernel,
        out_shape=jax.ShapeDtypeStruct((64, 128), BF16),
        in_specs=[VMEM],
        out_specs=VMEM,
        name="combine",
    )(parts)


def exchange(blocks, axes):
    return lax.all_to_all(blocks, axes, split_axis=0, concat_axis=0, tiled=True)


def swap(block, axis):
    return lax.ppermute(block, axis, [(0, 1), (1, 0)])


def local(queries, keys, values, w_out):
    held = exchange(pack(queries, keys, values), PLACE)
    held_x = swap(held, "xb")
    held_core = swap(held, "core")
    q_place = held[:, 128:132, :].reshape(1, 64, 128)
    q_all = exchange(jnp.broadcast_to(q_place, (STEPS, 64, 128)), DEPTH)
    held_x, q_all = lax.optimization_barrier((held_x, q_all))
    held_both = swap(held_x, "core")
    state = jax.ShapeDtypeStruct((STEPS * 128, 128), F32)
    top, total = attend(attend_first_kernel, (state, state), q_all, held, held_core)
    result = jax.ShapeDtypeStruct((STEPS, 80, 128), BF16)
    parts = attend(attend_second_kernel, result, q_all, held_x, held_both, top, total)
    attended = combine(exchange(parts, DEPTH)).reshape(HEADS, 4, 128)
    rows = exchange(attended, PLACE).reshape(HEADS, 4, 2, HD)
    rows = rows.transpose(2, 1, 0, 3).reshape(8, HEADS * HD)
    return jnp.dot(rows, w_out, preferred_element_type=F32).astype(BF16)


def solution(mesh):
    split = Mesh(mesh.devices.reshape(4, 2, 2, 2, 2, 4, 2), ALL)
    return jax.shard_map(
        local,
        mesh=split,
        in_specs=(P(ALL, None), P(ALL, None), P(ALL, None), P()),
        out_specs=P(ALL, None),
        check_vma=False,
    )
```

time: 104 us -> 110 us (1.058)
  Pallas kernels: 14.4 us -> 20.8 us
  waiting for transfers between devices: 14.1 us -> 12.2 us
    pallas_call x2 -> x3, Pallas kernels: 12.3 us -> 18.5 us  [the longest x2 16.6 us: attend(): pl.pallas_call(functools.partial(kernel, group), out_shape=shapes, in_spe...]
    ppermute x3, waiting for transfers between devices: 1.96 us -> 0.01 us  [swap(): return lax.ppermute(block, axis, [(0, 1), (1, 0)])]
    all_to_all x2 -> x3, blocking collectives: 52.9 us -> 53.6 us  [exchange(): return lax.all_to_all(blocks, axes, split_axis=0, concat_axis=0, tiled=True)]
  transfers between devices with their start and end apart: 4 -> 4, of which waited for: 2 -> 1; matrix products, arithmetic and copies ran while one was open for 1% -> 1% of each run, Pallas kernels for 0% -> 5%
where the time goes in v6:
time: 110 us
  blocking collectives  53.6 us (49%)
  starting transfers between devices  21.3 us (19%)
  Pallas kernels  20.8 us (19%)
  waiting for transfers between devices  12.2 us (11%)
    all_to_all x3, blocking collectives, exchange(): return lax.all_to_all(blocks, axes, split_axis=0, concat_axis=0, tiled=True)  53.6 us
    pallas_call x2, Pallas kernels, attend(): pl.pallas_call(functools.partial(kernel, group), out_shape=shapes, in_spe...  16.6 us
    all_to_all x1, starting transfers between devices, exchange(): return lax.all_to_all(blocks, axes, split_axis=0, concat_axis=0, tiled=True)  14.2 us
    all_to_all x1, waiting for transfers between devices, exchange(): return lax.all_to_all(blocks, axes, split_axis=0, concat_axis=0, tiled=True)  12.2 us
    ppermute x3, starting transfers between devices, swap(): return lax.ppermute(block, axis, [(0, 1), (1, 0)])  7.15 us
    pallas_call x1, Pallas kernels, pack(): pl.pallas_call(pack_kernel, out_shape=jax.ShapeDtypeStruct((HEADS, 144, 1...  2.23 us
  transfers between devices with their start and end apart: 4, of which 1 were waited for; matrix products, arithmetic and copies ran while one was open for 1% of the time, Pallas kernels for 5%

profile of v6, /device:TPU:2, one launch (start us, length us, event | category | flops | bytes accessed | tf_op | source)
XLA Modules:
  0.0 109.8 jit_solution(16822952463799294680)
XLA Ops:
  0.0 0.0 copy-start
  0.0 2.2 %pack.1 = bf16[16,144,128]{2,1,0:T(8,128)(2,1)} custom-call(bf16[8,1024]{1,0:T(8,128)(2,1)} %q_ref.1, bf16[128,1024]{1,0:T(8,128)(2,1)} %k_ref.1, bf16[128,1024]{1,0:T(8,128)(2,1)} %v_ref.1), custom_call_target="tpu_custom_call" | custom-call | tf_op jit(solution)/shard_map/pack/pallas_call | solution.py:46
  2.2 20.7 %all_to_all.20.kva_ref = bf16[16,144,128]{2,1,0:T(8,128)(2,1)S(1)} all-to-all(bf16[16,144,128]{2,1,0:T(8,128)(2,1)} %pack.1), channel_id=1, replica_groups=mesh['y'=4,'zh'=2,'core'=2,'xa'=2,'xb'=2,'zq'=4,'zo'=2] {'y','xa','zo'}, dimensions={0} | all-to-all | bytes 1179648 | tf_op jit(solution)/shard_map/all_to_all | solution.py:155
  22.9 3.3 %collective-permute-start = (bf16[16,144,128]{2,1,0:T(8,128)(2,1)S(1)}, bf16[16,144,128]{2,1,0:T(8,128)(2,1)S(1)}, u32[]{:S(2)}, u32[]{:S(2)}) collective-permute-start(bf16[16,144,128]{2,1,0:T(8,128)(2,1)S(1)} %all_to_all.20.kva_ref), channel_id=1, source_target_pairs={{0,8},{8,0},{1,9},{9,1},{2,10},{10,2},{3,11},{11,3},{4,12},{12,4},... | collective-permute-start | bytes 1769480 | tf_op jit(solution)/shard_map/ppermute | solution.py:159
  26.2 0.7 broadcast_in_dim.8
  26.9 14.2 %all-to-all-start.1 = ((bf16[8,64,128]{2,1,0:T(8,128)(2,1)}), bf16[8,64,128]{2,1,0:T(8,128)(2,1)S(1)}, u32[]{:S(2)}, u32[]{:S(2)}) async-start(bf16[8,64,128]{2,1,0:T(8,128)(2,1)} %broadcast_in_dim.8), calls=%async_computation.1 | async-start | bytes 262144 | tf_op jit(solution)/shard_map/all_to_all | solution.py:155
  41.1 1.9 %collective-permute-start.2 = (bf16[16,144,128]{2,1,0:T(8,128)(2,1)S(1)}, bf16[16,144,128]{2,1,0:T(8,128)(2,1)}, u32[]{:S(2)}, u32[]{:S(2)}) collective-permute-start(bf16[16,144,128]{2,1,0:T(8,128)(2,1)S(1)} %all_to_all.20.kva_ref), channel_id=1, source_target_pairs={{0,32},{32,0},{1,33},{33,1},{2,34},{34,2},{3,35},{35,3},{4,36},{36... | collective-permute-start | bytes 1769480 | tf_op jit(solution)/shard_map/ppermute | solution.py:159
  43.0 12.2 %all-to-all-done.1.q_ref = bf16[8,64,128]{2,1,0:T(8,128)(2,1)S(1)} async-done(((bf16[8,64,128]{2,1,0:T(8,128)(2,1)}), bf16[8,64,128]{2,1,0:T(8,128)(2,1)S(1)}, u32[]{:S(2)}, u32[]{:S(2)}) %all-to-all-start.1) | async-done | bytes 131104 | tf_op jit(solution)/shard_map/all_to_all | solution.py:155
  55.2 0.0 collective-permute-done.kva_ref
  55.2 1.9 %collective-permute-start.1 = (bf16[16,144,128]{2,1,0:T(8,128)(2,1)S(1)}, bf16[16,144,128]{2,1,0:T(8,128)(2,1)S(1)}, u32[]{:S(2)}, u32[]{:S(2)}) collective-permute-start(bf16[16,144,128]{2,1,0:T(8,128)(2,1)S(1)} %collective-permute-done.kva_ref), channel_id=1, source_target_pairs={{0,32},{32,0},{1,33},{33,1},{2,34},{34,2},{3,35},{35,3},{4,36},{36... | collective-permute-start | bytes 1769480 | tf_op jit(solution)/shard_map/ppermute | solution.py:159
  57.1 0.0 collective-permute-done.2.kvb_ref
  57.1 5.9 %attend_first_kernel.1 = (f32[1024,128]{1,0:T(8,128)S(1)}, f32[1024,128]{1,0:T(8,128)S(1)}) custom-call(bf16[8,64,128]{2,1,0:T(8,128)(2,1)S(1)} %all-to-all-done.1.q_ref, bf16[16,144,128]{2,1,0:T(8,128)(2,1)S(1)} %all_to_all.20.kva_ref, bf16[16,144,128]{2,1,0:T(8,128)(2,1)} %collective-permute-done.2.kvb_ref), custom_call_target="tpu_custom_call" | custom-call | flops 2147483648 | bytes 2097152 | tf_op jit(solution)/shard_map/attend_first_kernel/pallas_call | solution.py:113
  63.1 0.0 collective-permute-done.1.kvb_ref
  63.1 10.7 %attend_second_kernel.1 = bf16[8,80,128]{2,1,0:T(8,128)(2,1)S(1)} custom-call(bf16[8,64,128]{2,1,0:T(8,128)(2,1)S(1)} %all-to-all-done.1.q_ref, bf16[16,144,128]{2,1,0:T(8,128)(2,1)S(1)} %collective-permute-done.kva_ref, bf16[16,144,128]{2,1,0:T(8,128)(2,1)S(1)} %collective-permute-done.1.kvb_ref, f32[1024,128]{1,0:T(8,128)S(1)} %get-tuple-element.11.top_ref, ...), custom_call_target="tpu_custom_call" | custom-call | flops 2147483648 | bytes 2097152 | tf_op jit(solution)/shard_map/attend_second_kernel/pallas_call | solution.py:113
  73.8 21.0 %all_to_all.21.part_ref = bf16[8,80,128]{2,1,0:T(8,128)(2,1)} all-to-all(bf16[8,80,128]{2,1,0:T(8,128)(2,1)S(1)} %attend_second_kernel.1), channel_id=1, replica_groups=mesh['y'=4,'zh'=2,'core'=2,'xa'=2,'xb'=2,'zq'=4,'zo'=2] {'zh','zq'}, dimensions={0} | all-to-all | bytes 327680 | tf_op jit(solution)/shard_map/all_to_all | solution.py:155
  94.7 1.9 %combine.1 = bf16[64,128]{1,0:T(8,128)(2,1)} custom-call(bf16[8,80,128]{2,1,0:T(8,128)(2,1)} %all_to_all.21.part_ref), custom_call_target="tpu_custom_call" | custom-call | tf_op jit(solution)/shard_map/combine/pallas_call | solution.py:145
  96.6 11.9 %all_to_all.22 = bf16[16,4,128]{2,1,0:T(4,128)(2,1)S(1)} all-to-all(bf16[16,4,128]{2,1,0:T(4,128)(2,1)} %bitcast.11), channel_id=1, replica_groups=mesh['y'=4,'zh'=2,'core'=2,'xa'=2,'xb'=2,'zq'=4,'zo'=2] {'y','xa','zo'}, dimensions={0} | all-to-all | bytes 32768 | tf_op jit(solution)/shard_map/all_to_all | solution.py:155
  108.6 0.1 reshape.12
  108.7 0.1 reshape.13
  108.8 0.0 copy-done
  108.8 1.0 convolution_convert_fusion
  (3 shorter events, 0.0 us)
Async XLA Ops:
  0.0 108.8 %copy-start = (bf16[1024,1024]{1,0:T(8,128)(2,1)S(1)}, bf16[1024,1024]{1,0:T(8,128)(2,1)}, u32[]{:S(2)}) copy-start(bf16[1024,1024]{1,0:T(8,128)(2,1)} %param.7) | copy-start | bytes 6291460
  22.9 32.3 %collective-permute-start = (bf16[16,144,128]{2,1,0:T(8,128)(2,1)S(1)}, bf16[16,144,128]{2,1,0:T(8,128)(2,1)S(1)}, u32[]{:S(2)}, u32[]{:S(2)}) collective-permute-start(bf16[16,144,128]{2,1,0:T(8,128)(2,1)S(1)} %all_to_all.20.kva_ref), channel_id=1, source_target_pairs={{0,8},{8,0},{1,9},{9,1},{2,10},{10,2},{3,11},{11,3},{4,12},{12,4},... | collective-permute-start | bytes 1769480 | tf_op jit(solution)/shard_map/ppermute | solution.py:159
  26.9 28.3 %all-to-all-start.1 = ((bf16[8,64,128]{2,1,0:T(8,128)(2,1)}), bf16[8,64,128]{2,1,0:T(8,128)(2,1)S(1)}, u32[]{:S(2)}, u32[]{:S(2)}) async-start(bf16[8,64,128]{2,1,0:T(8,128)(2,1)} %broadcast_in_dim.8), calls=%async_computation.1 | async-start | bytes 262144 | tf_op jit(solution)/shard_map/all_to_all | solution.py:155
  41.1 16.0 %collective-permute-start.2 = (bf16[16,144,128]{2,1,0:T(8,128)(2,1)S(1)}, bf16[16,144,128]{2,1,0:T(8,128)(2,1)}, u32[]{:S(2)}, u32[]{:S(2)}) collective-permute-start(bf16[16,144,128]{2,1,0:T(8,128)(2,1)S(1)} %all_to_all.20.kva_ref), channel_id=1, source_target_pairs={{0,32},{32,0},{1,33},{33,1},{2,34},{34,2},{3,35},{35,3},{4,36},{36... | collective-permute-start | bytes 1769480 | tf_op jit(solution)/shard_map/ppermute | solution.py:159
  55.2 7.9 %collective-permute-start.1 = (bf16[16,144,128]{2,1,0:T(8,128)(2,1)S(1)}, bf16[16,144,128]{2,1,0:T(8,128)(2,1)S(1)}, u32[]{:S(2)}, u32[]{:S(2)}) collective-permute-start(bf16[16,144,128]{2,1,0:T(8,128)(2,1)S(1)} %collective-permute-done.kva_ref), channel_id=1, source_target_pairs={{0,32},{32,0},{1,33},{33,1},{2,34},{34,2},{3,35},{35,3},{4,36},{36... | collective-permute-start | bytes 1769480 | tf_op jit(solution)/shard_map/ppermute | solution.py:159

commit v7 on v3

--- a/solution.py
+++ b/solution.py
@@ -52,24 +52,23 @@
     )(q, k, v)
 
 
-def attend_kernel(group, q_ref, *refs):
-    kv_refs, out_ref = refs[:4], refs[4]
+def take_queries(q_ref):
     low64 = iota((64, 128), 1) < HD
-    rows = group * 128
-    low = iota((rows, 128), 1) < HD
     parts = []
     for step in range(STEPS):
         pair = q_ref[step].astype(F32) * HD**-0.5
         parts.append(jnp.where(low64, pair, 0.0))
         parts.append(jnp.where(low64, pltpu.roll(pair, HD, 1), 0.0))
-    q = jnp.concatenate(parts, 0).astype(BF16)
-    top, total = None, None
+    return jnp.concatenate(parts, 0).astype(BF16)
+
+
+def absorb(group, q, kv_refs, top, total):
+    rows = group * 128
+    low = iota((rows, 128), 1) < HD
     for kv_ref in kv_refs:
         for c in range(HEADS // group):
             kv = kv_ref[c * group : (c + 1) * group, 0:128, :].reshape(rows, 128)
-            score = lax.dot_general(
-                q, kv, (((1,), (1,)), ((), ())), preferred_element_type=F32
-            )
+            score = lax.dot_general(q, kv, (((1,), (1,)), ((), ())), preferred_element_type=F32)
             here = jnp.max(score, 1, keepdims=True)
             new = here if top is None else jnp.maximum(top, here)
             weights = jnp.exp(score - new).astype(BF16)
@@ -77,6 +76,19 @@
             part = jnp.dot(weights, marked, preferred_element_type=F32)
             total = part if top is None else total * jnp.exp(top - new) + part
             top = new
+    return top, total
+
+
+def attend_first_kernel(group, q_ref, kva_ref, kvb_ref, top_ref, total_ref):
+    top, total = absorb(group, take_queries(q_ref), (kva_ref, kvb_ref), None, None)
+    top_ref[...] = jnp.broadcast_to(top, top_ref.shape)
+    total_ref[...] = total
+
+
+def attend_second_kernel(group, q_ref, kva_ref, kvb_ref, top_ref, total_ref, out_ref):
+    top, total = jnp.max(top_ref[...], 1, keepdims=True), total_ref[...]
+    top, total = absorb(group, take_queries(q_ref), (kva_ref, kvb_ref), top, total)
+    low64 = iota((64, 128), 1) < HD
     sub = iota((64, 128), 0) % 8 < 4
     first_half = iota((64, 128), 1) % HD < HD // 2
     for step in range(STEPS):
@@ -98,21 +110,19 @@
         out_ref[step * 128 : (step + 1) * 128, :] = both.astype(BF16)
 
 
-def attend(q, kvs, group=2):
-    rows = len(kvs) * HEADS * 128
+def attend(kernel, shapes, q, *rest, group=2):
+    queries, rows = STEPS * 128, 2 * HEADS * 128
     return pl.pallas_call(
-        functools.partial(attend_kernel, group),
-        out_shape=jax.ShapeDtypeStruct((STEPS * 128, 128), BF16),
-        in_specs=[VMEM] * (1 + len(kvs)),
-        out_specs=VMEM,
-        compiler_params=pltpu.CompilerParams(vmem_limit_bytes=48 * 2**20),
+        functools.partial(kernel, group),
+        out_shape=shapes,
+        in_specs=[VMEM] * (1 + len(rest)),
+        out_specs=jax.tree.map(lambda shape: VMEM, shapes),
+        compiler_params=pltpu.CompilerParams(vmem_limit_bytes=32 * 2**20),
         cost_estimate=pl.CostEstimate(
-            flops=4 * STEPS * 128 * rows * 128,
-            bytes_accessed=2**22,
-            transcendentals=STEPS * 128 * rows,
+            flops=4 * queries * rows * 128, bytes_accessed=2**21, transcendentals=queries * rows
         ),
-        name="attend",
-    )(q, *kvs)
+        name=kernel.__name__,
+    )(q, *rest)
 
 
 def finish_kernel(part_ref, w_ref, out_ref):
@@ -165,7 +175,10 @@
     q_all = exchange(jnp.broadcast_to(q_place, (STEPS, 64, 128)), DEPTH)
     held_x, q_all = lax.optimization_barrier((held_x, q_all))
     held_both = swap(held_x, "core")
-    parts = attend(q_all, (held, held_core, held_x, held_both))
+    state = jax.ShapeDtypeStruct((STEPS * 128, 128), F32)
+    top, total = attend(attend_first_kernel, (state, state), q_all, held, held_core)
+    result = jax.ShapeDtypeStruct((STEPS * 128, 128), BF16)
+    parts = attend(attend_second_kernel, result, q_all, held_x, held_both, top, total)
     parts = exchange(parts.reshape(STEPS * HEADS, 8, 128), DEPTH + PLACE)
     return finish(parts.reshape(STEPS * HEADS * 8, 128), w_out)
 

time: 104 us -> 103 us (level)
  waiting for transfers between devices: 14.1 us -> 12.2 us
    ppermute x3, waiting for transfers between devices: 1.96 us -> 0.01 us  [swap(): return lax.ppermute(block, axis, [(0, 1), (1, 0)])]
    pallas_call x1 -> x2, Pallas kernels: 9.38 us -> 9.92 us  [attend(): pl.pallas_call(functools.partial(kernel, group), out_shape=shapes, in_spe...]
  transfers between devices with their start and end apart: 4 -> 4, of which waited for: 2 -> 1; matrix products, arithmetic and copies ran while one was open for 1% -> 1% of each run, Pallas kernels for 0% -> 5%
where the time goes in v7:
time: 103 us
  blocking collectives  53.3 us (52%)
  starting transfers between devices  21.3 us (21%)
  Pallas kernels  15 us (15%)
  waiting for transfers between devices  12.2 us (12%)
    all_to_all x2, blocking collectives, exchange(): return lax.all_to_all(blocks, axes, split_axis=0, concat_axis=0, tiled=True)  53.3 us
    all_to_all x1, starting transfers between devices, exchange(): return lax.all_to_all(blocks, axes, split_axis=0, concat_axis=0, tiled=True)  14.2 us
    all_to_all x1, waiting for transfers between devices, exchange(): return lax.all_to_all(blocks, axes, split_axis=0, concat_axis=0, tiled=True)  12.2 us
    pallas_call x2, Pallas kernels, attend(): pl.pallas_call(functools.partial(kernel, group), out_shape=shapes, in_spe...  9.92 us
    ppermute x3, starting transfers between devices, swap(): return lax.ppermute(block, axis, [(0, 1), (1, 0)])  7.15 us
    pallas_call x1, Pallas kernels, finish(): pl.pallas_call(finish_kernel, out_shape=jax.ShapeDtypeStruct((8, HEADS *...  2.97 us
    pallas_call x1, Pallas kernels, pack(): pl.pallas_call(pack_kernel, out_shape=jax.ShapeDtypeStruct((HEADS, 144, 1...  2.09 us
  transfers between devices with their start and end apart: 4, of which 1 were waited for; matrix products, arithmetic and copies ran while one was open for 1% of the time, Pallas kernels for 5%

profile of v7, /device:TPU:2, one launch (start us, length us, event | category | flops | bytes accessed | tf_op | source)
XLA Modules:
  0.0 102.6 jit_solution(1530002206025309181)
XLA Ops:
  0.0 2.1 %pack.1 = bf16[16,144,128]{2,1,0:T(8,128)(2,1)} custom-call(bf16[8,1024]{1,0:T(8,128)(2,1)} %q_ref.1, bf16[128,1024]{1,0:T(8,128)(2,1)} %k_ref.1, bf16[128,1024]{1,0:T(8,128)(2,1)} %v_ref.1), custom_call_target="tpu_custom_call" | custom-call | tf_op jit(solution)/shard_map/pack/pallas_call | solution.py:46
  2.1 20.7 %all_to_all.15.kva_ref = bf16[16,144,128]{2,1,0:T(8,128)(2,1)S(1)} all-to-all(bf16[16,144,128]{2,1,0:T(8,128)(2,1)} %pack.1), channel_id=1, replica_groups=mesh['y'=4,'zh'=2,'core'=2,'xa'=2,'xb'=2,'zq'=4,'zo'=2] {'y','xa','zo'}, dimensions={0} | all-to-all | bytes 1179648 | tf_op jit(solution)/shard_map/all_to_all | solution.py:163
  22.7 3.3 %collective-permute-start = (bf16[16,144,128]{2,1,0:T(8,128)(2,1)S(1)}, bf16[16,144,128]{2,1,0:T(8,128)(2,1)S(1)}, u32[]{:S(2)}, u32[]{:S(2)}) collective-permute-start(bf16[16,144,128]{2,1,0:T(8,128)(2,1)S(1)} %all_to_all.15.kva_ref), channel_id=1, source_target_pairs={{0,8},{8,0},{1,9},{9,1},{2,10},{10,2},{3,11},{11,3},{4,12},{12,4},... | collective-permute-start | bytes 1769480 | tf_op jit(solution)/shard_map/ppermute | solution.py:167
  26.1 0.7 broadcast_in_dim.8
  26.8 14.2 %all-to-all-start.1 = ((bf16[8,64,128]{2,1,0:T(8,128)(2,1)}), bf16[8,64,128]{2,1,0:T(8,128)(2,1)S(1)}, u32[]{:S(2)}, u32[]{:S(2)}) async-start(bf16[8,64,128]{2,1,0:T(8,128)(2,1)} %broadcast_in_dim.8), calls=%async_computation.1 | async-start | bytes 262144 | tf_op jit(solution)/shard_map/all_to_all | solution.py:163
  41.0 1.9 %collective-permute-start.2 = (bf16[16,144,128]{2,1,0:T(8,128)(2,1)S(1)}, bf16[16,144,128]{2,1,0:T(8,128)(2,1)S(1)}, u32[]{:S(2)}, u32[]{:S(2)}) collective-permute-start(bf16[16,144,128]{2,1,0:T(8,128)(2,1)S(1)} %all_to_all.15.kva_ref), channel_id=1, source_target_pairs={{0,32},{32,0},{1,33},{33,1},{2,34},{34,2},{3,35},{35,3},{4,36},{36... | collective-permute-start | bytes 1769480 | tf_op jit(solution)/shard_map/ppermute | solution.py:167
  42.9 12.2 %all-to-all-done.1.q_ref = bf16[8,64,128]{2,1,0:T(8,128)(2,1)S(1)} async-done(((bf16[8,64,128]{2,1,0:T(8,128)(2,1)}), bf16[8,64,128]{2,1,0:T(8,128)(2,1)S(1)}, u32[]{:S(2)}, u32[]{:S(2)}) %all-to-all-start.1) | async-done | bytes 131104 | tf_op jit(solution)/shard_map/all_to_all | solution.py:163
  55.0 0.0 collective-permute-done.kva_ref
  55.0 1.9 %collective-permute-start.1 = (bf16[16,144,128]{2,1,0:T(8,128)(2,1)S(1)}, bf16[16,144,128]{2,1,0:T(8,128)(2,1)S(1)}, u32[]{:S(2)}, u32[]{:S(2)}) collective-permute-start(bf16[16,144,128]{2,1,0:T(8,128)(2,1)S(1)} %collective-permute-done.kva_ref), channel_id=1, source_target_pairs={{0,32},{32,0},{1,33},{33,1},{2,34},{34,2},{3,35},{35,3},{4,36},{36... | collective-permute-start | bytes 1769480 | tf_op jit(solution)/shard_map/ppermute | solution.py:167
  57.0 0.0 collective-permute-done.2.kvb_ref
  57.0 4.9 %attend_first_kernel.1 = (f32[1024,128]{1,0:T(8,128)S(1)}, f32[1024,128]{1,0:T(8,128)S(1)}) custom-call(bf16[8,64,128]{2,1,0:T(8,128)(2,1)S(1)} %all-to-all-done.1.q_ref, bf16[16,144,128]{2,1,0:T(8,128)(2,1)S(1)} %all_to_all.15.kva_ref, bf16[16,144,128]{2,1,0:T(8,128)(2,1)S(1)} %collective-permute-done.2.kvb_ref), custom_call_target="tpu_custom_call" | custom-call | flops 2147483648 | bytes 2097152 | tf_op jit(solution)/shard_map/attend_first_kernel/pallas_call | solution.py:115
  61.9 0.0 collective-permute-done.1.kvb_ref
  61.9 5.0 %attend_second_kernel.1 = bf16[1024,128]{1,0:T(8,128)(2,1)S(1)} custom-call(bf16[8,64,128]{2,1,0:T(8,128)(2,1)S(1)} %all-to-all-done.1.q_ref, bf16[16,144,128]{2,1,0:T(8,128)(2,1)S(1)} %collective-permute-done.kva_ref, bf16[16,144,128]{2,1,0:T(8,128)(2,1)S(1)} %collective-permute-done.1.kvb_ref, f32[1024,128]{1,0:T(8,128)S(1)} %get-tuple-element.11.top_ref, ...), custom_call_target="tpu_custom_call" | custom-call | flops 2147483648 | bytes 2097152 | tf_op jit(solution)/shard_map/attend_second_kernel/pallas_call | solution.py:115
  66.9 32.7 %all_to_all.16 = bf16[128,8,128]{2,1,0:T(8,128)(2,1)} all-to-all(bf16[128,8,128]{2,1,0:T(8,128)(2,1)S(1)} %bitcast.3), channel_id=1, replica_groups=mesh['y'=4,'zh'=2,'core'=2,'xa'=2,'xb'=2,'zq'=4,'zo'=2] {'zh','zq','y','..., dimensions={0} | all-to-all | bytes 524288 | tf_op jit(solution)/shard_map/all_to_all | solution.py:163
  99.6 3.0 %finish.1 = bf16[8,1024]{1,0:T(8,128)(2,1)} custom-call(bf16[1024,128]{1,0:T(8,128)(2,1)} %bitcast.4, bf16[1024,1024]{1,0:T(8,128)(2,1)} %w_ref.1), custom_call_target="tpu_custom_call" | custom-call | tf_op jit(solution)/shard_map/finish/pallas_call | solution.py:153
  (1 shorter events, 0.0 us)
Async XLA Ops:
  22.7 32.3 %collective-permute-start = (bf16[16,144,128]{2,1,0:T(8,128)(2,1)S(1)}, bf16[16,144,128]{2,1,0:T(8,128)(2,1)S(1)}, u32[]{:S(2)}, u32[]{:S(2)}) collective-permute-start(bf16[16,144,128]{2,1,0:T(8,128)(2,1)S(1)} %all_to_all.15.kva_ref), channel_id=1, source_target_pairs={{0,8},{8,0},{1,9},{9,1},{2,10},{10,2},{3,11},{11,3},{4,12},{12,4},... | collective-permute-start | bytes 1769480 | tf_op jit(solution)/shard_map/ppermute | solution.py:167
  26.8 28.3 %all-to-all-start.1 = ((bf16[8,64,128]{2,1,0:T(8,128)(2,1)}), bf16[8,64,128]{2,1,0:T(8,128)(2,1)S(1)}, u32[]{:S(2)}, u32[]{:S(2)}) async-start(bf16[8,64,128]{2,1,0:T(8,128)(2,1)} %broadcast_in_dim.8), calls=%async_computation.1 | async-start | bytes 262144 | tf_op jit(solution)/shard_map/all_to_all | solution.py:163
  41.0 16.0 %collective-permute-start.2 = (bf16[16,144,128]{2,1,0:T(8,128)(2,1)S(1)}, bf16[16,144,128]{2,1,0:T(8,128)(2,1)S(1)}, u32[]{:S(2)}, u32[]{:S(2)}) collective-permute-start(bf16[16,144,128]{2,1,0:T(8,128)(2,1)S(1)} %all_to_all.15.kva_ref), channel_id=1, source_target_pairs={{0,32},{32,0},{1,33},{33,1},{2,34},{34,2},{3,35},{35,3},{4,36},{36... | collective-permute-start | bytes 1769480 | tf_op jit(solution)/shard_map/ppermute | solution.py:167
  55.0 6.8 %collective-permute-start.1 = (bf16[16,144,128]{2,1,0:T(8,128)(2,1)S(1)}, bf16[16,144,128]{2,1,0:T(8,128)(2,1)S(1)}, u32[]{:S(2)}, u32[]{:S(2)}) collective-permute-start(bf16[16,144,128]{2,1,0:T(8,128)(2,1)S(1)} %collective-permute-done.kva_ref), channel_id=1, source_target_pairs={{0,32},{32,0},{1,33},{33,1},{2,34},{34,2},{3,35},{35,3},{4,36},{36... | collective-permute-start | bytes 1769480 | tf_op jit(solution)/shard_map/ppermute | solution.py:167

commit v8 on v7

--- a/solution.py
+++ b/solution.py
@@ -173,12 +173,11 @@
     held_core = swap(held, "core")
     q_place = held[:, 128:132, :].reshape(1, 64, 128)
     q_all = exchange(jnp.broadcast_to(q_place, (STEPS, 64, 128)), DEPTH)
-    held_x, q_all = lax.optimization_barrier((held_x, q_all))
-    held_both = swap(held_x, "core")
+    held_both = lax.ppermute(held, ("core", "xb"), [(0, 3), (1, 2), (2, 1), (3, 0)])
     state = jax.ShapeDtypeStruct((STEPS * 128, 128), F32)
-    top, total = attend(attend_first_kernel, (state, state), q_all, held, held_core)
+    top, total = attend(attend_first_kernel, (state, state), q_all, held, held_x)
     result = jax.ShapeDtypeStruct((STEPS * 128, 128), BF16)
-    parts = attend(attend_second_kernel, result, q_all, held_x, held_both, top, total)
+    parts = attend(attend_second_kernel, result, q_all, held_core, held_both, top, total)
     parts = exchange(parts.reshape(STEPS * HEADS, 8, 128), DEPTH + PLACE)
     return finish(parts.reshape(STEPS * HEADS * 8, 128), w_out)
 

time: 103 us -> 107 us (1.039)
  blocking collectives: 53.3 us -> 58.8 us
  waiting for transfers between devices: 12.2 us -> 9.57 us
    all_to_all x2, blocking collectives: 53.3 us -> 58.8 us  [exchange(): return lax.all_to_all(blocks, axes, split_axis=0, concat_axis=0, tiled=True)]
    all_to_all x1, waiting for transfers between devices: 12.2 us -> 9.56 us  [exchange(): return lax.all_to_all(blocks, axes, split_axis=0, concat_axis=0, tiled=True)]
    ppermute x0 -> x1, starting transfers between devices: none -> 1.91 us  [local(): lax.ppermute(held, ('core', 'xb'), [(0, 3), (1, 2), (2, 1), (3, 0)])]
    ppermute x3 -> x2, starting transfers between devices: 7.15 us -> 5.93 us  [swap(): return lax.ppermute(block, axis, [(0, 1), (1, 0)])]
where the time goes in v8:
time: 107 us; the launch traced here: 106 us
  blocking collectives  58.8 us (55%)
  starting transfers between devices  22 us (21%)
  Pallas kernels  15 us (14%)
  waiting for transfers between devices  9.57 us (9%)
    all_to_all x2, blocking collectives, exchange(): return lax.all_to_all(blocks, axes, split_axis=0, concat_axis=0, tiled=True)  58.8 us
    all_to_all x1, starting transfers between devices, exchange(): return lax.all_to_all(blocks, axes, split_axis=0, concat_axis=0, tiled=True)  14.2 us
    pallas_call x2, Pallas kernels, attend(): pl.pallas_call(functools.partial(kernel, group), out_shape=shapes, in_spe...  9.91 us
    all_to_all x1, waiting for transfers between devices, exchange(): return lax.all_to_all(blocks, axes, split_axis=0, concat_axis=0, tiled=True)  9.56 us
    ppermute x2, starting transfers between devices, swap(): return lax.ppermute(block, axis, [(0, 1), (1, 0)])  5.93 us
    pallas_call x1, Pallas kernels, finish(): pl.pallas_call(finish_kernel, out_shape=jax.ShapeDtypeStruct((8, HEADS *...  2.97 us
  transfers between devices with their start and end apart: 4, of which 1 were waited for; matrix products, arithmetic and copies ran while one was open for 1% of the time, Pallas kernels for 5%

profile of v8, /device:TPU:2, one launch (start us, length us, event | category | flops | bytes accessed | tf_op | source)
XLA Modules:
  0.0 106.1 jit_solution(15533212324233002597)
XLA Ops:
  0.0 2.1 %pack.1 = bf16[16,144,128]{2,1,0:T(8,128)(2,1)} custom-call(bf16[8,1024]{1,0:T(8,128)(2,1)} %q_ref.1, bf16[128,1024]{1,0:T(8,128)(2,1)} %k_ref.1, bf16[128,1024]{1,0:T(8,128)(2,1)} %v_ref.1), custom_call_target="tpu_custom_call" | custom-call | tf_op jit(solution)/shard_map/pack/pallas_call | solution.py:46
  2.1 20.7 %all_to_all.15.kva_ref = bf16[16,144,128]{2,1,0:T(8,128)(2,1)S(1)} all-to-all(bf16[16,144,128]{2,1,0:T(8,128)(2,1)} %pack.1), channel_id=1, replica_groups=mesh['y'=4,'zh'=2,'core'=2,'xa'=2,'xb'=2,'zq'=4,'zo'=2] {'y','xa','zo'}, dimensions={0} | all-to-all | bytes 1179648 | tf_op jit(solution)/shard_map/all_to_all | solution.py:163
  22.7 3.3 %collective-permute-start.2 = (bf16[16,144,128]{2,1,0:T(8,128)(2,1)S(1)}, bf16[16,144,128]{2,1,0:T(8,128)(2,1)S(1)}, u32[]{:S(2)}, u32[]{:S(2)}) collective-permute-start(bf16[16,144,128]{2,1,0:T(8,128)(2,1)S(1)} %all_to_all.15.kva_ref), channel_id=1, source_target_pairs={{0,8},{8,0},{1,9},{9,1},{2,10},{10,2},{3,11},{11,3},{4,12},{12,4},... | collective-permute-start | bytes 1769480 | tf_op jit(solution)/shard_map/ppermute | solution.py:167
  26.1 0.7 broadcast_in_dim.8
  26.8 14.2 %all-to-all-start.1 = ((bf16[8,64,128]{2,1,0:T(8,128)(2,1)}), bf16[8,64,128]{2,1,0:T(8,128)(2,1)S(1)}, u32[]{:S(2)}, u32[]{:S(2)}) async-start(bf16[8,64,128]{2,1,0:T(8,128)(2,1)} %broadcast_in_dim.8), calls=%async_computation.1 | async-start | bytes 262144 | tf_op jit(solution)/shard_map/all_to_all | solution.py:163
  41.0 1.9 %collective-permute-start.1 = (bf16[16,144,128]{2,1,0:T(8,128)(2,1)S(1)}, bf16[16,144,128]{2,1,0:T(8,128)(2,1)S(1)}, u32[]{:S(2)}, u32[]{:S(2)}) collective-permute-start(bf16[16,144,128]{2,1,0:T(8,128)(2,1)S(1)} %all_to_all.15.kva_ref), channel_id=1, source_target_pairs={{0,40},{8,32},{32,8},{40,0},{1,41},{9,33},{33,9},{41,1},{2,42},{10... | collective-permute-start | bytes 1769480 | tf_op jit(solution)/shard_map/ppermute | solution.py:176
  42.9 2.6 %collective-permute-start = (bf16[16,144,128]{2,1,0:T(8,128)(2,1)S(1)}, bf16[16,144,128]{2,1,0:T(8,128)(2,1)S(1)}, u32[]{:S(2)}, u32[]{:S(2)}) collective-permute-start(bf16[16,144,128]{2,1,0:T(8,128)(2,1)S(1)} %all_to_all.15.kva_ref), channel_id=1, source_target_pairs={{0,32},{32,0},{1,33},{33,1},{2,34},{34,2},{3,35},{35,3},{4,36},{36... | collective-permute-start | bytes 1769480 | tf_op jit(solution)/shard_map/ppermute | solution.py:167
  45.5 9.6 %all-to-all-done.1.q_ref = bf16[8,64,128]{2,1,0:T(8,128)(2,1)S(1)} async-done(((bf16[8,64,128]{2,1,0:T(8,128)(2,1)}), bf16[8,64,128]{2,1,0:T(8,128)(2,1)S(1)}, u32[]{:S(2)}, u32[]{:S(2)}) %all-to-all-start.1) | async-done | bytes 131104 | tf_op jit(solution)/shard_map/all_to_all | solution.py:163
  55.0 0.0 collective-permute-done.2.kvb_ref
  55.0 4.9 %attend_first_kernel.1 = (f32[1024,128]{1,0:T(8,128)S(1)}, f32[1024,128]{1,0:T(8,128)S(1)}) custom-call(bf16[8,64,128]{2,1,0:T(8,128)(2,1)S(1)} %all-to-all-done.1.q_ref, bf16[16,144,128]{2,1,0:T(8,128)(2,1)S(1)} %all_to_all.15.kva_ref, bf16[16,144,128]{2,1,0:T(8,128)(2,1)S(1)} %collective-permute-done.2.kvb_ref), custom_call_target="tpu_custom_call" | custom-call | flops 2147483648 | bytes 2097152 | tf_op jit(solution)/shard_map/attend_first_kernel/pallas_call | solution.py:115
  59.9 0.0 collective-permute-done.1.kvb_ref
  59.9 0.0 collective-permute-done.kva_ref
  59.9 5.0 %attend_second_kernel.1 = bf16[1024,128]{1,0:T(8,128)(2,1)S(1)} custom-call(bf16[8,64,128]{2,1,0:T(8,128)(2,1)S(1)} %all-to-all-done.1.q_ref, bf16[16,144,128]{2,1,0:T(8,128)(2,1)S(1)} %collective-permute-done.kva_ref, bf16[16,144,128]{2,1,0:T(8,128)(2,1)S(1)} %collective-permute-done.1.kvb_ref, f32[1024,128]{1,0:T(8,128)S(1)} %get-tuple-element.7.top_ref, ...), custom_call_target="tpu_custom_call" | custom-call | flops 2147483648 | bytes 2097152 | tf_op jit(solution)/shard_map/attend_second_kernel/pallas_call | solution.py:115
  65.0 38.2 %all_to_all.16 = bf16[128,8,128]{2,1,0:T(8,128)(2,1)} all-to-all(bf16[128,8,128]{2,1,0:T(8,128)(2,1)S(1)} %bitcast.3), channel_id=1, replica_groups=mesh['y'=4,'zh'=2,'core'=2,'xa'=2,'xb'=2,'zq'=4,'zo'=2] {'zh','zq','y','..., dimensions={0} | all-to-all | bytes 524288 | tf_op jit(solution)/shard_map/all_to_all | solution.py:163
  103.2 3.0 %finish.1 = bf16[8,1024]{1,0:T(8,128)(2,1)} custom-call(bf16[1024,128]{1,0:T(8,128)(2,1)} %bitcast.4, bf16[1024,1024]{1,0:T(8,128)(2,1)} %w_ref.1), custom_call_target="tpu_custom_call" | custom-call | tf_op jit(solution)/shard_map/finish/pallas_call | solution.py:153
  (1 shorter events, 0.0 us)
Async XLA Ops:
  22.7 32.3 %collective-permute-start.2 = (bf16[16,144,128]{2,1,0:T(8,128)(2,1)S(1)}, bf16[16,144,128]{2,1,0:T(8,128)(2,1)S(1)}, u32[]{:S(2)}, u32[]{:S(2)}) collective-permute-start(bf16[16,144,128]{2,1,0:T(8,128)(2,1)S(1)} %all_to_all.15.kva_ref), channel_id=1, source_target_pairs={{0,8},{8,0},{1,9},{9,1},{2,10},{10,2},{3,11},{11,3},{4,12},{12,4},... | collective-permute-start | bytes 1769480 | tf_op jit(solution)/shard_map/ppermute | solution.py:167
  26.8 28.3 %all-to-all-start.1 = ((bf16[8,64,128]{2,1,0:T(8,128)(2,1)}), bf16[8,64,128]{2,1,0:T(8,128)(2,1)S(1)}, u32[]{:S(2)}, u32[]{:S(2)}) async-start(bf16[8,64,128]{2,1,0:T(8,128)(2,1)} %broadcast_in_dim.8), calls=%async_computation.1 | async-start | bytes 262144 | tf_op jit(solution)/shard_map/all_to_all | solution.py:163
  41.0 19.0 %collective-permute-start.1 = (bf16[16,144,128]{2,1,0:T(8,128)(2,1)S(1)}, bf16[16,144,128]{2,1,0:T(8,128)(2,1)S(1)}, u32[]{:S(2)}, u32[]{:S(2)}) collective-permute-start(bf16[16,144,128]{2,1,0:T(8,128)(2,1)S(1)} %all_to_all.15.kva_ref), channel_id=1, source_target_pairs={{0,40},{8,32},{32,8},{40,0},{1,41},{9,33},{33,9},{41,1},{2,42},{10... | collective-permute-start | bytes 1769480 | tf_op jit(solution)/shard_map/ppermute | solution.py:176
  42.9 17.1 %collective-permute-start = (bf16[16,144,128]{2,1,0:T(8,128)(2,1)S(1)}, bf16[16,144,128]{2,1,0:T(8,128)(2,1)S(1)}, u32[]{:S(2)}, u32[]{:S(2)}) collective-permute-start(bf16[16,144,128]{2,1,0:T(8,128)(2,1)S(1)} %all_to_all.15.kva_ref), channel_id=1, source_target_pairs={{0,32},{32,0},{1,33},{33,1},{2,34},{34,2},{3,35},{35,3},{4,36},{36... | collective-permute-start | bytes 1769480 | tf_op jit(solution)/shard_map/ppermute | solution.py:167

commit v9 on v7

--- a/solution.py
+++ b/solution.py
@@ -11,7 +11,7 @@
 HEADS = 16
 STEPS = 8
 ALL = ("y", "zh", "core", "xa", "xb", "zq", "zo")
-PLACE = ("y", "xa", "zo")
+PLACE = ("zo", "xa", "y")
 DEPTH = ("zh", "zq")
 F32 = jnp.float32
 BF16 = jnp.bfloat16

time: 103 us -> 101 us (0.981)
  the two profiles are of different devices: /device:TPU:2 before, /device:TPU:32 now
where the time goes in v9:
time: 101 us
  blocking collectives  52.5 us (52%)
  starting transfers between devices  20.5 us (20%)
  Pallas kernels  15 us (15%)
  waiting for transfers between devices  12.1 us (12%)
    all_to_all x2, blocking collectives, exchange(): return lax.all_to_all(blocks, axes, split_axis=0, concat_axis=0, tiled=True)  52.5 us
    all_to_all x1, starting transfers between devices, exchange(): return lax.all_to_all(blocks, axes, split_axis=0, concat_axis=0, tiled=True)  14.2 us
    all_to_all x1, waiting for transfers between devices, exchange(): return lax.all_to_all(blocks, axes, split_axis=0, concat_axis=0, tiled=True)  12.1 us
    pallas_call x2, Pallas kernels, attend(): pl.pallas_call(functools.partial(kernel, group), out_shape=shapes, in_spe...  9.91 us
    ppermute x3, starting transfers between devices, swap(): return lax.ppermute(block, axis, [(0, 1), (1, 0)])  6.35 us
    pallas_call x1, Pallas kernels, finish(): pl.pallas_call(finish_kernel, out_shape=jax.ShapeDtypeStruct((8, HEADS *...  2.97 us
    pallas_call x1, Pallas kernels, pack(): pl.pallas_call(pack_kernel, out_shape=jax.ShapeDtypeStruct((HEADS, 144, 1...  2.09 us
  transfers between devices with their start and end apart: 4, of which 1 were waited for; matrix products, arithmetic and copies ran while one was open for 1% of the time, Pallas kernels for 5%

profile of v9, /device:TPU:32, one launch (start us, length us, event | category | flops | bytes accessed | tf_op | source)
XLA Modules:
  0.0 100.9 jit_solution(2238098949356332885)
XLA Ops:
  0.0 2.1 %pack.1 = bf16[16,144,128]{2,1,0:T(8,128)(2,1)} custom-call(bf16[8,1024]{1,0:T(8,128)(2,1)} %q_ref.1, bf16[128,1024]{1,0:T(8,128)(2,1)} %k_ref.1, bf16[128,1024]{1,0:T(8,128)(2,1)} %v_ref.1), custom_call_target="tpu_custom_call" | custom-call | tf_op jit(solution)/shard_map/pack/pallas_call | solution.py:46
  2.1 20.4 %all_to_all.15.kva_ref = bf16[16,144,128]{2,1,0:T(8,128)(2,1)S(1)} all-to-all(bf16[16,144,128]{2,1,0:T(8,128)(2,1)} %pack.1), channel_id=1, replica_groups=mesh['y'=4,'zh'=2,'core'=2,'xa'=2,'xb'=2,'zq'=4,'zo'=2] {'zo','xa','y'}, dimensions={0} | all-to-all | bytes 1179648 | tf_op jit(solution)/shard_map/all_to_all | solution.py:163
  22.5 2.5 %collective-permute-start = (bf16[16,144,128]{2,1,0:T(8,128)(2,1)S(1)}, bf16[16,144,128]{2,1,0:T(8,128)(2,1)S(1)}, u32[]{:S(2)}, u32[]{:S(2)}) collective-permute-start(bf16[16,144,128]{2,1,0:T(8,128)(2,1)S(1)} %all_to_all.15.kva_ref), channel_id=1, source_target_pairs={{0,8},{8,0},{1,9},{9,1},{2,10},{10,2},{3,11},{11,3},{4,12},{12,4},... | collective-permute-start | bytes 1769480 | tf_op jit(solution)/shard_map/ppermute | solution.py:167
  25.1 0.7 broadcast_in_dim.8
  25.7 14.2 %all-to-all-start.1 = ((bf16[8,64,128]{2,1,0:T(8,128)(2,1)}), bf16[8,64,128]{2,1,0:T(8,128)(2,1)S(1)}, u32[]{:S(2)}, u32[]{:S(2)}) async-start(bf16[8,64,128]{2,1,0:T(8,128)(2,1)} %broadcast_in_dim.8), calls=%async_computation.1 | async-start | bytes 262144 | tf_op jit(solution)/shard_map/all_to_all | solution.py:163
  39.9 1.9 %collective-permute-start.2 = (bf16[16,144,128]{2,1,0:T(8,128)(2,1)S(1)}, bf16[16,144,128]{2,1,0:T(8,128)(2,1)S(1)}, u32[]{:S(2)}, u32[]{:S(2)}) collective-permute-start(bf16[16,144,128]{2,1,0:T(8,128)(2,1)S(1)} %all_to_all.15.kva_ref), channel_id=1, source_target_pairs={{0,32},{32,0},{1,33},{33,1},{2,34},{34,2},{3,35},{35,3},{4,36},{36... | collective-permute-start | bytes 1769480 | tf_op jit(solution)/shard_map/ppermute | solution.py:167
  41.8 12.1 %all-to-all-done.1.q_ref = bf16[8,64,128]{2,1,0:T(8,128)(2,1)S(1)} async-done(((bf16[8,64,128]{2,1,0:T(8,128)(2,1)}), bf16[8,64,128]{2,1,0:T(8,128)(2,1)S(1)}, u32[]{:S(2)}, u32[]{:S(2)}) %all-to-all-start.1) | async-done | bytes 131104 | tf_op jit(solution)/shard_map/all_to_all | solution.py:163
  53.9 0.0 collective-permute-done.kva_ref
  53.9 1.9 %collective-permute-start.1 = (bf16[16,144,128]{2,1,0:T(8,128)(2,1)S(1)}, bf16[16,144,128]{2,1,0:T(8,128)(2,1)S(1)}, u32[]{:S(2)}, u32[]{:S(2)}) collective-permute-start(bf16[16,144,128]{2,1,0:T(8,128)(2,1)S(1)} %collective-permute-done.kva_ref), channel_id=1, source_target_pairs={{0,32},{32,0},{1,33},{33,1},{2,34},{34,2},{3,35},{35,3},{4,36},{36... | collective-permute-start | bytes 1769480 | tf_op jit(solution)/shard_map/ppermute | solution.py:167
  55.8 0.0 collective-permute-done.2.kvb_ref
  55.8 4.9 %attend_first_kernel.1 = (f32[1024,128]{1,0:T(8,128)S(1)}, f32[1024,128]{1,0:T(8,128)S(1)}) custom-call(bf16[8,64,128]{2,1,0:T(8,128)(2,1)S(1)} %all-to-all-done.1.q_ref, bf16[16,144,128]{2,1,0:T(8,128)(2,1)S(1)} %all_to_all.15.kva_ref, bf16[16,144,128]{2,1,0:T(8,128)(2,1)S(1)} %collective-permute-done.2.kvb_ref), custom_call_target="tpu_custom_call" | custom-call | flops 2147483648 | bytes 2097152 | tf_op jit(solution)/shard_map/attend_first_kernel/pallas_call | solution.py:115
  60.7 0.0 collective-permute-done.1.kvb_ref
  60.7 5.0 %attend_second_kernel.1 = bf16[1024,128]{1,0:T(8,128)(2,1)S(1)} custom-call(bf16[8,64,128]{2,1,0:T(8,128)(2,1)S(1)} %all-to-all-done.1.q_ref, bf16[16,144,128]{2,1,0:T(8,128)(2,1)S(1)} %collective-permute-done.kva_ref, bf16[16,144,128]{2,1,0:T(8,128)(2,1)S(1)} %collective-permute-done.1.kvb_ref, f32[1024,128]{1,0:T(8,128)S(1)} %get-tuple-element.11.top_ref, ...), custom_call_target="tpu_custom_call" | custom-call | flops 2147483648 | bytes 2097152 | tf_op jit(solution)/shard_map/attend_second_kernel/pallas_call | solution.py:115
  65.8 32.1 %all_to_all.16 = bf16[128,8,128]{2,1,0:T(8,128)(2,1)} all-to-all(bf16[128,8,128]{2,1,0:T(8,128)(2,1)S(1)} %bitcast.3), channel_id=1, replica_groups=mesh['y'=4,'zh'=2,'core'=2,'xa'=2,'xb'=2,'zq'=4,'zo'=2] {'zh','zq','zo',..., dimensions={0} | all-to-all | bytes 524288 | tf_op jit(solution)/shard_map/all_to_all | solution.py:163
  97.9 3.0 %finish.1 = bf16[8,1024]{1,0:T(8,128)(2,1)} custom-call(bf16[1024,128]{1,0:T(8,128)(2,1)} %bitcast.4, bf16[1024,1024]{1,0:T(8,128)(2,1)} %w_ref.1), custom_call_target="tpu_custom_call" | custom-call | tf_op jit(solution)/shard_map/finish/pallas_call | solution.py:153
  (1 shorter events, 0.0 us)
Async XLA Ops:
  22.5 31.4 %collective-permute-start = (bf16[16,144,128]{2,1,0:T(8,128)(2,1)S(1)}, bf16[16,144,128]{2,1,0:T(8,128)(2,1)S(1)}, u32[]{:S(2)}, u32[]{:S(2)}) collective-permute-start(bf16[16,144,128]{2,1,0:T(8,128)(2,1)S(1)} %all_to_all.15.kva_ref), channel_id=1, source_target_pairs={{0,8},{8,0},{1,9},{9,1},{2,10},{10,2},{3,11},{11,3},{4,12},{12,4},... | collective-permute-start | bytes 1769480 | tf_op jit(solution)/shard_map/ppermute | solution.py:167
  25.7 28.2 %all-to-all-start.1 = ((bf16[8,64,128]{2,1,0:T(8,128)(2,1)}), bf16[8,64,128]{2,1,0:T(8,128)(2,1)S(1)}, u32[]{:S(2)}, u32[]{:S(2)}) async-start(bf16[8,64,128]{2,1,0:T(8,128)(2,1)} %broadcast_in_dim.8), calls=%async_computation.1 | async-start | bytes 262144 | tf_op jit(solution)/shard_map/all_to_all | solution.py:163
  39.9 15.9 %collective-permute-start.2 = (bf16[16,144,128]{2,1,0:T(8,128)(2,1)S(1)}, bf16[16,144,128]{2,1,0:T(8,128)(2,1)S(1)}, u32[]{:S(2)}, u32[]{:S(2)}) collective-permute-start(bf16[16,144,128]{2,1,0:T(8,128)(2,1)S(1)} %all_to_all.15.kva_ref), channel_id=1, source_target_pairs={{0,32},{32,0},{1,33},{33,1},{2,34},{34,2},{3,35},{35,3},{4,36},{36... | collective-permute-start | bytes 1769480 | tf_op jit(solution)/shard_map/ppermute | solution.py:167
  53.9 6.8 %collective-permute-start.1 = (bf16[16,144,128]{2,1,0:T(8,128)(2,1)S(1)}, bf16[16,144,128]{2,1,0:T(8,128)(2,1)S(1)}, u32[]{:S(2)}, u32[]{:S(2)}) collective-permute-start(bf16[16,144,128]{2,1,0:T(8,128)(2,1)S(1)} %collective-permute-done.kva_ref), channel_id=1, source_target_pairs={{0,32},{32,0},{1,33},{33,1},{2,34},{34,2},{3,35},{35,3},{4,36},{36... | collective-permute-start | bytes 1769480 | tf_op jit(solution)/shard_map/ppermute | solution.py:167

commit v10 on v9

--- a/solution.py
+++ b/solution.py
@@ -117,7 +117,7 @@
         out_shape=shapes,
         in_specs=[VMEM] * (1 + len(rest)),
         out_specs=jax.tree.map(lambda shape: VMEM, shapes),
-        compiler_params=pltpu.CompilerParams(vmem_limit_bytes=32 * 2**20),
+        compiler_params=pltpu.CompilerParams(vmem_limit_bytes=20 * 2**20),
         cost_estimate=pl.CostEstimate(
             flops=4 * queries * rows * 128, bytes_accessed=2**21, transcendentals=queries * rows
         ),
@@ -155,6 +155,7 @@
         out_shape=jax.ShapeDtypeStruct((8, HEADS * HD), BF16),
         in_specs=[VMEM, VMEM],
         out_specs=VMEM,
+        compiler_params=pltpu.CompilerParams(vmem_limit_bytes=8 * 2**20),
         name="finish",
     )(parts, w_out)
 

time: 101 us -> 99.4 us (0.984)
  Pallas kernels: 15 us -> 13.3 us
    pallas_call x1, Pallas kernels: 2.97 us -> 1.28 us  [finish(): pl.pallas_call(finish_kernel, out_shape=jax.ShapeDtypeStruct((8, HEADS *...]
where the time goes in v10:
time: 99.4 us; the launch traced here: 99 us
  blocking collectives  52.4 us (53%)
  starting transfers between devices  20.5 us (21%)
  Pallas kernels  13.3 us (13%)
  waiting for transfers between devices  12.1 us (12%)
    all_to_all x2, blocking collectives, exchange(): return lax.all_to_all(blocks, axes, split_axis=0, concat_axis=0, tiled=True)  52.4 us
    all_to_all x1, starting transfers between devices, exchange(): return lax.all_to_all(blocks, axes, split_axis=0, concat_axis=0, tiled=True)  14.2 us
    all_to_all x1, waiting for transfers between devices, exchange(): return lax.all_to_all(blocks, axes, split_axis=0, concat_axis=0, tiled=True)  12.1 us
    pallas_call x2, Pallas kernels, attend(): pl.pallas_call(functools.partial(kernel, group), out_shape=shapes, in_spe...  9.91 us
    ppermute x3, starting transfers between devices, swap(): return lax.ppermute(block, axis, [(0, 1), (1, 0)])  6.35 us
    pallas_call x1, Pallas kernels, pack(): pl.pallas_call(pack_kernel, out_shape=jax.ShapeDtypeStruct((HEADS, 144, 1...  2.08 us
  transfers between devices with their start and end apart: 4, of which 1 were waited for; matrix products, arithmetic and copies ran while one was open for 1% of the time, Pallas kernels for 5%

profile of v10, /device:TPU:32, one launch (start us, length us, event | category | flops | bytes accessed | tf_op | source)
XLA Modules:
  0.0 99.0 jit_solution(12005215005385519725)
XLA Ops:
  0.0 2.1 %pack.1 = bf16[16,144,128]{2,1,0:T(8,128)(2,1)} custom-call(bf16[8,1024]{1,0:T(8,128)(2,1)} %q_ref.1, bf16[128,1024]{1,0:T(8,128)(2,1)} %k_ref.1, bf16[128,1024]{1,0:T(8,128)(2,1)} %v_ref.1), custom_call_target="tpu_custom_call" | custom-call | tf_op jit(solution)/shard_map/pack/pallas_call | solution.py:46
  2.1 20.4 %all_to_all.15.kva_ref = bf16[16,144,128]{2,1,0:T(8,128)(2,1)S(1)} all-to-all(bf16[16,144,128]{2,1,0:T(8,128)(2,1)} %pack.1), channel_id=1, replica_groups=mesh['y'=4,'zh'=2,'core'=2,'xa'=2,'xb'=2,'zq'=4,'zo'=2] {'zo','xa','y'}, dimensions={0} | all-to-all | bytes 1179648 | tf_op jit(solution)/shard_map/all_to_all | solution.py:164
  22.5 2.5 %collective-permute-start = (bf16[16,144,128]{2,1,0:T(8,128)(2,1)S(1)}, bf16[16,144,128]{2,1,0:T(8,128)(2,1)S(1)}, u32[]{:S(2)}, u32[]{:S(2)}) collective-permute-start(bf16[16,144,128]{2,1,0:T(8,128)(2,1)S(1)} %all_to_all.15.kva_ref), channel_id=1, source_target_pairs={{0,8},{8,0},{1,9},{9,1},{2,10},{10,2},{3,11},{11,3},{4,12},{12,4},... | collective-permute-start | bytes 1769480 | tf_op jit(solution)/shard_map/ppermute | solution.py:168
  25.1 0.7 broadcast_in_dim.8
  25.7 14.2 %all-to-all-start.1 = ((bf16[8,64,128]{2,1,0:T(8,128)(2,1)}), bf16[8,64,128]{2,1,0:T(8,128)(2,1)S(1)}, u32[]{:S(2)}, u32[]{:S(2)}) async-start(bf16[8,64,128]{2,1,0:T(8,128)(2,1)} %broadcast_in_dim.8), calls=%async_computation.1 | async-start | bytes 262144 | tf_op jit(solution)/shard_map/all_to_all | solution.py:164
  39.9 1.9 %collective-permute-start.2 = (bf16[16,144,128]{2,1,0:T(8,128)(2,1)S(1)}, bf16[16,144,128]{2,1,0:T(8,128)(2,1)S(1)}, u32[]{:S(2)}, u32[]{:S(2)}) collective-permute-start(bf16[16,144,128]{2,1,0:T(8,128)(2,1)S(1)} %all_to_all.15.kva_ref), channel_id=1, source_target_pairs={{0,32},{32,0},{1,33},{33,1},{2,34},{34,2},{3,35},{35,3},{4,36},{36... | collective-permute-start | bytes 1769480 | tf_op jit(solution)/shard_map/ppermute | solution.py:168
  41.8 12.1 %all-to-all-done.1.q_ref = bf16[8,64,128]{2,1,0:T(8,128)(2,1)S(1)} async-done(((bf16[8,64,128]{2,1,0:T(8,128)(2,1)}), bf16[8,64,128]{2,1,0:T(8,128)(2,1)S(1)}, u32[]{:S(2)}, u32[]{:S(2)}) %all-to-all-start.1) | async-done | bytes 131104 | tf_op jit(solution)/shard_map/all_to_all | solution.py:164
  53.9 0.0 collective-permute-done.kva_ref
  53.9 1.9 %collective-permute-start.1 = (bf16[16,144,128]{2,1,0:T(8,128)(2,1)S(1)}, bf16[16,144,128]{2,1,0:T(8,128)(2,1)S(1)}, u32[]{:S(2)}, u32[]{:S(2)}) collective-permute-start(bf16[16,144,128]{2,1,0:T(8,128)(2,1)S(1)} %collective-permute-done.kva_ref), channel_id=1, source_target_pairs={{0,32},{32,0},{1,33},{33,1},{2,34},{34,2},{3,35},{35,3},{4,36},{36... | collective-permute-start | bytes 1769480 | tf_op jit(solution)/shard_map/ppermute | solution.py:168
  55.8 0.0 collective-permute-done.2.kvb_ref
  55.8 4.9 %attend_first_kernel.1 = (f32[1024,128]{1,0:T(8,128)S(1)}, f32[1024,128]{1,0:T(8,128)S(1)}) custom-call(bf16[8,64,128]{2,1,0:T(8,128)(2,1)S(1)} %all-to-all-done.1.q_ref, bf16[16,144,128]{2,1,0:T(8,128)(2,1)S(1)} %all_to_all.15.kva_ref, bf16[16,144,128]{2,1,0:T(8,128)(2,1)S(1)} %collective-permute-done.2.kvb_ref), custom_call_target="tpu_custom_call" | custom-call | flops 2147483648 | bytes 2097152 | tf_op jit(solution)/shard_map/attend_first_kernel/pallas_call | solution.py:115
  60.7 0.0 collective-permute-done.1.kvb_ref
  60.7 0.0 copy-start
  60.8 5.0 %attend_second_kernel.1 = bf16[1024,128]{1,0:T(8,128)(2,1)S(1)} custom-call(bf16[8,64,128]{2,1,0:T(8,128)(2,1)S(1)} %all-to-all-done.1.q_ref, bf16[16,144,128]{2,1,0:T(8,128)(2,1)S(1)} %collective-permute-done.kva_ref, bf16[16,144,128]{2,1,0:T(8,128)(2,1)S(1)} %collective-permute-done.1.kvb_ref, f32[1024,128]{1,0:T(8,128)S(1)} %get-tuple-element.11.top_ref, ...), custom_call_target="tpu_custom_call" | custom-call | flops 2147483648 | bytes 2097152 | tf_op jit(solution)/shard_map/attend_second_kernel/pallas_call | solution.py:115
  65.8 31.9 %all_to_all.16 = bf16[128,8,128]{2,1,0:T(8,128)(2,1)S(1)} all-to-all(bf16[128,8,128]{2,1,0:T(8,128)(2,1)S(1)} %bitcast.4), channel_id=1, replica_groups=mesh['y'=4,'zh'=2,'core'=2,'xa'=2,'xb'=2,'zq'=4,'zo'=2] {'zh','zq','zo',..., dimensions={0} | all-to-all | bytes 524288 | tf_op jit(solution)/shard_map/all_to_all | solution.py:164
  97.7 0.0 copy-done
  97.7 1.3 %finish.1 = bf16[8,1024]{1,0:T(8,128)(2,1)} custom-call(bf16[1024,128]{1,0:T(8,128)(2,1)S(1)} %bitcast.3, bf16[1024,1024]{1,0:T(8,128)(2,1)S(1)} %copy-done), custom_call_target="tpu_custom_call" | custom-call | tf_op jit(solution)/shard_map/finish/pallas_call | solution.py:153
  (1 shorter events, 0.0 us)
Async XLA Ops:
  22.5 31.4 %collective-permute-start = (bf16[16,144,128]{2,1,0:T(8,128)(2,1)S(1)}, bf16[16,144,128]{2,1,0:T(8,128)(2,1)S(1)}, u32[]{:S(2)}, u32[]{:S(2)}) collective-permute-start(bf16[16,144,128]{2,1,0:T(8,128)(2,1)S(1)} %all_to_all.15.kva_ref), channel_id=1, source_target_pairs={{0,8},{8,0},{1,9},{9,1},{2,10},{10,2},{3,11},{11,3},{4,12},{12,4},... | collective-permute-start | bytes 1769480 | tf_op jit(solution)/shard_map/ppermute | solution.py:168
  25.7 28.2 %all-to-all-start.1 = ((bf16[8,64,128]{2,1,0:T(8,128)(2,1)}), bf16[8,64,128]{2,1,0:T(8,128)(2,1)S(1)}, u32[]{:S(2)}, u32[]{:S(2)}) async-start(bf16[8,64,128]{2,1,0:T(8,128)(2,1)} %broadcast_in_dim.8), calls=%async_computation.1 | async-start | bytes 262144 | tf_op jit(solution)/shard_map/all_to_all | solution.py:164
  39.9 15.9 %collective-permute-start.2 = (bf16[16,144,128]{2,1,0:T(8,128)(2,1)S(1)}, bf16[16,144,128]{2,1,0:T(8,128)(2,1)S(1)}, u32[]{:S(2)}, u32[]{:S(2)}) collective-permute-start(bf16[16,144,128]{2,1,0:T(8,128)(2,1)S(1)} %all_to_all.15.kva_ref), channel_id=1, source_target_pairs={{0,32},{32,0},{1,33},{33,1},{2,34},{34,2},{3,35},{35,3},{4,36},{36... | collective-permute-start | bytes 1769480 | tf_op jit(solution)/shard_map/ppermute | solution.py:168
  53.9 6.8 %collective-permute-start.1 = (bf16[16,144,128]{2,1,0:T(8,128)(2,1)S(1)}, bf16[16,144,128]{2,1,0:T(8,128)(2,1)S(1)}, u32[]{:S(2)}, u32[]{:S(2)}) collective-permute-start(bf16[16,144,128]{2,1,0:T(8,128)(2,1)S(1)} %collective-permute-done.kva_ref), channel_id=1, source_target_pairs={{0,32},{32,0},{1,33},{33,1},{2,34},{34,2},{3,35},{35,3},{4,36},{36... | collective-permute-start | bytes 1769480 | tf_op jit(solution)/shard_map/ppermute | solution.py:168
  60.7 37.0 %copy-start = (bf16[1024,1024]{1,0:T(8,128)(2,1)S(1)}, bf16[1024,1024]{1,0:T(8,128)(2,1)}, u32[]{:S(2)}) copy-start(bf16[1024,1024]{1,0:T(8,128)(2,1)} %w_ref.1) | copy-start | bytes 6291460

commit v11 on v10

--- a/solution.py
+++ b/solution.py
@@ -62,17 +62,40 @@
     return jnp.concatenate(parts, 0).astype(BF16)
 
 
-def absorb(group, q, kv_refs, top, total):
+def mark(kv):
+    return jnp.where(iota(kv.shape, 1) < HD, jnp.ones((), BF16), kv)
+
+
+def mark_kernel(kv_ref, out_ref):
+    for source in range(HEADS):
+        out_ref[source] = mark(kv_ref[source, 0:128, :])
+
+
+def mark_all(kv):
+    return pl.pallas_call(
+        mark_kernel,
+        out_shape=jax.ShapeDtypeStruct((HEADS, 128, 128), BF16),
+        in_specs=[VMEM],
+        out_specs=VMEM,
+        compiler_params=pltpu.CompilerParams(vmem_limit_bytes=8 * 2**20),
+        cost_estimate=pl.CostEstimate(flops=2**33, bytes_accessed=2**20, transcendentals=0),
+        name="mark",
+    )(kv)
+
+
+def absorb(group, q, pairs, top, total):
     rows = group * 128
-    low = iota((rows, 128), 1) < HD
-    for kv_ref in kv_refs:
+    for kv_ref, marked_ref in pairs:
         for c in range(HEADS // group):
             kv = kv_ref[c * group : (c + 1) * group, 0:128, :].reshape(rows, 128)
             score = lax.dot_general(q, kv, (((1,), (1,)), ((), ())), preferred_element_type=F32)
             here = jnp.max(score, 1, keepdims=True)
             new = here if top is None else jnp.maximum(top, here)
             weights = jnp.exp(score - new).astype(BF16)
-            marked = jnp.where(low, jnp.ones((), BF16), kv)
+            if marked_ref is None:
+                marked = mark(kv)
+            else:
+                marked = marked_ref[c * group : (c + 1) * group].reshape(rows, 128)
             part = jnp.dot(weights, marked, preferred_element_type=F32)
             total = part if top is None else total * jnp.exp(top - new) + part
             top = new
@@ -80,14 +103,14 @@
 
 
 def attend_first_kernel(group, q_ref, kva_ref, kvb_ref, top_ref, total_ref):
-    top, total = absorb(group, take_queries(q_ref), (kva_ref, kvb_ref), None, None)
+    top, total = absorb(group, take_queries(q_ref), ((kva_ref, None), (kvb_ref, None)), None, None)
     top_ref[...] = jnp.broadcast_to(top, top_ref.shape)
     total_ref[...] = total
 
 
-def attend_second_kernel(group, q_ref, kva_ref, kvb_ref, top_ref, total_ref, out_ref):
+def attend_second_kernel(group, q_ref, kva_ref, marked_ref, kvb_ref, top_ref, total_ref, out_ref):
     top, total = jnp.max(top_ref[...], 1, keepdims=True), total_ref[...]
-    top, total = absorb(group, take_queries(q_ref), (kva_ref, kvb_ref), top, total)
+    top, total = absorb(group, take_queries(q_ref), ((kva_ref, marked_ref), (kvb_ref, None)), top, total)
     low64 = iota((64, 128), 1) < HD
     sub = iota((64, 128), 0) % 8 < 4
     first_half = iota((64, 128), 1) % HD < HD // 2
@@ -174,12 +197,13 @@
     held_core = swap(held, "core")
     q_place = held[:, 128:132, :].reshape(1, 64, 128)
     q_all = exchange(jnp.broadcast_to(q_place, (STEPS, 64, 128)), DEPTH)
-    held_x, q_all = lax.optimization_barrier((held_x, q_all))
+    marked_x = mark_all(held_x)
+    held_x, marked_x = lax.optimization_barrier((held_x, marked_x))
     held_both = swap(held_x, "core")
     state = jax.ShapeDtypeStruct((STEPS * 128, 128), F32)
     top, total = attend(attend_first_kernel, (state, state), q_all, held, held_core)
     result = jax.ShapeDtypeStruct((STEPS * 128, 128), BF16)
-    parts = attend(attend_second_kernel, result, q_all, held_x, held_both, top, total)
+    parts = attend(attend_second_kernel, result, q_all, held_x, marked_x, held_both, top, total)
     parts = exchange(parts.reshape(STEPS * HEADS, 8, 128), DEPTH + PLACE)
     return finish(parts.reshape(STEPS * HEADS * 8, 128), w_out)
 

time: 99.4 us -> 96.3 us (0.969)
  waiting for transfers between devices: 12.1 us -> 9.57 us
  blocking collectives: 52.4 us -> 51.2 us
    all_to_all x1, waiting for transfers between devices: 12.1 us -> 9.56 us  [exchange(): return lax.all_to_all(blocks, axes, split_axis=0, concat_axis=0, tiled=True)]
    all_to_all x2, blocking collectives: 52.4 us -> 51.2 us  [exchange(): return lax.all_to_all(blocks, axes, split_axis=0, concat_axis=0, tiled=True)]
where the time goes in v11:
time: 96.3 us; the launch traced here: 95.9 us
  blocking collectives  51.2 us (53%)
  starting transfers between devices  21 us (22%)
  Pallas kernels  13.4 us (14%)
  waiting for transfers between devices  9.57 us (10%)
    all_to_all x2, blocking collectives, exchange(): return lax.all_to_all(blocks, axes, split_axis=0, concat_axis=0, tiled=True)  51.2 us
    all_to_all x1, starting transfers between devices, exchange(): return lax.all_to_all(blocks, axes, split_axis=0, concat_axis=0, tiled=True)  14.2 us
    pallas_call x2, Pallas kernels, attend(): pl.pallas_call(functools.partial(kernel, group), out_shape=shapes, in_spe...  9.91 us
    all_to_all x1, waiting for transfers between devices, exchange(): return lax.all_to_all(blocks, axes, split_axis=0, concat_axis=0, tiled=True)  9.56 us
    ppermute x3, starting transfers between devices, swap(): return lax.ppermute(block, axis, [(0, 1), (1, 0)])  6.85 us
    pallas_call x1, Pallas kernels, pack(): pl.pallas_call(pack_kernel, out_shape=jax.ShapeDtypeStruct((HEADS, 144, 1...  2.08 us
  transfers between devices with their start and end apart: 4, of which 1 were waited for; matrix products, arithmetic and copies ran while one was open for 1% of the time, Pallas kernels for 5%

profile of v11, /device:TPU:32, one launch (start us, length us, event | category | flops | bytes accessed | tf_op | source)
XLA Modules:
  0.0 95.9 jit_solution(3462831236447672387)
XLA Ops:
  0.0 2.1 %pack.1 = bf16[16,144,128]{2,1,0:T(8,128)(2,1)} custom-call(bf16[8,1024]{1,0:T(8,128)(2,1)} %q_ref.1, bf16[128,1024]{1,0:T(8,128)(2,1)} %k_ref.1, bf16[128,1024]{1,0:T(8,128)(2,1)} %v_ref.1), custom_call_target="tpu_custom_call" | custom-call | tf_op jit(solution)/shard_map/pack/pallas_call | solution.py:46
  2.1 20.4 %all_to_all.15.kva_ref = bf16[16,144,128]{2,1,0:T(8,128)(2,1)S(1)} all-to-all(bf16[16,144,128]{2,1,0:T(8,128)(2,1)} %pack.1), channel_id=1, replica_groups=mesh['y'=4,'zh'=2,'core'=2,'xa'=2,'xb'=2,'zq'=4,'zo'=2] {'zo','xa','y'}, dimensions={0} | all-to-all | bytes 1179648 | tf_op jit(solution)/shard_map/all_to_all | solution.py:187
  22.5 2.5 %collective-permute-start = (bf16[16,144,128]{2,1,0:T(8,128)(2,1)S(1)}, bf16[16,144,128]{2,1,0:T(8,128)(2,1)S(1)}, u32[]{:S(2)}, u32[]{:S(2)}) collective-permute-start(bf16[16,144,128]{2,1,0:T(8,128)(2,1)S(1)} %all_to_all.15.kva_ref), channel_id=1, source_target_pairs={{0,8},{8,0},{1,9},{9,1},{2,10},{10,2},{3,11},{11,3},{4,12},{12,4},... | collective-permute-start | bytes 1769480 | tf_op jit(solution)/shard_map/ppermute | solution.py:191
  25.1 0.7 broadcast_in_dim.8
  25.7 14.2 %all-to-all-start.1 = ((bf16[8,64,128]{2,1,0:T(8,128)(2,1)}), bf16[8,64,128]{2,1,0:T(8,128)(2,1)S(1)}, u32[]{:S(2)}, u32[]{:S(2)}) async-start(bf16[8,64,128]{2,1,0:T(8,128)(2,1)} %broadcast_in_dim.8), calls=%async_computation.1 | async-start | bytes 262144 | tf_op jit(solution)/shard_map/all_to_all | solution.py:187
  39.9 1.9 %collective-permute-start.2 = (bf16[16,144,128]{2,1,0:T(8,128)(2,1)S(1)}, bf16[16,144,128]{2,1,0:T(8,128)(2,1)S(1)}, u32[]{:S(2)}, u32[]{:S(2)}) collective-permute-start(bf16[16,144,128]{2,1,0:T(8,128)(2,1)S(1)} %all_to_all.15.kva_ref), channel_id=1, source_target_pairs={{0,32},{32,0},{1,33},{33,1},{2,34},{34,2},{3,35},{35,3},{4,36},{36... | collective-permute-start | bytes 1769480 | tf_op jit(solution)/shard_map/ppermute | solution.py:191
  41.8 0.0 collective-permute-done.kv_ref.kva_ref
  41.8 0.1 mark.1.marked_ref
  41.9 2.4 %collective-permute-start.1 = (bf16[16,144,128]{2,1,0:T(8,128)(2,1)S(1)}, bf16[16,144,128]{2,1,0:T(8,128)(2,1)S(1)}, u32[]{:S(2)}, u32[]{:S(2)}) collective-permute-start(bf16[16,144,128]{2,1,0:T(8,128)(2,1)S(1)} %collective-permute-done.kv_ref.kva_ref), channel_id=1, source_target_pairs={{0,32},{32,0},{1,33},{33,1},{2,34},{34,2},{3,35},{35,3},{4,36},{36... | collective-permute-start | bytes 1769480 | tf_op jit(solution)/shard_map/ppermute | solution.py:191
  44.4 9.6 %all-to-all-done.1.q_ref = bf16[8,64,128]{2,1,0:T(8,128)(2,1)S(1)} async-done(((bf16[8,64,128]{2,1,0:T(8,128)(2,1)}), bf16[8,64,128]{2,1,0:T(8,128)(2,1)S(1)}, u32[]{:S(2)}, u32[]{:S(2)}) %all-to-all-start.1) | async-done | bytes 131104 | tf_op jit(solution)/shard_map/all_to_all | solution.py:187
  53.9 0.0 collective-permute-done.2.kvb_ref
  53.9 4.9 %attend_first_kernel.1 = (f32[1024,128]{1,0:T(8,128)S(1)}, f32[1024,128]{1,0:T(8,128)S(1)}) custom-call(bf16[8,64,128]{2,1,0:T(8,128)(2,1)S(1)} %all-to-all-done.1.q_ref, bf16[16,144,128]{2,1,0:T(8,128)(2,1)S(1)} %all_to_all.15.kva_ref, bf16[16,144,128]{2,1,0:T(8,128)(2,1)S(1)} %collective-permute-done.2.kvb_ref), custom_call_target="tpu_custom_call" | custom-call | flops 2147483648 | bytes 2097152 | tf_op jit(solution)/shard_map/attend_first_kernel/pallas_call | solution.py:138
  58.8 0.0 collective-permute-done.1.kvb_ref
  58.8 0.0 copy-start
  58.8 5.0 %attend_second_kernel.1 = bf16[1024,128]{1,0:T(8,128)(2,1)S(1)} custom-call(bf16[8,64,128]{2,1,0:T(8,128)(2,1)S(1)} %all-to-all-done.1.q_ref, bf16[16,144,128]{2,1,0:T(8,128)(2,1)S(1)} %collective-permute-done.kv_ref.kva_ref, bf16[16,128,128]{2,1,0:T(8,128)(2,1)S(1)} %mark.1.marked_ref, bf16[16,144,128]{2,1,0:T(8,128)(2,1)S(1)} %collective-permute-done.1.kvb_ref, ...), custom_call_target="tpu_custom_call" | custom-call | flops 2147483648 | bytes 2097152 | tf_op jit(solution)/shard_map/attend_second_kernel/pallas_call | solution.py:138
  63.9 30.8 %all_to_all.16 = bf16[128,8,128]{2,1,0:T(8,128)(2,1)S(1)} all-to-all(bf16[128,8,128]{2,1,0:T(8,128)(2,1)S(1)} %bitcast.4), channel_id=1, replica_groups=mesh['y'=4,'zh'=2,'core'=2,'xa'=2,'xb'=2,'zq'=4,'zo'=2] {'zh','zq','zo',..., dimensions={0} | all-to-all | bytes 524288 | tf_op jit(solution)/shard_map/all_to_all | solution.py:187
  94.7 0.0 copy-done
  94.7 1.3 %finish.1 = bf16[8,1024]{1,0:T(8,128)(2,1)} custom-call(bf16[1024,128]{1,0:T(8,128)(2,1)S(1)} %bitcast.3, bf16[1024,1024]{1,0:T(8,128)(2,1)S(1)} %copy-done), custom_call_target="tpu_custom_call" | custom-call | tf_op jit(solution)/shard_map/finish/pallas_call | solution.py:176
  (1 shorter events, 0.0 us)
Async XLA Ops:
  22.5 19.3 %collective-permute-start = (bf16[16,144,128]{2,1,0:T(8,128)(2,1)S(1)}, bf16[16,144,128]{2,1,0:T(8,128)(2,1)S(1)}, u32[]{:S(2)}, u32[]{:S(2)}) collective-permute-start(bf16[16,144,128]{2,1,0:T(8,128)(2,1)S(1)} %all_to_all.15.kva_ref), channel_id=1, source_target_pairs={{0,8},{8,0},{1,9},{9,1},{2,10},{10,2},{3,11},{11,3},{4,12},{12,4},... | collective-permute-start | bytes 1769480 | tf_op jit(solution)/shard_map/ppermute | solution.py:191
  25.7 28.2 %all-to-all-start.1 = ((bf16[8,64,128]{2,1,0:T(8,128)(2,1)}), bf16[8,64,128]{2,1,0:T(8,128)(2,1)S(1)}, u32[]{:S(2)}, u32[]{:S(2)}) async-start(bf16[8,64,128]{2,1,0:T(8,128)(2,1)} %broadcast_in_dim.8), calls=%async_computation.1 | async-start | bytes 262144 | tf_op jit(solution)/shard_map/all_to_all | solution.py:187
  39.9 14.0 %collective-permute-start.2 = (bf16[16,144,128]{2,1,0:T(8,128)(2,1)S(1)}, bf16[16,144,128]{2,1,0:T(8,128)(2,1)S(1)}, u32[]{:S(2)}, u32[]{:S(2)}) collective-permute-start(bf16[16,144,128]{2,1,0:T(8,128)(2,1)S(1)} %all_to_all.15.kva_ref), channel_id=1, source_target_pairs={{0,32},{32,0},{1,33},{33,1},{2,34},{34,2},{3,35},{35,3},{4,36},{36... | collective-permute-start | bytes 1769480 | tf_op jit(solution)/shard_map/ppermute | solution.py:191
  41.9 16.9 %collective-permute-start.1 = (bf16[16,144,128]{2,1,0:T(8,128)(2,1)S(1)}, bf16[16,144,128]{2,1,0:T(8,128)(2,1)S(1)}, u32[]{:S(2)}, u32[]{:S(2)}) collective-permute-start(bf16[16,144,128]{2,1,0:T(8,128)(2,1)S(1)} %collective-permute-done.kv_ref.kva_ref), channel_id=1, source_target_pairs={{0,32},{32,0},{1,33},{33,1},{2,34},{34,2},{3,35},{35,3},{4,36},{36... | collective-permute-start | bytes 1769480 | tf_op jit(solution)/shard_map/ppermute | solution.py:191
  58.8 35.8 %copy-start = (bf16[1024,1024]{1,0:T(8,128)(2,1)S(1)}, bf16[1024,1024]{1,0:T(8,128)(2,1)}, u32[]{:S(2)}) copy-start(bf16[1024,1024]{1,0:T(8,128)(2,1)} %w_ref.1) | copy-start | bytes 6291460
